TPU v7x, 32 devices: a whole 2x2x4 slice. The times are simulated.
32 devices in a mesh: dp: 8 (over y, x, core), expert: 4 (over z).
Axes of the slice: x: 2, y: 2, z: 4, core: 2. Of those that a mesh axis runs over, the one named last changes fastest.
Arguments:
- layer_in: bfloat16 [4, 8192, 768], P(None, ('dp', 'expert')), may hold values from -6 to 6
- out_grad: bfloat16 [4, 8192, 768], P(None, ('dp', 'expert')), may hold values from -6 to 6
- routes: int32 [4, 8192, 2], P(None, ('dp', 'expert')), may hold values from 0 to 3, all different within a row; in each aligned block of 256 rows (0 to 255, 256 to 511, ..., all dimensions but the last counted through in order) at most 192 rows name the same one
- segments: int32 [4, 8192], P(None, 'dp'), may hold values from 0 to 3, as said below
- buckets: int32 [1024], replicated, may hold values from 0 to 31, as said below
- gain_attn: bfloat16 [768], P('dp'), may hold values from 0.25 to 1.75
- w_query: bfloat16 [768, 768], P('dp'), may hold values from -0.21875 to 0.21875
- w_key: bfloat16 [768, 768], P('dp'), may hold values from -0.21875 to 0.21875
- w_value: bfloat16 [768, 768], P('dp'), may hold values from -0.21875 to 0.21875
- w_output: bfloat16 [768, 768], P('dp'), may hold values from -1.25 to 1.25
- gain_moe: bfloat16 [768], P('dp'), may hold values from 0.25 to 1.75
- router: bfloat16 [768, 4], P('dp'), may hold values from -0.15625 to 0.15625
- rel_bias: bfloat16 [32, 12], P('dp'), may hold values from -4 to 4
- w_expert_in: bfloat16 [4, 768, 3072], P('expert'), may hold values from -0.21875 to 0.21875
- w_expert_out: bfloat16 [4, 3072, 768], P('expert'), may hold values from -0.109375 to 0.109375
Outputs:
- layer_out: bfloat16 [4, 8192, 768], P(None, ('dp', 'expert'))
- grad_in: float32 [4, 8192, 768], P(None, ('dp', 'expert'))
- grad_gain_attn: float32 [768], P('dp')
- grad_query: float32 [768, 768], P('dp')
- grad_key: float32 [768, 768], P('dp')
- grad_value: float32 [768, 768], P('dp')
- grad_output: float32 [768, 768], P('dp')
- grad_gain_moe: float32 [768], P('dp')
- grad_router: float32 [768, 4], P('dp')
- grad_rel_bias: float32 [32, 12], P('dp')
- grad_expert_in: float32 [4, 768, 3072], P('expert')
- grad_expert_out: float32 [4, 3072, 768], P('expert')
Inputs may be any that keep to these rules, and one draw needn't show every extreme that they name: `routes`: within the 256 rows of one device in one micro-batch (aligned blocks of rows), no expert is named more than 192 times; a row names two different experts. `segments`: each sequence of 1024 rows holds exactly four documents, numbered 0 to 3 in order; document 2 begins before row 256 of its sequence and includes row 768. Entry r is the bucket of a key r rows before its query; buckets never fall as r grows, and r = 0 has bucket 0.
All inputs are finite; a program needn't handle non-finite values.
Results may differ from a plain program's by a relative error of at most 0.015.
Values may be sent and summed in bfloat16 or wider, within the bound.
A program may use at most 512 MiB of HBM per device.

v0:
```python
import math

import jax
import jax.numpy as jnp
from jax import lax
from jax.sharding import PartitionSpec as P

D = 768
NB = 32
MICRO = 4


EPSILON = 1e-06
MASKED = -1e30
TOP_PRECISION = lax.Precision.HIGHEST


def norm_forward(values, gain):
    inverse = lax.rsqrt(jnp.mean(values * values, axis=-1, keepdims=True) + EPSILON)
    scaled = values * inverse
    return (scaled, inverse, scaled * gain)


def norm_backward(grad_top, scaled, inverse, gain):
    grad_scaled = grad_top * gain
    grad_values = inverse * (
        grad_scaled - scaled * jnp.mean(grad_scaled * scaled, axis=-1, keepdims=True)
    )
    return (grad_values, jnp.sum(grad_top * scaled, axis=0))


def split_heads(values, heads):
    return values.reshape(values.shape[0], heads, -1).transpose(1, 0, 2)


def merge_heads(values):
    return values.transpose(1, 0, 2).reshape(values.shape[1], -1)


def score_block(q_heads, k_heads, bias, allowed, scale):
    raw = jnp.einsum("hqd,hkd->hqk", q_heads, k_heads, preferred_element_type=jnp.float32)
    return jnp.where(allowed[None], raw * scale + bias, MASKED)


def bucket_table(distances, bucket_starts):
    lower = bucket_starts[:-1]
    upper = bucket_starts[1:]
    return (
        (distances[:, :, None] >= lower[None, None, :])
        & (distances[:, :, None] < upper[None, None, :])
    ).astype(jnp.bfloat16)


def on_device(
    layer_in,
    out_grad,
    routes,
    segments,
    buckets,
    gain_attn,
    w_query,
    w_key,
    w_value,
    w_output,
    gain_moe,
    router,
    rel_bias,
    w_expert_in,
    w_expert_out,
):
    tok_rows = layer_in.shape[1]
    seq_len = segments.shape[1]
    heads = rel_bias.shape[1]
    group_size = lax.axis_size("expert")
    rank_here = lax.axis_index("expert")
    expert_count = router.shape[1]
    local_experts = w_expert_in.shape[0]
    capacity = 3 * tok_rows // group_size
    scale = 1.0 / math.sqrt(D // heads)
    bucket_starts = jnp.sum(
        (buckets[None, :] < jnp.arange(NB + 1, dtype=jnp.int32)[:, None]).astype(jnp.int32), axis=1
    )
    query_pos = rank_here * tok_rows + jnp.arange(tok_rows, dtype=jnp.int32)
    key_pos = jnp.arange(seq_len, dtype=jnp.int32)
    offsets = jnp.maximum(query_pos[:, None] - key_pos[None, :], 0)
    bucket_onehot = bucket_table(offsets, bucket_starts)
    causal = query_pos[:, None] >= key_pos[None, :]
    slot_ids = jnp.arange(expert_count * capacity, dtype=jnp.int32)
    expert_ids = jnp.arange(expert_count, dtype=jnp.int32)
    pair_ids = jnp.arange(2 * tok_rows, dtype=jnp.int32)
    earlier = (pair_ids[None, :] < pair_ids[:, None]).astype(jnp.bfloat16)
    dense_sums = [
        jnp.zeros((D,), jnp.float32),
        jnp.zeros((D, D), jnp.float32),
        jnp.zeros((D, D), jnp.float32),
        jnp.zeros((D, D), jnp.float32),
        jnp.zeros((D, D), jnp.float32),
        jnp.zeros((D,), jnp.float32),
        jnp.zeros((D, expert_count), jnp.float32),
        jnp.zeros((NB, heads), jnp.float32),
    ]
    in_sum = jnp.zeros(w_expert_in.shape, jnp.float32)
    out_sum = jnp.zeros(w_expert_out.shape, jnp.float32)
    outputs_list = []
    grads_list = []
    for step_index in range(MICRO):
        weights_now = (
            lax.all_gather(gain_attn, "dp", axis=0, tiled=True),
            lax.all_gather(w_query, "dp", axis=0, tiled=True),
            lax.all_gather(w_key, "dp", axis=0, tiled=True),
            lax.all_gather(w_value, "dp", axis=0, tiled=True),
            lax.all_gather(w_output, "dp", axis=0, tiled=True),
            lax.all_gather(gain_moe, "dp", axis=0, tiled=True),
            lax.all_gather(router, "dp", axis=0, tiled=True),
            lax.all_gather(rel_bias, "dp", axis=0, tiled=True),
        )
        gain_a, query_w, key_w, value_w, output_w, gain_m, router_w, bias_table = weights_now
        gain_af = gain_a.astype(jnp.float32)
        gain_mf = gain_m.astype(jnp.float32)
        inputs = layer_in[step_index].astype(jnp.float32)
        scaled_a, inverse_a, normed_a = norm_forward(inputs, gain_af)
        normed_ab = normed_a.astype(jnp.bfloat16)
        queries = jnp.dot(normed_ab, query_w, preferred_element_type=jnp.float32).astype(
            jnp.bfloat16
        )
        keys_loc = jnp.dot(normed_ab, key_w, preferred_element_type=jnp.float32).astype(
            jnp.bfloat16
        )
        values_loc = jnp.dot(normed_ab, value_w, preferred_element_type=jnp.float32).astype(
            jnp.bfloat16
        )
        keys_all, values_all = (
            lax.all_gather(keys_loc, "expert", axis=0, tiled=True),
            lax.all_gather(values_loc, "expert", axis=0, tiled=True),
        )
        q_heads = split_heads(queries, heads)
        k_heads = split_heads(keys_all, heads)
        v_heads = split_heads(values_all, heads)
        bias = jnp.einsum(
            "qkb,bh->hqk", bucket_onehot, bias_table, preferred_element_type=jnp.float32
        )
        seg_all = segments[step_index]
        seg_here = lax.dynamic_slice_in_dim(seg_all, rank_here * tok_rows, tok_rows)
        allowed = causal & (seg_here[:, None] == seg_all[None, :])
        scores = score_block(q_heads, k_heads, bias, allowed, scale)
        top_score = jnp.max(scores, axis=-1, keepdims=True)
        lifted = jnp.exp(scores - top_score)
        total = jnp.sum(lifted, axis=-1, keepdims=True)
        log_total = top_score + jnp.log(total)
        probs_b = (lifted / total).astype(jnp.bfloat16)
        attended = merge_heads(
            jnp.einsum("hqk,hkd->hqd", probs_b, v_heads, preferred_element_type=jnp.float32)
        ).astype(jnp.bfloat16)
        resid = inputs + jnp.dot(attended, output_w, preferred_element_type=jnp.float32)
        scaled_m, inverse_m, normed_m = norm_forward(resid, gain_mf)
        normed_mb = normed_m.astype(jnp.bfloat16)
        logits = jnp.dot(normed_mb, router_w, preferred_element_type=jnp.float32)
        router_probs = jax.nn.softmax(logits, axis=-1)
        routes_now = routes[step_index]
        pick_first = (routes_now[:, 0:1] == expert_ids[None, :]).astype(jnp.float32)
        pick_second = (routes_now[:, 1:2] == expert_ids[None, :]).astype(jnp.float32)
        prob_first = jnp.sum(router_probs * pick_first, axis=-1)
        prob_second = jnp.sum(router_probs * pick_second, axis=-1)
        denom = prob_first + prob_second
        gate_first = prob_first / denom
        gate_second = prob_second / denom
        flat = routes_now.reshape(-1)
        flat_hot = (flat[:, None] == expert_ids[None, :]).astype(jnp.bfloat16)
        before = jnp.dot(earlier, flat_hot, preferred_element_type=jnp.float32)
        places = jnp.sum(before * flat_hot.astype(jnp.float32), axis=1).astype(jnp.int32)
        slot_pairs = (flat * capacity + places).reshape(tok_rows, 2)
        place_first = (slot_ids[:, None] == slot_pairs[None, :, 0]).astype(jnp.bfloat16)
        place_second = (slot_ids[:, None] == slot_pairs[None, :, 1]).astype(jnp.bfloat16)
        place_both = place_first + place_second
        outgoing = jnp.dot(place_both, normed_mb, preferred_element_type=jnp.float32).astype(
            jnp.bfloat16
        )
        outgoing = outgoing.reshape(group_size, local_experts, capacity, D)
        arrived_rows = lax.all_to_all(outgoing, "expert", split_axis=0, concat_axis=0, tiled=True)
        pre_act = jnp.einsum(
            "sjcd,jdf->sjcf", arrived_rows, w_expert_in, preferred_element_type=jnp.float32
        )
        post_act = jax.nn.gelu(pre_act).astype(jnp.bfloat16)
        produced = jnp.einsum(
            "sjcf,jfd->sjcd", post_act, w_expert_out, preferred_element_type=jnp.float32
        ).astype(jnp.bfloat16)
        produced, pre_act, post_act, arrived = (produced, pre_act, post_act, arrived_rows)
        returned = lax.all_to_all(
            produced, "expert", split_axis=0, concat_axis=0, tiled=True
        ).reshape(expert_count * capacity, D)
        got_first = jnp.einsum(
            "st,sd->td", place_first, returned, preferred_element_type=jnp.float32
        )
        got_second = jnp.einsum(
            "st,sd->td", place_second, returned, preferred_element_type=jnp.float32
        )
        result = resid + (gate_first[:, None] * got_first + gate_second[:, None] * got_second)
        outputs_list.append(result.astype(jnp.bfloat16))
        grad_top = out_grad[step_index].astype(jnp.float32)
        dgate_first = jnp.sum(grad_top * got_first, axis=-1)
        dgate_second = jnp.sum(grad_top * got_second, axis=-1)
        sent_first = (gate_first[:, None] * grad_top).astype(jnp.bfloat16)
        sent_second = (gate_second[:, None] * grad_top).astype(jnp.bfloat16)
        grad_slots = (
            jnp.dot(place_first, sent_first, preferred_element_type=jnp.float32)
            + jnp.dot(place_second, sent_second, preferred_element_type=jnp.float32)
        ).astype(jnp.bfloat16)
        grad_slots = grad_slots.reshape(group_size, local_experts, capacity, D)
        grad_arrived = lax.all_to_all(grad_slots, "expert", split_axis=0, concat_axis=0, tiled=True)
        grad_post = jnp.einsum(
            "sjcd,jfd->sjcf", grad_arrived, w_expert_out, preferred_element_type=jnp.float32
        )
        out_sum = out_sum + jnp.einsum(
            "sjcf,sjcd->jfd", post_act, grad_arrived, preferred_element_type=jnp.float32
        )
        grad_pre = jax.vjp(jax.nn.gelu, pre_act)[1](grad_post)[0].astype(jnp.bfloat16)
        in_sum = in_sum + jnp.einsum(
            "sjcd,sjcf->jdf", arrived, grad_pre, preferred_element_type=jnp.float32
        )
        grad_rows = jnp.einsum(
            "sjcf,jdf->sjcd", grad_pre, w_expert_in, preferred_element_type=jnp.float32
        ).astype(jnp.bfloat16)
        grad_back = lax.all_to_all(
            grad_rows, "expert", split_axis=0, concat_axis=0, tiled=True
        ).reshape(expert_count * capacity, D)
        grad_moe = jnp.einsum(
            "st,sd->td", place_both, grad_back, preferred_element_type=jnp.float32
        )
        weighted = dgate_first * gate_first + dgate_second * gate_second
        grad_pick = ((dgate_first - weighted) / denom)[:, None] * pick_first + (
            (dgate_second - weighted) / denom
        )[:, None] * pick_second
        grad_logits = router_probs * (
            grad_pick - jnp.sum(router_probs * grad_pick, axis=-1, keepdims=True)
        )
        normed_mf = normed_mb.astype(jnp.float32)
        grad_router_w = jnp.dot(normed_mf.T, grad_logits, precision=TOP_PRECISION)
        grad_moe = grad_moe + jnp.dot(
            grad_logits, router_w.astype(jnp.float32).T, precision=TOP_PRECISION
        )
        grad_resid_norm, grad_gain_m = norm_backward(grad_moe, scaled_m, inverse_m, gain_mf)
        grad_resid = grad_top + grad_resid_norm
        grad_branch = grad_resid.astype(jnp.bfloat16)
        grad_output_w = jnp.einsum(
            "td,te->de", attended, grad_branch, preferred_element_type=jnp.float32
        )
        grad_attended = jnp.einsum(
            "te,de->td", grad_branch, output_w, preferred_element_type=jnp.float32
        ).astype(jnp.bfloat16)
        grad_heads = split_heads(grad_attended, heads)
        scores_again = score_block(q_heads, k_heads, bias, allowed, scale)
        probs_again = jnp.exp(scores_again - log_total)
        probs_again_b = probs_again.astype(jnp.bfloat16)
        grad_probs = jnp.einsum(
            "hqd,hkd->hqk", grad_heads, v_heads, preferred_element_type=jnp.float32
        )
        row_delta = jnp.sum(probs_again * grad_probs, axis=-1, keepdims=True)
        grad_scores = probs_again * (grad_probs - row_delta)
        grad_table = jnp.einsum(
            "hqk,qkb->bh", grad_scores, bucket_onehot.astype(jnp.float32), precision=TOP_PRECISION
        )
        grad_scores_b = (grad_scores * scale).astype(jnp.bfloat16)
        grad_q_heads = jnp.einsum(
            "hqk,hkd->hqd", grad_scores_b, k_heads, preferred_element_type=jnp.float32
        )
        grad_v_heads = jnp.einsum(
            "hqk,hqd->hkd", probs_again_b, grad_heads, preferred_element_type=jnp.float32
        )
        grad_k_heads = jnp.einsum(
            "hqk,hqd->hkd", grad_scores_b, q_heads, preferred_element_type=jnp.float32
        )
        grad_keys, grad_values = (
            lax.psum_scatter(merge_heads(grad_k_heads), "expert", scatter_dimension=0, tiled=True),
            lax.psum_scatter(merge_heads(grad_v_heads), "expert", scatter_dimension=0, tiled=True),
        )
        grad_queries_b = merge_heads(grad_q_heads).astype(jnp.bfloat16)
        grad_keys_b = grad_keys.astype(jnp.bfloat16)
        grad_values_b = grad_values.astype(jnp.bfloat16)
        grad_query_w = jnp.einsum(
            "td,te->de", normed_ab, grad_queries_b, preferred_element_type=jnp.float32
        )
        grad_key_w = jnp.einsum(
            "td,te->de", normed_ab, grad_keys_b, preferred_element_type=jnp.float32
        )
        grad_value_w = jnp.einsum(
            "td,te->de", normed_ab, grad_values_b, preferred_element_type=jnp.float32
        )
        grad_normed = (
            jnp.einsum("te,de->td", grad_queries_b, query_w, preferred_element_type=jnp.float32)
            + jnp.einsum("te,de->td", grad_keys_b, key_w, preferred_element_type=jnp.float32)
            + jnp.einsum("te,de->td", grad_values_b, value_w, preferred_element_type=jnp.float32)
        )
        grad_in_norm, grad_gain_a = norm_backward(grad_normed, scaled_a, inverse_a, gain_af)
        grads_list.append(grad_resid + grad_in_norm)
        parts_now = (
            grad_gain_a,
            grad_query_w,
            grad_key_w,
            grad_value_w,
            grad_output_w,
            grad_gain_m,
            grad_router_w,
            grad_table,
        )
        dense_sums = [running + addend for running, addend in zip(dense_sums, parts_now)]
    sum_gain_a, sum_query, sum_key, sum_value, sum_output, sum_gain_m, sum_router, sum_table = (
        dense_sums
    )
    summed = lax.psum(
        (sum_gain_a, sum_query, sum_key, sum_value, sum_output, sum_gain_m, sum_router, sum_table),
        "expert",
    )
    (
        full_gain_a,
        full_query,
        full_key,
        full_value,
        full_output,
        full_gain_m,
        full_router,
        full_table,
    ) = summed
    shares = (
        lax.psum_scatter(full_gain_a, "dp", scatter_dimension=0, tiled=True),
        lax.psum_scatter(full_query, "dp", scatter_dimension=0, tiled=True),
        lax.psum_scatter(full_key, "dp", scatter_dimension=0, tiled=True),
        lax.psum_scatter(full_value, "dp", scatter_dimension=0, tiled=True),
        lax.psum_scatter(full_output, "dp", scatter_dimension=0, tiled=True),
        lax.psum_scatter(full_gain_m, "dp", scatter_dimension=0, tiled=True),
        lax.psum_scatter(full_router, "dp", scatter_dimension=0, tiled=True),
        lax.psum_scatter(full_table, "dp", scatter_dimension=0, tiled=True),
    )
    expert_in_grad, expert_out_grad = (
        lax.psum(in_sum.astype(jnp.bfloat16), "dp").astype(jnp.float32),
        lax.psum(out_sum.astype(jnp.bfloat16), "dp").astype(jnp.float32),
    )
    layer_out = jnp.stack(outputs_list)
    grad_in = jnp.stack(grads_list)
    return (
        layer_out,
        grad_in,
        shares[0],
        shares[1],
        shares[2],
        shares[3],
        shares[4],
        shares[5],
        shares[6],
        shares[7],
        expert_in_grad,
        expert_out_grad,
    )


def solution(mesh):
    in_specs = (
        P(None, ("dp", "expert"), None),
        P(None, ("dp", "expert"), None),
        P(None, ("dp", "expert"), None),
        P(None, "dp"),
        P(),
        P("dp"),
        P("dp", None),
        P("dp", None),
        P("dp", None),
        P("dp", None),
        P("dp"),
        P("dp", None),
        P("dp", None),
        P("expert", None, None),
        P("expert", None, None),
    )
    out_specs = (
        P(None, ("dp", "expert"), None),
        P(None, ("dp", "expert"), None),
        P("dp"),
        P("dp", None),
        P("dp", None),
        P("dp", None),
        P("dp", None),
        P("dp"),
        P("dp", None),
        P("dp", None),
        P("expert", None, None),
        P("expert", None, None),
    )
    return jax.shard_map(
        on_device, mesh=mesh, in_specs=in_specs, out_specs=out_specs, check_vma=False
    )
```

profile of v0, /device:TPU:0, one launch (start us, length us, event | category | flops | bytes accessed | tf_op | source)
XLA Modules:
  0.0 1875.5 jit_solution(381780187712008868)
XLA Ops:
  39.6 23.1 %all-gather.21.cloned.1.call-done = bf16[768,768]{1,0:T(8,128)(2,1)} async-done(((bf16[96,768]{1,0:T(8,128)(2,1)}), bf16[768,768]{1,0:T(8,128)(2,1)}) %all-gather.21.cloned.1.call-update) | async-done | bytes 1179664 | tf_op jit(solution)/shard_map/all_gather | solution.py:111
  101.3 15.7 copy.159
  174.2 29.2 %all-gather.31.cloned.1.call-done = bf16[1024,768]{1,0:T(8,128)(2,1)} async-done(((bf16[256,768]{1,0:T(8,128)(2,1)}), bf16[1024,768]{1,0:T(8,128)(2,1)}) %all-gather.31.cloned.1.call-update) | async-done | bytes 1572880 | tf_op jit(solution)/shard_map/all_gather | solution.py:133
  219.9 21.6 %all-gather.33.cloned.1.call-done = bf16[1024,768]{1,0:T(8,128)(2,1)} async-done(((bf16[256,768]{1,0:T(8,128)(2,1)}), bf16[1024,768]{1,0:T(8,128)(2,1)}) %all-gather.33.cloned.1.call-update) | async-done | bytes 1572880 | tf_op jit(solution)/shard_map/all_gather | solution.py:134
  250.5 28.6 %all-gather.35.cloned.1.call-done = bf16[1024,768]{1,0:T(8,128)(2,1)} async-done(((bf16[256,768]{1,0:T(8,128)(2,1)}), bf16[1024,768]{1,0:T(8,128)(2,1)}) %all-gather.35.cloned.1.call-update) | async-done | bytes 1572880 | tf_op jit(solution)/shard_map/all_gather | solution.py:133
  294.8 21.8 %all-gather.37.cloned.1.call-done = bf16[1024,768]{1,0:T(8,128)(2,1)} async-done(((bf16[256,768]{1,0:T(8,128)(2,1)}), bf16[1024,768]{1,0:T(8,128)(2,1)}) %all-gather.37.cloned.1.call-update) | async-done | bytes 1572880 | tf_op jit(solution)/shard_map/all_gather | solution.py:134
  325.6 15.7 all-gather.25.cloned.1.call-done
  347.0 33.0 %all-gather.19.cloned.1.call-done = bf16[1024,768]{1,0:T(8,128)(2,1)} async-done(((bf16[256,768]{1,0:T(8,128)(2,1)}), bf16[1024,768]{1,0:T(8,128)(2,1)}) %all-gather.19.cloned.1.call-update) | async-done | bytes 1572880 | tf_op jit(solution)/shard_map/all_gather | solution.py:133
  402.4 15.6 all-gather.23.cloned.1.call-done
  437.3 26.2 %all-to-all-done.4 = bf16[4,1,192,768]{3,2,1,0:T(8,128)(2,1)S(1)} async-done(((bf16[4,1,192,768]{3,2,1,0:T(8,128)(2,1)}), bf16[4,1,192,768]{3,2,1,0:T(8,128)(2,1)S(1)}, u32[]{:S(2)}, u32[]{:S(2)}) %all-to-all-start.4) | async-done | bytes 1179680 | tf_op jit(solution)/shard_map/all_to_all | solution.py:179
  473.1 22.9 %all-to-all-done.2 = bf16[4,1,192,768]{3,2,1,0:T(8,128)(2,1)} async-done(((bf16[4,1,192,768]{3,2,1,0:T(8,128)(2,1)}), bf16[4,1,192,768]{3,2,1,0:T(8,128)(2,1)}, u32[]{:S(2)}, u32[]{:S(2)}) %all-to-all-start.2) | async-done | bytes 1179680 | tf_op jit(solution)/shard_map/all_to_all | solution.py:179
  703.4 24.7 %all-to-all-done.14 = bf16[4,1,192,768]{3,2,1,0:T(8,128)(2,1)S(1)} async-done(((bf16[4,1,192,768]{3,2,1,0:T(8,128)(2,1)}), bf16[4,1,192,768]{3,2,1,0:T(8,128)(2,1)S(1)}, u32[]{:S(2)}, u32[]{:S(2)}) %all-to-all-start.14) | async-done | bytes 1179680 | tf_op jit(solution)/shard_map/all_to_all | solution.py:209
  735.0 25.4 %all-to-all-done.12 = bf16[4,1,192,768]{3,2,1,0:T(8,128)(2,1)} async-done(((bf16[4,1,192,768]{3,2,1,0:T(8,128)(2,1)}), bf16[4,1,192,768]{3,2,1,0:T(8,128)(2,1)}, u32[]{:S(2)}, u32[]{:S(2)}) %all-to-all-start.12) | async-done | bytes 1179680 | tf_op jit(solution)/shard_map/all_to_all | solution.py:209
  769.4 23.4 %all-to-all-done.8 = bf16[4,1,192,768]{3,2,1,0:T(8,128)(2,1)} async-done(((bf16[4,1,192,768]{3,2,1,0:T(8,128)(2,1)}), bf16[4,1,192,768]{3,2,1,0:T(8,128)(2,1)}, u32[]{:S(2)}, u32[]{:S(2)}) %all-to-all-start.8) | async-done | bytes 1179680 | tf_op jit(solution)/shard_map/all_to_all | solution.py:209
  936.0 16.9 all-to-all-done.13
  1154.0 18.2 fusion.128
  1172.2 17.6 fusion.131
  1214.5 16.3 copy.197
  1230.8 16.1 copy.196
  1263.2 21.6 %convolution_bitcast_fusion.1 = f32[32,12]{1,0:T(8,128)} fusion(f32[12,256,1024]{1,0,2:T(8,128)} %copy.197, s32[256,1024]{0,1:T(8,128)S(1)} %copy-done.117, s32[32]{0:T(128)S(1)} %copy-done.265, s32[32]{0:T(128)S(1)} %copy-done.263), kind=kOutput, calls=%fused_computation.296 | convolution fusion | flops 1233125376 | bytes 13633280 | tf_op jit(solution)/shard_map/hqk,qkb->bh/dot_general | solution.py:259
  1284.8 21.8 %convolution_bitcast_fusion.2 = f32[32,12]{1,0:T(8,128)} fusion(f32[12,256,1024]{1,0,2:T(8,128)} %copy.196, s32[256,1024]{0,1:T(8,128)S(1)} %copy-done.117, s32[32]{0:T(128)S(1)} %copy-done.265, s32[32]{0:T(128)S(1)} %copy-done.263), kind=kOutput, calls=%fused_computation.297 | convolution fusion | flops 1233125376 | bytes 13633280 | tf_op jit(solution)/shard_map/hqk,qkb->bh/dot_general | solution.py:259
  1306.6 15.9 copy.195
  1322.5 16.0 copy.198
  1343.3 21.7 %convolution_bitcast_fusion = f32[32,12]{1,0:T(8,128)} fusion(f32[12,256,1024]{1,0,2:T(8,128)} %copy.198, s32[256,1024]{0,1:T(8,128)} %copy.156, s32[32]{0:T(128)} %copy-done.264, s32[32]{0:T(128)} %copy-done.262), kind=kOutput, calls=%fused_computation.295 | convolution fusion | flops 1233125376 | bytes 13633280 | tf_op jit(solution)/shard_map/hqk,qkb->bh/dot_general | solution.py:259
  1384.3 24.3 %fusion.264 = f32[32,12]{1,0:T(8,128)S(1)} fusion(f32[32,12]{1,0:T(8,128)S(1)} %copy-done.276, f32[32,12]{1,0:T(8,128)S(1)} %copy-done.274, f32[32,12]{1,0:T(8,128)S(1)} %copy-done.275, f32[12,256,1024]{1,0,2:T(8,128)} %copy.195, s32[256,1024]{0,1:T(8,128)S(1)} %copy-done.118, s32[32]{0:T(128)} %copy-done.264, s32[32]{0:T(128)} %copy-done.262), kind=kOutput, calls=%fused_computation.301 | convolution fusion | flops 1233126528 | bytes 13637888 | tf_op jit(solution)/shard_map/hqk,qkb->bh/dot_general | solution.py:259
  1418.1 56.5 %reduce-scatter.28.cloned.1.call-done = f32[256,768]{0,1:T(8,128)} async-done(((f32[1024,768]{0,1:T(8,128)}), f32[256,768]{0,1:T(8,128)}) %reduce-scatter.28.cloned.1.call-update) | async-done | bytes 786448 | tf_op jit(solution)/shard_map/reduce_scatter | solution.py:273
  1481.4 135.8 %all-reduce.15.cloned.1.call-done = (bf16[1,768,3072]{2,1,0:T(8,128)(2,1)}, bf16[1,3072,768]{2,1,0:T(8,128)(2,1)}) async-done(((bf16[1,768,3072]{2,1,0:T(8,128)(2,1)}, bf16[1,3072,768]{2,1,0:T(8,128)(2,1)}), (bf16[1,768,3072]{2,1,0:T(8,128)(2,1)}, bf16[1,3072,768]{2,1,0:T(8,128)(2,1)})) %all-reduce.15.cloned.1.call-update) | async-done | bytes 9437200 | tf_op jit(solution)/shard_map/psum | solution.py:334
  1636.4 22.9 %all-reduce.5 = (f32[768]{0:T(1024)S(1)}, f32[768]{0:T(1024)S(1)}, f32[32,12]{1,0:T(8,128)S(1)}) all-reduce(f32[768]{0:T(1024)S(1)} %add_add_fusion.5, f32[768]{0:T(1024)S(1)} %copy-done.196, f32[32,12]{1,0:T(8,128)S(1)} %fusion.264), channel_id=10, replica_groups=mesh['dp'=8,'expert'=4] {'dp'}, use_global_device_ids=true, to_apply=%region_74.75.clone | all-reduce | flops 1920 | bytes 15360
  1663.8 45.7 %reduce-scatter.32.cloned.1.call-done = f32[96,768]{1,0:T(8,128)} async-done(((f32[768,768]{1,0:T(8,128)}), f32[96,768]{1,0:T(8,128)}) %reduce-scatter.32.cloned.1.call-update) | async-done | bytes 294928 | tf_op jit(solution)/shard_map/reduce_scatter | solution.py:325
  1709.5 46.2 %reduce-scatter.36.cloned.1.call-done = f32[96,768]{1,0:T(8,128)} async-done(((f32[768,768]{1,0:T(8,128)}), f32[96,768]{1,0:T(8,128)}) %reduce-scatter.36.cloned.1.call-update) | async-done | bytes 294928 | tf_op jit(solution)/shard_map/reduce_scatter | solution.py:327
  1755.7 46.3 %reduce-scatter.34.cloned.1.call-done = f32[96,768]{1,0:T(8,128)} async-done(((f32[768,768]{1,0:T(8,128)}), f32[96,768]{1,0:T(8,128)}) %reduce-scatter.34.cloned.1.call-update) | async-done | bytes 294928 | tf_op jit(solution)/shard_map/reduce_scatter | solution.py:326
  1820.8 40.8 %all-reduce.13.cloned.1.call-done = (f32[96,768]{1,0:T(8,128)}, f32[96,768]{1,0:T(8,128)}, f32[96,768]{1,0:T(8,128)}, f32[96,768]{1,0:T(8,128)}) async-done(((f32[96,768]{1,0:T(8,128)}, f32[96,768]{1,0:T(8,128)}, f32[96,768]{1,0:T(8,128)}, f32[96,768]{1,0:T(8,128)}), (f32[96,768]{1,0:T(8,128)}, f32[96,768]{1,0:T(8,128)}, f32[96,768]{1,0:T(8,128)}, f32[96,768]{1,0:T(8,128)})) %all-reduce.13.cloned.1.call-update) | async-done | bytes 1179664 | tf_op jit(solution)/shard_map/psum | solution.py:309
  (945 shorter events, 927.0 us)
Async XLA Ops:
  7.9 54.8 %all-gather.21.cloned.1.call-start = ((), (), s32[]{:S(2)}) async-start(), calls=%async_computation.32 | async-start | bytes 1327104 | tf_op jit(solution)/shard_map/all_gather | solution.py:111
  8.7 110.9 %all-gather.15.cloned.1.call-start = ((), (), s32[]{:S(2)}) async-start(), calls=%async_computation.29 | async-start | bytes 1327104 | tf_op jit(solution)/shard_map/all_gather | solution.py:109
  9.4 125.7 %all-gather.27.cloned.1.call-start = ((), (), s32[]{:S(2)}) async-start(), calls=%async_computation.35 | async-start | bytes 1966080 | tf_op jit(solution)/shard_map/all_gather | solution.py:133
  39.5 125.7 %all-gather.29.cloned.1.call-start = ((), (), s32[]{:S(2)}) async-start(), calls=%async_computation.36 | async-start | bytes 1966080 | tf_op jit(solution)/shard_map/all_gather | solution.py:134
  65.3 138.1 %all-gather.31.cloned.1.call-start = ((), (), s32[]{:S(2)}) async-start(), calls=%async_computation.37 | async-start | bytes 1966080 | tf_op jit(solution)/shard_map/all_gather | solution.py:133
  66.7 174.9 %all-gather.33.cloned.1.call-start = ((), (), s32[]{:S(2)}) async-start(), calls=%async_computation.38 | async-start | bytes 1966080 | tf_op jit(solution)/shard_map/all_gather | solution.py:134
  69.3 209.8 %all-gather.35.cloned.1.call-start = ((), (), s32[]{:S(2)}) async-start(), calls=%async_computation.39 | async-start | bytes 1966080 | tf_op jit(solution)/shard_map/all_gather | solution.py:133
  70.7 246.0 %all-gather.37.cloned.1.call-start = ((), (), s32[]{:S(2)}) async-start(), calls=%async_computation.40 | async-start | bytes 1966080 | tf_op jit(solution)/shard_map/all_gather | solution.py:134
  73.3 268.0 %all-gather.25.cloned.1.call-start = ((), (), s32[]{:S(2)}) async-start(), calls=%async_computation.34 | async-start | bytes 1327104 | tf_op jit(solution)/shard_map/all_gather | solution.py:112
  73.9 306.1 %all-gather.19.cloned.1.call-start = ((), (), s32[]{:S(2)}) async-start(), calls=%async_computation.31 | async-start | bytes 1966080 | tf_op jit(solution)/shard_map/all_gather | solution.py:133
  100.6 317.4 %all-gather.23.cloned.1.call-start = ((), (), s32[]{:S(2)}) async-start(), calls=%async_computation.33 | async-start | bytes 1966080 | tf_op jit(solution)/shard_map/all_gather | solution.py:134
  463.5 32.4 %all-to-all-start.2 = ((bf16[4,1,192,768]{3,2,1,0:T(8,128)(2,1)}), bf16[4,1,192,768]{3,2,1,0:T(8,128)(2,1)}, u32[]{:S(2)}, u32[]{:S(2)}) async-start(bf16[4,1,192,768]{3,2,1,0:T(8,128)(2,1)} %bitcast.1055), calls=%async_computation.2 | async-start | bytes 2359296 | tf_op jit(solution)/shard_map/all_to_all | solution.py:179
  495.9 32.4 %all-to-all-start.6 = ((bf16[4,1,192,768]{3,2,1,0:T(8,128)(2,1)}), bf16[4,1,192,768]{3,2,1,0:T(8,128)(2,1)}, u32[]{:S(2)}, u32[]{:S(2)}) async-start(bf16[4,1,192,768]{3,2,1,0:T(8,128)(2,1)} %bitcast.1057), calls=%async_computation.6 | async-start | bytes 2359296 | tf_op jit(solution)/shard_map/all_to_all | solution.py:179
  728.1 32.4 %all-to-all-start.12 = ((bf16[4,1,192,768]{3,2,1,0:T(8,128)(2,1)}), bf16[4,1,192,768]{3,2,1,0:T(8,128)(2,1)}, u32[]{:S(2)}, u32[]{:S(2)}) async-start(bf16[4,1,192,768]{3,2,1,0:T(8,128)(2,1)} %bitcast.179), calls=%async_computation.16 | async-start | bytes 2359296 | tf_op jit(solution)/shard_map/all_to_all | solution.py:209
  760.5 32.4 %all-to-all-start.8 = ((bf16[4,1,192,768]{3,2,1,0:T(8,128)(2,1)}), bf16[4,1,192,768]{3,2,1,0:T(8,128)(2,1)}, u32[]{:S(2)}, u32[]{:S(2)}) async-start(bf16[4,1,192,768]{3,2,1,0:T(8,128)(2,1)} %bitcast.121), calls=%async_computation.8 | async-start | bytes 2359296 | tf_op jit(solution)/shard_map/all_to_all | solution.py:209
  764.8 426.4 %reduce-scatter.40.cloned.1.call-start = ((), (), s32[]{:S(2)}) async-start(), calls=%async_computation.53 | async-start | bytes 442368
  887.9 32.6 %all-to-all-start.15 = ((bf16[4,1,192,768]{3,2,1,0:T(8,128)(2,1)}), bf16[4,1,192,768]{3,2,1,0:T(8,128)(2,1)}, u32[]{:S(2)}, u32[]{:S(2)}) async-start(bf16[4,1,192,768]{3,2,1,0:T(8,128)(2,1)} %fusion.190), calls=%async_computation.21 | async-start | bytes 2359296 | tf_op jit(solution)/shard_map/all_to_all | solution.py:223
  920.5 32.4 %all-to-all-start.13 = ((bf16[4,1,192,768]{3,2,1,0:T(8,128)(2,1)}), bf16[4,1,192,768]{3,2,1,0:T(8,128)(2,1)}, u32[]{:S(2)}, u32[]{:S(2)}) async-start(bf16[4,1,192,768]{3,2,1,0:T(8,128)(2,1)} %fusion.195), calls=%async_computation.17 | async-start | bytes 2359296 | tf_op jit(solution)/shard_map/all_to_all | solution.py:223
  924.7 440.3 %reduce-scatter.22.cloned.1.call-start = ((), (), s32[]{:S(2)}) async-start(), calls=%async_computation.44 | async-start | bytes 3932160 | tf_op jit(solution)/shard_map/reduce_scatter | solution.py:274
  977.0 391.2 %reduce-scatter.26.cloned.1.call-start = ((), (), s32[]{:S(2)}) async-start(), calls=%async_computation.46 | async-start | bytes 3932160 | tf_op jit(solution)/shard_map/reduce_scatter | solution.py:274
  990.1 381.2 %reduce-scatter.18.cloned.1.call-start = ((), (), s32[]{:S(2)}) async-start(), calls=%async_computation.42 | async-start | bytes 3932160 | tf_op jit(solution)/shard_map/reduce_scatter | solution.py:274
  1005.1 369.4 %reduce-scatter.30.cloned.1.call-start = ((), (), s32[]{:S(2)}) async-start(), calls=%async_computation.48 | async-start | bytes 3932160 | tf_op jit(solution)/shard_map/reduce_scatter | solution.py:274
  1014.5 394.1 %reduce-scatter.16.cloned.1.call-start = ((), (), s32[]{:S(2)}) async-start(), calls=%async_computation.41 | async-start | bytes 3932160 | tf_op jit(solution)/shard_map/reduce_scatter | solution.py:273
  1033.4 378.5 %reduce-scatter.24.cloned.1.call-start = ((), (), s32[]{:S(2)}) async-start(), calls=%async_computation.45 | async-start | bytes 3932160 | tf_op jit(solution)/shard_map/reduce_scatter | solution.py:273
  1052.4 362.6 %reduce-scatter.20.cloned.1.call-start = ((), (), s32[]{:S(2)}) async-start(), calls=%async_computation.43 | async-start | bytes 3932160 | tf_op jit(solution)/shard_map/reduce_scatter | solution.py:273
  1082.5 392.1 %reduce-scatter.28.cloned.1.call-start = ((), (), s32[]{:S(2)}) async-start(), calls=%async_computation.47 | async-start | bytes 3932160 | tf_op jit(solution)/shard_map/reduce_scatter | solution.py:273
  1132.0 485.2 %all-reduce.15.cloned.1.call-start = ((), (), s32[]{:S(2)}) async-start(), calls=%async_computation.55 | async-start | bytes 18874368 | tf_op jit(solution)/shard_map/psum | solution.py:334
  1189.8 474.0 %reduce-scatter.38.cloned.1.call-start = ((), (), s32[]{:S(2)}) async-start(), calls=%async_computation.52 | async-start | bytes 2654208 | tf_op jit(solution)/shard_map/reduce_scatter | solution.py:328
  1212.4 497.1 %reduce-scatter.32.cloned.1.call-start = ((), (), s32[]{:S(2)}) async-start(), calls=%async_computation.49 | async-start | bytes 2654208 | tf_op jit(solution)/shard_map/reduce_scatter | solution.py:325
  1284.8 470.9 %reduce-scatter.36.cloned.1.call-start = ((), (), s32[]{:S(2)}) async-start(), calls=%async_computation.51 | async-start | bytes 2654208 | tf_op jit(solution)/shard_map/reduce_scatter | solution.py:327
  1380.0 422.1 %reduce-scatter.34.cloned.1.call-start = ((), (), s32[]{:S(2)}) async-start(), calls=%async_computation.50 | async-start | bytes 2654208 | tf_op jit(solution)/shard_map/reduce_scatter | solution.py:326
  1480.0 381.7 %all-reduce.13.cloned.1.call-start = ((), (), s32[]{:S(2)}) async-start(), calls=%async_computation.54 | async-start | bytes 2359296 | tf_op jit(solution)/shard_map/psum | solution.py:309
  (299 other events, 6299.1 us)
Sparse Core Ops, SparseCore 0:
  9.9 26.7 all-gather.16
  38.6 24.0 all-gather.20
  64.6 24.0 all-gather.14
  90.2 37.0 all-gather.26
  129.3 35.9 all-gather.28
  167.3 36.0 all-gather.30
  205.5 35.9 all-gather.32
  243.1 35.9 all-gather.34
  280.6 35.9 all-gather.36
  318.4 22.9 all-gather.24
  342.9 37.0 all-gather.18
  382.0 35.9 all-gather.22
  768.7 35.1 reduce-scatter.39
  977.1 59.2 reduce-scatter.21
  1038.6 60.2 reduce-scatter.25
  1101.1 60.2 reduce-scatter.17
  1163.5 60.2 reduce-scatter.29
  1226.6 60.2 reduce-scatter.15
  1289.2 60.2 reduce-scatter.23
  1351.7 60.2 reduce-scatter.19
  1414.3 60.2 reduce-scatter.27
  1478.9 138.2 all-reduce.14
  1621.0 42.7 reduce-scatter.37
  1667.0 42.4 reduce-scatter.31
  1713.2 42.4 reduce-scatter.35
  1759.5 42.4 reduce-scatter.33
  1804.7 56.8 all-reduce.12
where the time goes:
time: 1890 us; the launch traced here: 1880 us
  waiting for transfers between devices  820 us (43%)
  matrix products  631 us (33%)
  local copies, waits for them, and re-layouts  186 us (10%)
  other arithmetic  85 us (4%)
  blocking collectives  68.4 us (4%)
  starting transfers between devices  64.9 us (3%)
  between operations  20.8 us (1%)
    psum x1, waiting for transfers between devices, on_device(): lax.psum(in_sum.astype(jnp.bfloat16), 'dp').astype(jnp.float32)  136 us
    all_gather x4, waiting for transfers between devices, on_device(): lax.all_gather(keys_loc, 'expert', axis=0, tiled=True)  90.8 us
    dot_general x4, matrix products, on_device(): jnp.einsum('hqk,qkb->bh', grad_scores, bucket_onehot.astype(jnp.float32),...  89.4 us
    all_to_all x4, waiting for transfers between devices, on_device(): lax.all_to_all(grad_slots, 'expert', split_axis=0, concat_axis=0, tiled=T...  80.1 us
    all_gather x4, waiting for transfers between devices, on_device(): lax.all_gather(values_loc, 'expert', axis=0, tiled=True)  72.6 us
    unnamed x595, local copies, waits for them, and re-layouts  71.6 us
    all_to_all x4, waiting for transfers between devices, on_device(): lax.all_to_all(outgoing, 'expert', split_axis=0, concat_axis=0, tiled=True)  70.4 us
    mul x4, local copies, waits for them, and re-layouts, on_device(): grad_scores = probs_again * (grad_probs - row_delta)  64.3 us
  transfers between devices with their start and end apart: 43, of which 33 were waited for; matrix products, arithmetic and copies ran while one was open for 44% of the time, Pallas kernels for 0%

commit v1 on v0

--- a/solution.py
+++ b/solution.py
@@ -1,8 +1,11 @@
+import functools
 import math
 
 import jax
 import jax.numpy as jnp
 from jax import lax
+from jax.experimental import pallas as pl
+from jax.experimental.pallas import tpu as pltpu
 from jax.sharding import PartitionSpec as P
 
 D = 768
@@ -13,6 +16,8 @@
 EPSILON = 1e-06
 MASKED = -1e30
 TOP_PRECISION = lax.Precision.HIGHEST
+GELU_A = math.sqrt(2.0 / math.pi)
+GELU_B = 0.044715
 
 
 def norm_forward(values, gain):
@@ -352,6 +357,516 @@
     )
 
 
+F32 = jnp.float32
+BF16 = jnp.bfloat16
+TILE = 256
+VMEM_LIMIT = 60 * 2**20
+
+
+def nn(left, right):
+    return lax.dot_general(left, right, (((1,), (0,)), ((), ())), preferred_element_type=F32)
+
+
+def nt(left, right):
+    return lax.dot_general(left, right, (((1,), (1,)), ((), ())), preferred_element_type=F32)
+
+
+def tn(left, right):
+    return lax.dot_general(left, right, (((0,), (0,)), ((), ())), preferred_element_type=F32)
+
+
+def call(body, name, grid, ins, outs, out_shapes, scratch=(), flops=0, nbytes=0):
+    return pl.pallas_call(
+        body,
+        grid=grid,
+        in_specs=ins,
+        out_specs=outs,
+        out_shape=out_shapes,
+        scratch_shapes=list(scratch),
+        compiler_params=pltpu.CompilerParams(
+            dimension_semantics=("arbitrary",) * len(grid), vmem_limit_bytes=VMEM_LIMIT
+        ),
+        cost_estimate=pl.CostEstimate(flops=flops, bytes_accessed=nbytes, transcendentals=0),
+        name=name,
+    )
+
+
+def whole(shape):
+    zeros = (0,) * len(shape)
+    return pl.BlockSpec(shape, lambda *_: zeros)
+
+
+def rows(width, tile=TILE):
+    return pl.BlockSpec((tile, width), lambda i: (i, 0))
+
+
+def sds(shape, dtype):
+    return jax.ShapeDtypeStruct(shape, dtype)
+
+
+def weight(wall_ref, index, share):
+    return wall_ref[:, index * share : (index + 1) * share, :].reshape(-1, D)
+
+
+def bias_kernel(bias_ref, table_ref):
+    row = bias_ref[0]
+    for delta in range(table_ref.shape[1]):
+        ahead = row[:, delta * TILE : (delta + 1) * TILE]
+        back = row[:, (delta - 1) * TILE : delta * TILE] if delta else jnp.zeros_like(ahead)
+        line = jnp.concatenate([ahead, back], axis=1)
+        grid = jnp.broadcast_to(line, (TILE, 2 * TILE))
+        grid = pltpu.roll(grid, 0, 1, stride=1, stride_axis=0)
+        table_ref[0, delta] = grid[:, :TILE].astype(BF16)
+
+
+def project_kernel(x_ref, gain_ref, wall_ref, a_ref, q_ref, k_ref, v_ref, *, share, scale):
+    x = x_ref[...].astype(F32)
+    inverse = lax.rsqrt(jnp.mean(x * x, axis=-1, keepdims=True) + EPSILON)
+    normed = (x * inverse * gain_ref[...]).astype(BF16)
+    a_ref[...] = normed
+    q = nn(normed, weight(wall_ref, 0, share)).astype(BF16)
+    q_ref[...] = (q.astype(F32) * scale).astype(BF16)
+    k_ref[...] = nn(normed, weight(wall_ref, 1, share)).astype(BF16)
+    v_ref[...] = nn(normed, weight(wall_ref, 2, share)).astype(BF16)
+
+
+def masked_scores(k, q, table_ref, head, i, j, seg_col, seg_row):
+    scores = nt(k, q) + table_ref[head, i - j].astype(F32)
+    allowed = seg_col == seg_row
+    if i == j:
+        key_at = lax.broadcasted_iota(jnp.int32, (TILE, TILE), 0)
+        query_at = lax.broadcasted_iota(jnp.int32, (TILE, TILE), 1)
+        allowed = allowed & (key_at <= query_at)
+    return jnp.where(allowed, scores, MASKED)
+
+
+def attend_kernel(q_ref, k_ref, v_ref, table_ref, col_ref, row_ref, o_ref, lse_ref, *, width):
+    blocks = q_ref.shape[0] // TILE
+    heads = q_ref.shape[1] // width
+    turned = [v_ref[:, h * width : (h + 1) * width].T for h in range(heads)]
+    for i in range(blocks):
+        here = slice(i * TILE, (i + 1) * TILE)
+        outs = []
+        for h in range(heads):
+            lanes = slice(h * width, (h + 1) * width)
+            q = q_ref[here, lanes]
+            pieces = []
+            for j in range(i + 1):
+                there = slice(j * TILE, (j + 1) * TILE)
+                pieces.append(
+                    masked_scores(
+                        k_ref[there, lanes], q, table_ref, h, i, j, col_ref[there, :], row_ref[:, here]
+                    )
+                )
+            top = pieces[0].max(axis=0, keepdims=True)
+            for piece in pieces[1:]:
+                top = jnp.maximum(top, piece.max(axis=0, keepdims=True))
+            total = jnp.zeros_like(top)
+            acc = jnp.zeros((width, TILE), F32)
+            for j, piece in enumerate(pieces):
+                lifted = jnp.exp(piece - top)
+                total = total + lifted.sum(axis=0, keepdims=True)
+                acc = acc + nn(turned[h][:, j * TILE : (j + 1) * TILE], lifted.astype(BF16))
+            outs.append(acc / total)
+            lse_ref[0, h : h + 1, here] = top + jnp.log(total)
+        o_ref[here, :] = jnp.concatenate(outs, axis=0).T.astype(BF16)
+
+
+def attend_back_kernel(
+    q_ref, k_ref, v_ref, do_ref, table_ref, col_ref, row_ref, lse_ref,
+    dq_ref, dk_ref, dv_ref, dist_ref, sum_ref, dk_sum, dv_sum, *, width, scale
+):
+    blocks = q_ref.shape[0] // TILE
+    heads = q_ref.shape[1] // width
+    turned = [k_ref[:, h * width : (h + 1) * width].T for h in range(heads)]
+    dist_ref[...] = jnp.zeros_like(dist_ref)
+    for h in range(heads):
+        lanes = slice(h * width, (h + 1) * width)
+        for i in range(blocks):
+            here = slice(i * TILE, (i + 1) * TILE)
+            q = q_ref[here, lanes]
+            do = do_ref[here, lanes]
+            lse = lse_ref[0, h : h + 1, here]
+            probs, dprobs = [], []
+            delta = jnp.zeros((1, TILE), F32)
+            for j in range(i + 1):
+                there = slice(j * TILE, (j + 1) * TILE)
+                scores = masked_scores(
+                    k_ref[there, lanes], q, table_ref, h, i, j, col_ref[there, :], row_ref[:, here]
+                )
+                p = jnp.exp(scores - lse)
+                dp = nt(v_ref[there, lanes], do)
+                delta = delta + (p * dp).sum(axis=0, keepdims=True)
+                probs.append(p)
+                dprobs.append(dp)
+            turned_dq = jnp.zeros((width, TILE), F32)
+            for j in range(i + 1):
+                there = slice(j * TILE, (j + 1) * TILE)
+                ds = probs[j] * (dprobs[j] - delta)
+                low = ds.astype(BF16)
+                dv = nn(probs[j].astype(BF16), do)
+                dk = nn(low, q)
+                if i == j:
+                    dv_sum[there, lanes] = dv
+                    dk_sum[there, lanes] = dk
+                else:
+                    dv_sum[there, lanes] += dv
+                    dk_sum[there, lanes] += dk
+                turned_dq = turned_dq + nn(turned[h][:, there], low)
+                if j == 0:
+                    sum_ref[i - j] = ds
+                else:
+                    sum_ref[i - j] += ds
+            dq_ref[here, lanes] = (turned_dq * scale).T.astype(BF16)
+        for gap in range(blocks):
+            part = sum_ref[gap]
+            part = jnp.concatenate([part, jnp.zeros_like(part)], axis=1)
+            half = TILE // 2
+            while half:
+                part = part[:half] + pltpu.roll(part[half : 2 * half], 2 * TILE - half, 1)
+                half //= 2
+            dist_ref[0, h : h + 1, gap * TILE : (gap + 1) * TILE] += part[:, :TILE]
+            if gap:
+                dist_ref[0, h : h + 1, (gap - 1) * TILE : gap * TILE] += part[:, TILE:]
+    dk_ref[...] = dk_sum[...].astype(BF16)
+    dv_ref[...] = dv_sum[...].astype(BF16)
+
+
+def route_kernel(
+    x_ref, o_ref, wall_ref, gain_ref, router_ref, routes_ref, h_ref, a_ref, gate_ref, pr_ref,
+    *, share, experts
+):
+    h1 = x_ref[...].astype(F32) + nn(o_ref[...], weight(wall_ref, 3, share))
+    h_ref[...] = h1
+    inverse = lax.rsqrt(jnp.mean(h1 * h1, axis=-1, keepdims=True) + EPSILON)
+    normed = (h1 * inverse * gain_ref[...]).astype(BF16)
+    a_ref[...] = normed
+    logits = nn(normed, router_ref[...])
+    lane = lax.broadcasted_iota(jnp.int32, logits.shape, 1)
+    logits = jnp.where(lane < experts, logits, MASKED)
+    lifted = jnp.exp(logits - logits.max(axis=-1, keepdims=True))
+    pr = lifted / lifted.sum(axis=-1, keepdims=True)
+    named = (routes_ref[:, 0:1] == lane) | (routes_ref[:, 1:2] == lane)
+    picked = jnp.where(named, pr, 0.0)
+    pr_ref[...] = pr
+    gate_ref[...] = picked / picked.sum(axis=-1, keepdims=True)
+
+
+def expert_kernel(
+    a_ref, g_ref, gate_ref, pos_ref, w_ref, eo_ref, da_ref, dw_ref, rows_a, rows_d, eo_sum, da_sum,
+    *, index, capacity
+):
+    step = pl.program_id(0)
+
+    @pl.when(step == 0)
+    def _():
+        tokens = a_ref.shape[0]
+        slot = lax.broadcasted_iota(jnp.int32, (capacity, tokens), 0)
+        pick = (pos_ref[index : index + 1, :] == slot).astype(BF16)
+        rows_a[...] = nn(pick, a_ref[...]).astype(BF16)
+        scaled = (gate_ref[:, index : index + 1] * g_ref[...].astype(F32)).astype(BF16)
+        rows_d[...] = nn(pick, scaled).astype(BF16)
+        eo_sum[...] = jnp.zeros_like(eo_sum)
+        da_sum[...] = jnp.zeros_like(da_sum)
+
+    a = rows_a[...]
+    d = rows_d[...]
+    w_in = w_ref[0, 0]
+    w_out = w_ref[0, 1]
+    u = nt(a, w_in)
+    cube = u * u
+    t = jnp.tanh(GELU_A * u * (1.0 + GELU_B * cube))
+    half = 0.5 * (1.0 + t)
+    z = (u * half).astype(BF16)
+    eo_sum[...] += nn(z, w_out)
+    dw_ref[0, 1] = tn(z, d).astype(BF16)
+    slope = half + (0.5 * GELU_A) * u * (1.0 - t * t) * (1.0 + 3.0 * GELU_B * cube)
+    du = (nt(d, w_out) * slope).astype(BF16)
+    da_sum[...] += nn(du, w_in)
+    dw_ref[0, 0] = tn(du, a).astype(BF16)
+
+    @pl.when(step == pl.num_programs(0) - 1)
+    def _():
+        eo_ref[...] = eo_sum[...].astype(BF16)
+        da_ref[...] = da_sum[...].astype(BF16)
+
+
+def combine_kernel(
+    h_ref, a_ref, g_ref, o_ref, gate_ref, pr_ref, routes_ref, pos_ref, eo0, eo1, eo2, eo3,
+    da0, da1, da2, da3, wall_ref, gain_ref, router_ref,
+    out_ref, dh_ref, do_ref, dw_ref, dgain_ref, drouter_ref, *, share, experts, capacity
+):
+    step = pl.program_id(0)
+
+    @pl.when(step == 0)
+    def _():
+        dw_ref[...] = jnp.zeros_like(dw_ref)
+        dgain_ref[...] = jnp.zeros_like(dgain_ref)
+        drouter_ref[...] = jnp.zeros_like(drouter_ref)
+
+    tile = h_ref.shape[0]
+    h1 = h_ref[...]
+    g = g_ref[...].astype(F32)
+    gates = gate_ref[...]
+    pr = pr_ref[...]
+    lane = lax.broadcasted_iota(jnp.int32, pr.shape, 1)
+    slot = lax.broadcasted_iota(jnp.int32, (tile, capacity), 1)
+    result = h1
+    dgate = jnp.zeros_like(pr)
+    da = jnp.zeros_like(h1)
+    for k, (eo, back) in enumerate(((eo0, da0), (eo1, da1), (eo2, da2), (eo3, da3))):
+        place = (pos_ref[:, k : k + 1] == slot).astype(BF16)
+        got = nn(place, eo[...])
+        result = result + gates[:, k : k + 1] * got
+        dgate = jnp.where(lane == k, jnp.sum(g * got, axis=-1, keepdims=True), dgate)
+        da = da + nn(place, back[...])
+    out_ref[...] = result.astype(BF16)
+    named = (routes_ref[:, 0:1] == lane) | (routes_ref[:, 1:2] == lane)
+    denom = jnp.sum(jnp.where(named, pr, 0.0), axis=-1, keepdims=True)
+    weighted = jnp.sum(dgate * gates, axis=-1, keepdims=True)
+    dpr = jnp.where(named, (dgate - weighted) / denom, 0.0)
+    dlog = pr * (dpr - jnp.sum(pr * dpr, axis=-1, keepdims=True))
+    high = dlog.astype(BF16)
+    lost = (dlog - high.astype(F32)).astype(BF16)
+    a = a_ref[...]
+    drouter_ref[...] += tn(a, high) + tn(a, lost)
+    for k in range(experts):
+        da = da + dlog[:, k : k + 1] * router_ref[k : k + 1, :]
+    inverse = lax.rsqrt(jnp.mean(h1 * h1, axis=-1, keepdims=True) + EPSILON)
+    n2 = h1 * inverse
+    dgain_ref[...] += jnp.sum(da * n2, axis=0, keepdims=True)
+    dn = da * gain_ref[...]
+    dh = g + inverse * (dn - n2 * jnp.mean(dn * n2, axis=-1, keepdims=True))
+    dh_ref[...] = dh
+    dy = dh.astype(BF16)
+    do_ref[...] = nt(dy, weight(wall_ref, 3, share)).astype(BF16)
+    dw_ref[...] += tn(o_ref[...], dy)
+
+
+def finish_kernel(
+    x_ref, a_ref, dq_ref, dk_ref, dv_ref, dh_ref, wall_ref, gain_ref, dwo_ref,
+    din_ref, pack_ref, dgain_ref, sum_ref, *, share
+):
+    step = pl.program_id(0)
+
+    @pl.when(step == 0)
+    def _():
+        sum_ref[...] = jnp.zeros_like(sum_ref)
+        dgain_ref[...] = jnp.zeros_like(dgain_ref)
+
+    a = a_ref[...]
+    da = jnp.zeros(dh_ref.shape, F32)
+    for index, grad_ref in enumerate((dq_ref, dk_ref, dv_ref)):
+        grad = grad_ref[...]
+        sum_ref[index] += tn(a, grad)
+        da = da + nt(grad, weight(wall_ref, index, share))
+    x = x_ref[...].astype(F32)
+    inverse = lax.rsqrt(jnp.mean(x * x, axis=-1, keepdims=True) + EPSILON)
+    n1 = x * inverse
+    dgain_ref[...] += jnp.sum(da * n1, axis=0, keepdims=True)
+    dn = da * gain_ref[...]
+    din = dh_ref[...] + inverse * (dn - n1 * jnp.mean(dn * n1, axis=-1, keepdims=True))
+    din_ref[...] = din.astype(BF16)
+
+    @pl.when(step == pl.num_programs(0) - 1)
+    def _():
+        for index in range(3):
+            pack_ref[:, index * share : (index + 1) * share, :] = (
+                sum_ref[index].astype(BF16).reshape(-1, share, D)
+            )
+        pack_ref[:, 3 * share :, :] = dwo_ref[...].astype(BF16).reshape(-1, share, D)
+
+
+def unpack_kernel(w_ref, in_ref, out_ref):
+    in_ref[0] = w_ref[0, 0].astype(F32).T
+    out_ref[0] = w_ref[0, 1].astype(F32)
+
+
+def on_device_whole(
+    layer_in, out_grad, routes, segments, buckets, gain_attn, w_query, w_key, w_value, w_output,
+    gain_moe, router, rel_bias, w_expert_in, w_expert_out,
+):
+    group = lax.axis_size("expert")
+    rank = lax.axis_index("expert")
+    shards = lax.axis_size("dp")
+    shard = lax.axis_index("dp")
+    experts = router.shape[1]
+    seq = segments.shape[1]
+    heads = rel_bias.shape[1]
+    width = D // heads
+    scale = 1.0 / math.sqrt(width)
+    share = D // shards
+    ff = w_expert_in.shape[2]
+    chunk = ff // shards
+    blocks = seq // TILE
+    capacity = 3 * seq // group
+    pairs = 128 // width
+
+    def across(values):
+        return lax.all_to_all(values, "expert", split_axis=0, concat_axis=1, tiled=True)[0]
+
+    x = across(layer_in)
+    routes_here = jnp.remainder(across(routes) - rank, experts)
+    g = across(out_grad)
+    row = lambda v: jnp.pad(v.reshape(1, -1), ((0, 0), (0, D - v.size)))
+    pack = jnp.concatenate(
+        [w_query, w_key, w_value, w_output, row(gain_attn), row(gain_moe), row(router), row(rel_bias),
+         jnp.zeros((4, D), BF16)], axis=0)
+    wall = lax.all_gather(pack, "dp", axis=0)
+    base = 4 * share
+    gain_a = wall[:, base, :share].reshape(1, D).astype(F32)
+    gain_m = wall[:, base + 1, :share].reshape(1, D).astype(F32)
+    router_all = wall[:, base + 2, : router.size].reshape(D, experts)
+    bias_all = wall[:, base + 3, : rel_bias.size].reshape(NB, heads)
+    turn = (jnp.arange(experts, dtype=jnp.int32)[:, None] == jnp.remainder(
+        jnp.arange(experts, dtype=jnp.int32)[None, :] + rank, experts)).astype(BF16)
+    router_rel = jnp.dot(router_all, turn, preferred_element_type=F32)
+    router_pad = jnp.pad(router_rel, ((0, 0), (0, 128 - experts))).astype(BF16)
+    router_turned = jnp.pad(router_rel.T, ((0, 8 - experts), (0, 0)))
+    own = jnp.stack([
+        lax.dynamic_slice_in_dim(w_expert_in[0], shard * chunk, chunk, axis=1).T,
+        lax.dynamic_slice_in_dim(w_expert_out[0], shard * chunk, chunk, axis=0),
+    ])
+    local = jnp.stack(
+        [w_expert_in[0].T.reshape(shards, chunk, D), w_expert_out[0].reshape(shards, chunk, D)], axis=1
+    )
+    weights = [local]
+    for k in range(1, experts):
+        moved = lax.ppermute(own, "expert", [((s + k) % group, s) for s in range(group)])
+        weights.append(lax.all_gather(moved, "dp", axis=0))
+    hot_buckets = (buckets[None, :] == jnp.arange(NB, dtype=jnp.int32)[:, None]).astype(BF16)
+    bias_line = lax.dot_general(
+        bias_all, hot_buckets, (((0,), (0,)), ((), ())), preferred_element_type=F32
+    ).reshape(heads, 1, seq)
+    table = call(
+        bias_kernel, "bias", (heads,),
+        [pl.BlockSpec((1, 1, seq), lambda i: (i, 0, 0))],
+        pl.BlockSpec((1, blocks, TILE, TILE), lambda i: (i, 0, 0, 0)),
+        sds((heads, blocks, TILE, TILE), BF16),
+    )(bias_line)
+    seg = lax.dynamic_slice_in_dim(segments, rank, 1, axis=0)
+    seg_row = seg.reshape(1, seq)
+    seg_col = seg.reshape(seq, 1)
+    expert_ids = jnp.arange(experts, dtype=jnp.int32)
+    named = (routes_here[:, 0:1] == expert_ids) | (routes_here[:, 1:2] == expert_ids)
+    at = jnp.arange(seq, dtype=jnp.int32)
+    before = jnp.dot(
+        (at[None, :] < at[:, None]).astype(BF16), named.astype(BF16), preferred_element_type=F32
+    ).astype(jnp.int32)
+    pos = jnp.where(named, before, -1)
+    pos_turned = jnp.pad(pos.T, ((0, 8 - experts), (0, 0)), constant_values=-1)
+
+    tokens = (seq, D)
+    normed, q, k, v = call(
+        functools.partial(project_kernel, share=share, scale=scale), "project", (blocks,),
+        [rows(D), whole((1, D)), whole(wall.shape)],
+        [rows(D)] * 4, [sds(tokens, BF16)] * 4, flops=6 * seq * D * D, nbytes=12 * 2**20,
+    )(x, gain_a, wall)
+    cols = pl.BlockSpec((seq, 128), lambda i: (0, i))
+    table_spec = pl.BlockSpec((pairs, blocks, TILE, TILE), lambda i: (i, 0, 0, 0))
+    line_spec = pl.BlockSpec((1, pairs, seq), lambda i: (i, 0, 0))
+    o, lse = call(
+        functools.partial(attend_kernel, width=width), "attend", (heads // pairs,),
+        [cols, cols, cols, table_spec, whole((seq, 1)), whole((1, seq))],
+        [cols, line_spec],
+        [sds(tokens, BF16), sds((heads // pairs, pairs, seq), F32)],
+        flops=8 * seq * seq * D, nbytes=16 * 2**20,
+    )(q, k, v, table, seg_col, seg_row)
+    h1, normed_m, gates, pr = call(
+        functools.partial(route_kernel, share=share, experts=experts), "route", (blocks,),
+        [rows(D), rows(D), whole(wall.shape), whole((1, D)), whole((D, 128)), rows(2)],
+        [rows(D), rows(D), rows(128), rows(128)],
+        [sds(tokens, F32), sds(tokens, BF16), sds((seq, 128), F32), sds((seq, 128), F32)],
+        flops=2 * seq * D * D, nbytes=12 * 2**20,
+    )(x, o, wall, gain_m, router_pad, routes_here)
+    produced, returned, partial_sums = [], [], []
+    slots = (capacity, D)
+    for index in range(experts):
+        eo, da, dw = call(
+            functools.partial(expert_kernel, index=index, capacity=capacity), f"expert{index}", (shards,),
+            [whole(tokens), whole(tokens), whole((seq, 128)), whole((8, seq)),
+             pl.BlockSpec((1, 2, chunk, D), lambda i: (i, 0, 0, 0))],
+            [whole(slots), whole(slots), pl.BlockSpec((1, 2, chunk, D), lambda i: (i, 0, 0, 0))],
+            [sds(slots, BF16), sds(slots, BF16), sds((shards, 2, chunk, D), BF16)],
+            [pltpu.VMEM(slots, BF16), pltpu.VMEM(slots, BF16), pltpu.VMEM(slots, F32), pltpu.VMEM(slots, F32)],
+            flops=12 * capacity * D * ff, nbytes=24 * 2**20,
+        )(normed_m, g, gates, pos_turned, weights[index])
+        produced.append(eo)
+        returned.append(da)
+        partial_sums.append(lax.psum_scatter(dw, "dp", scatter_dimension=0, tiled=True)[0])
+    result, dh, do, grad_output, grad_gain_m, grad_router = call(
+        functools.partial(combine_kernel, share=share, experts=experts, capacity=capacity), "combine",
+        (blocks,),
+        [rows(D)] * 4 + [rows(128), rows(128), rows(2), rows(experts)] + [whole(slots)] * 8
+        + [whole(wall.shape), whole((1, D)), whole((8, D))],
+        [rows(D), rows(D), rows(D), whole((D, D)), whole((1, D)), whole((D, 128))],
+        [sds(tokens, BF16), sds(tokens, F32), sds(tokens, BF16), sds((D, D), F32), sds((1, D), F32),
+         sds((D, 128), F32)],
+        flops=24 * seq * D * D, nbytes=32 * 2**20,
+    )(h1, normed_m, g, o, gates, pr, routes_here, pos, *produced, *returned, wall, gain_m, router_turned)
+    dq, dk, dv, dist = call(
+        functools.partial(attend_back_kernel, width=width, scale=scale), "attend_back", (heads // pairs,),
+        [cols, cols, cols, cols, table_spec, whole((seq, 1)), whole((1, seq)), line_spec],
+        [cols, cols, cols, line_spec],
+        [sds(tokens, BF16)] * 3 + [sds((heads // pairs, pairs, seq), F32)],
+        [pltpu.VMEM((blocks, TILE, TILE), F32), pltpu.VMEM((seq, 128), F32), pltpu.VMEM((seq, 128), F32)],
+        flops=20 * seq * seq * D, nbytes=24 * 2**20,
+    )(q, k, v, do, table, seg_col, seg_row, lse)
+    din, dense, grad_gain_a = call(
+        functools.partial(finish_kernel, share=share), "finish", (blocks,),
+        [rows(D)] * 6 + [whole(wall.shape), whole((1, D)), whole((D, D))],
+        [rows(D), whole((shards, 4 * share, D)), whole((1, D))],
+        [sds(tokens, BF16), sds((shards, 4 * share, D), BF16), sds((1, D), F32)],
+        [pltpu.VMEM((3, D, D), F32)],
+        flops=12 * seq * D * D, nbytes=24 * 2**20,
+    )(x, normed, dq, dk, dv, dh, wall, gain_a, grad_output)
+
+    def back(values):
+        return lax.all_to_all(
+            values.reshape(group, seq // group, D), "expert", split_axis=0, concat_axis=0, tiled=True
+        )
+
+    layer_out = back(result)
+    grad_in = back(din).astype(F32)
+    total = partial_sums[0].astype(F32)
+    for k in range(1, experts):
+        moved = lax.ppermute(partial_sums[k], "expert", [(s, (s + k) % group) for s in range(group)])
+        total = total + moved.astype(F32)
+    gathered = lax.all_gather(total.astype(BF16), "dp", axis=0)
+    expert_in, expert_out = call(
+        unpack_kernel, "unpack", (shards,),
+        [pl.BlockSpec((1, 2, chunk, D), lambda i: (i, 0, 0, 0))],
+        [pl.BlockSpec((1, D, chunk), lambda i: (0, 0, i)), pl.BlockSpec((1, chunk, D), lambda i: (0, i, 0))],
+        [sds(w_expert_in.shape, F32), sds(w_expert_out.shape, F32)], nbytes=28 * 2**20,
+    )(gathered)
+    dense = lax.psum(lax.psum_scatter(dense, "dp", scatter_dimension=0, tiled=True)[0], "expert").astype(F32)
+    grad_table = jnp.einsum(
+        "bx,hx->bh", hot_buckets.astype(F32), dist.reshape(heads, seq), precision=TOP_PRECISION
+    )
+    grad_router = jnp.dot(grad_router[:, :experts], turn.astype(F32).T, precision=TOP_PRECISION)
+    small = lax.psum(
+        jnp.concatenate([
+            grad_gain_a.reshape(shards, -1), grad_gain_m.reshape(shards, -1),
+            grad_router.reshape(shards, -1), grad_table.reshape(shards, -1)], axis=1),
+        ("dp", "expert"),
+    )
+    small = lax.dynamic_slice_in_dim(small, shard, 1, axis=0)[0]
+    return (
+        layer_out,
+        grad_in,
+        small[:share],
+        dense[:share],
+        dense[share : 2 * share],
+        dense[2 * share : 3 * share],
+        dense[3 * share :],
+        small[share : 2 * share],
+        small[2 * share : 2 * share + router.size].reshape(router.shape),
+        small[2 * share + router.size :].reshape(rel_bias.shape),
+        expert_in,
+        expert_out,
+    )
+
+
 def solution(mesh):
     in_specs = (
         P(None, ("dp", "expert"), None),
@@ -384,6 +899,7 @@
         P("expert", None, None),
         P("expert", None, None),
     )
+    body = on_device_whole if mesh.shape["expert"] == MICRO else on_device
     return jax.shard_map(
-        on_device, mesh=mesh, in_specs=in_specs, out_specs=out_specs, check_vma=False
-    )
+        body, mesh=mesh, in_specs=in_specs, out_specs=out_specs, check_vma=False
+    )

time: 1890 us -> 817 us (0.43)
  matrix products: 631 us -> 3.62 us
  waiting for transfers between devices: 820 us -> 299 us
  Pallas kernels: 0 us -> 290 us
  local copies, waits for them, and re-layouts: 186 us -> 40.4 us
  other arithmetic: 85 us -> 18.1 us
  blocking collectives: 68.4 us -> 122 us
  starting transfers between devices: 64.9 us -> 25.1 us
    dot_general x141 -> x5, matrix products: 631 us -> 3.62 us  [the longest x1 1.69 us: on_device_whole(): jnp.dot((at[None, :] < at[:, None]).astype(BF16), named.astype(BF16), pre...]
    pallas_call x0 -> x12, Pallas kernels: none -> 290 us  [the longest x4 152 us: on_device_whole(): call(functools.partial(expert_kernel, index=index, capacity=capacity), f'...]
    all_gather x12 -> x5, waiting for transfers between devices: 209 us -> 0.06 us  [the longest x3 0.06 us: on_device_whole(): weights.append(lax.all_gather(moved, 'dp', axis=0))]
    all_to_all x16 -> x3, waiting for transfers between devices: 232 us -> 32 us  [the longest x2 32 us: across(): lax.all_to_all(values, 'expert', split_axis=0, concat_axis=1, tiled=True)[0]]
    psum x2 -> x1, waiting for transfers between devices: 177 us -> 0.01 us  [on_device_whole(): lax.psum(lax.psum_scatter(dense, 'dp', scatter_dimension=0, tiled=True)[0...]
    ppermute x0 -> x6, waiting for transfers between devices: none -> 106 us  [the longest x3 106 us: on_device_whole(): lax.ppermute(own, 'expert', [((s + k) % group, s) for s in range(group)])]
    all_to_all x0 -> x2, blocking collectives: none -> 68.8 us  [the longest x1 58.6 us: back(): lax.all_to_all(values.reshape(group, seq // group, D), 'expert', split_ax...]
    mul x4 -> x0, local copies, waits for them, and re-layouts: 64.3 us -> none  [on_device(): grad_scores = probs_again * (grad_probs - row_delta)]
  transfers between devices with their start and end apart: 43 -> 20, of which waited for: 33 -> 7; matrix products, arithmetic and copies ran while one was open for 44% -> 6% of each run, Pallas kernels for 0% -> 34%
where the time goes in v1:
time: 817 us; the launch traced here: 812 us
  waiting for transfers between devices  299 us (37%)
  Pallas kernels  290 us (35%)
  blocking collectives  122 us (15%)
  local copies, waits for them, and re-layouts  40.4 us (5%)
  starting transfers between devices  25.1 us (3%)
  other arithmetic  18.1 us (2%)
  between operations  14.6 us (2%)
    pallas_call x4, Pallas kernels, on_device_whole(): call(functools.partial(expert_kernel, index=index, capacity=capacity), f'...  152 us
    ppermute x3, waiting for transfers between devices, on_device_whole(): lax.ppermute(own, 'expert', [((s + k) % group, s) for s in range(group)])  106 us
    reduce_scatter x4, waiting for transfers between devices, on_device_whole(): lax.psum_scatter(dw, 'dp', scatter_dimension=0, tiled=True)[0]  104 us
    all_to_all x1, blocking collectives, back(): lax.all_to_all(values.reshape(group, seq // group, D), 'expert', split_ax...  58.6 us
    reduce_scatter x1, waiting for transfers between devices, on_device_whole(): lax.psum_scatter(dense, 'dp', scatter_dimension=0, tiled=True)[0]  56.5 us
    psum x1, blocking collectives, on_device_whole(): lax.psum(jnp.concatenate([grad_gain_a.reshape(shards, -1), grad_gain_m.re...  52.8 us
    pallas_call x1, Pallas kernels, on_device_whole(): call(functools.partial(attend_back_kernel, width=width, scale=scale), 'at...  35.1 us
    all_to_all x2, waiting for transfers between devices, across(): lax.all_to_all(values, 'expert', split_axis=0, concat_axis=1, tiled=True)[0]  32 us
  transfers between devices with their start and end apart: 20, of which 7 were waited for; matrix products, arithmetic and copies ran while one was open for 6% of the time, Pallas kernels for 34%

profile of v1, /device:TPU:0, one launch (start us, length us, event | category | flops | bytes accessed | tf_op | source)
XLA Modules:
  0.0 812.0 jit_solution(7023266084023921146)
XLA Ops:
  10.3 6.9 concatenate.6
  19.9 4.1 collective-permute-start.1
  24.0 51.2 %collective-permute-done.1 = bf16[2,384,768]{2,1,0:T(8,128)(2,1)S(1)} collective-permute-done((bf16[2,384,768]{2,1,0:T(8,128)(2,1)S(1)}, bf16[2,384,768]{2,1,0:T(8,128)(2,1)S(1)}, u32[]{:S(2)}, u32[]{:S(2)}) %collective-permute-start.1) | collective-permute-done | bytes 1179680 | tf_op jit(solution)/shard_map/ppermute | solution.py:735
  77.1 29.0 %collective-permute-done.2 = bf16[2,384,768]{2,1,0:T(8,128)(2,1)S(1)} collective-permute-done((bf16[2,384,768]{2,1,0:T(8,128)(2,1)S(1)}, bf16[2,384,768]{2,1,0:T(8,128)(2,1)S(1)}, u32[]{:S(2)}, u32[]{:S(2)}) %collective-permute-start.2) | collective-permute-done | bytes 1179680 | tf_op jit(solution)/shard_map/ppermute | solution.py:735
  108.9 25.3 %collective-permute-done = bf16[2,384,768]{2,1,0:T(8,128)(2,1)S(1)} collective-permute-done((bf16[2,384,768]{2,1,0:T(8,128)(2,1)S(1)}, bf16[2,384,768]{2,1,0:T(8,128)(2,1)S(1)}, u32[]{:S(2)}, u32[]{:S(2)}) %collective-permute-start) | collective-permute-done | bytes 1179680 | tf_op jit(solution)/shard_map/ppermute | solution.py:735
  135.3 10.2 %all_to_all.37 = s32[4,256,2]{1,2,0:T(2,128)S(1)} all-to-all(s32[4,256,2]{1,2,0:T(2,128)S(1)} %copy-done.12), channel_id=1, replica_groups=mesh['dp'=8,'expert'=4] {'expert'}, dimensions={0} | all-to-all | bytes 16384 | tf_op jit(solution)/shard_map/all_to_all | solution.py:706
  145.5 3.6 all-to-all-start
  151.2 32.0 %all-to-all-done = bf16[4,256,768]{2,1,0:T(8,128)(2,1)S(1)} async-done(((bf16[4,256,768]{2,1,0:T(8,128)(2,1)}), bf16[4,256,768]{2,1,0:T(8,128)(2,1)S(1)}, u32[]{:S(2)}, u32[]{:S(2)}) %all-to-all-start) | async-done | bytes 1572896 | tf_op jit(solution)/shard_map/all_to_all | solution.py:706
  184.4 4.4 all-to-all-start.2
  195.4 8.0 bias.1.table_ref
  206.5 8.5 %project.1 = (bf16[1024,768]{1,0:T(8,128)(2,1)}, bf16[1024,768]{1,0:T(8,128)(2,1)}, bf16[1024,768]{1,0:T(8,128)(2,1)}, bf16[1024,768]{1,0:T(8,128)(2,1)}) custom-call(bf16[1024,768]{1,0:T(8,128)(2,1)} %bitcast.48, f32[1,768]{1,0:T(1,128)} %reshape.160.gain_ref, bf16[8,392,768]{2,1,0:T(8,128)(2,1)} %bitcast.56), custom_call_target="tpu_custom_call" | custom-call | flops 3623878656 | bytes 12582912 | tf_op jit(solution)/shard_map/project/pallas_call | solution.py:760
  215.0 23.3 %attend.1 = (bf16[1024,768]{1,0:T(8,128)(2,1)}, f32[6,2,1024]{2,1,0:T(2,128)}) custom-call(bf16[1024,768]{1,0:T(8,128)(2,1)} %get-tuple-element.49.q_ref, bf16[1024,768]{1,0:T(8,128)(2,1)} %get-tuple-element.50.k_ref, bf16[1024,768]{1,0:T(8,128)(2,1)} %get-tuple-element.51.v_ref, bf16[12,4,256,256]{3,2,1,0:T(8,128)(2,1)} %bias.1.table_ref, ...), custom_call_target="tpu_custom_call" | custom-call | flops 6442450944 | bytes 16777216 | tf_op jit(solution)/shard_map/attend/pallas_call | solution.py:768
  238.4 8.6 %route.1 = (f32[1024,768]{1,0:T(8,128)}, bf16[1024,768]{1,0:T(8,128)(2,1)}, f32[1024,128]{1,0:T(8,128)}, f32[1024,128]{1,0:T(8,128)}) custom-call(bf16[1024,768]{1,0:T(8,128)(2,1)} %bitcast.49, bf16[1024,768]{1,0:T(8,128)(2,1)} %get-tuple-element.52.o_ref, bf16[8,392,768]{2,1,0:T(8,128)(2,1)} %bitcast.57, f32[1,768]{1,0:T(1,128)} %reshape.161.gain_ref, ...), custom_call_target="tpu_custom_call" | custom-call | flops 1207959552 | bytes 12582912 | tf_op jit(solution)/shard_map/route/pallas_call | solution.py:775
  247.0 37.8 %expert2.1 = (bf16[768,768]{1,0:T(8,128)(2,1)}, bf16[768,768]{1,0:T(8,128)(2,1)}, bf16[8,2,384,768]{3,2,1,0:T(8,128)(2,1)}) custom-call(bf16[1024,768]{1,0:T(8,128)(2,1)} %get-tuple-element.54.a_ref, bf16[1024,768]{1,0:T(8,128)(2,1)} %bitcast.6.g_ref, f32[1024,128]{1,0:T(8,128)} %get-tuple-element.55.gate_ref, s32[8,1024]{1,0:T(8,128)} %pad.33.clone.pos_ref, ...), custom_call_target="tpu_custom_call" | custom-call | flops 21743271936 | bytes 25165824 | tf_op jit(solution)/shard_map/expert2/pallas_call | solution.py:785
  284.9 37.9 %expert3.1 = (bf16[768,768]{1,0:T(8,128)(2,1)}, bf16[768,768]{1,0:T(8,128)(2,1)}, bf16[8,2,384,768]{3,2,1,0:T(8,128)(2,1)}) custom-call(bf16[1024,768]{1,0:T(8,128)(2,1)} %get-tuple-element.54.a_ref, bf16[1024,768]{1,0:T(8,128)(2,1)} %bitcast.6.g_ref, f32[1024,128]{1,0:T(8,128)} %get-tuple-element.55.gate_ref, s32[8,1024]{1,0:T(8,128)} %pad.33.clone.pos_ref, ...), custom_call_target="tpu_custom_call" | custom-call | flops 21743271936 | bytes 25165824 | tf_op jit(solution)/shard_map/expert3/pallas_call | solution.py:785
  322.9 37.7 %expert1.1 = (bf16[768,768]{1,0:T(8,128)(2,1)}, bf16[768,768]{1,0:T(8,128)(2,1)}, bf16[8,2,384,768]{3,2,1,0:T(8,128)(2,1)}) custom-call(bf16[1024,768]{1,0:T(8,128)(2,1)} %get-tuple-element.54.a_ref, bf16[1024,768]{1,0:T(8,128)(2,1)} %bitcast.6.g_ref, f32[1024,128]{1,0:T(8,128)} %get-tuple-element.55.gate_ref, s32[8,1024]{1,0:T(8,128)} %pad.33.clone.pos_ref, ...), custom_call_target="tpu_custom_call" | custom-call | flops 21743271936 | bytes 25165824 | tf_op jit(solution)/shard_map/expert1/pallas_call | solution.py:785
  360.6 6.8 copy.71
  367.5 9.5 %pad_maximum_fusion.w_ref = bf16[8,2,384,768]{3,2,1,0:T(8,128)(2,1)} fusion(bf16[8,1,384,768]{3,2,1,0:T(8,128)(2,1)} %bitcast.52, bf16[8,1,384,768]{3,2,1,0:T(8,128)(2,1)} %bitcast.46), kind=kLoop, calls=%fused_computation | loop fusion | flops 4718592 | bytes 18874368 | tf_op jit(solution)/shard_map/stack | solution.py:730
  377.6 38.8 %expert0.1 = (bf16[768,768]{1,0:T(8,128)(2,1)}, bf16[768,768]{1,0:T(8,128)(2,1)}, bf16[8,2,384,768]{3,2,1,0:T(8,128)(2,1)}) custom-call(bf16[1024,768]{1,0:T(8,128)(2,1)} %get-tuple-element.54.a_ref, bf16[1024,768]{1,0:T(8,128)(2,1)} %bitcast.6.g_ref, f32[1024,128]{1,0:T(8,128)} %get-tuple-element.55.gate_ref, s32[8,1024]{1,0:T(8,128)} %pad.33.clone.pos_ref, ...), custom_call_target="tpu_custom_call" | custom-call | flops 21743271936 | bytes 25165824 | tf_op jit(solution)/shard_map/expert0/pallas_call | solution.py:785
  416.3 26.2 %combine.1 = (bf16[1024,768]{1,0:T(8,128)(2,1)}, f32[1024,768]{1,0:T(8,128)}, bf16[1024,768]{1,0:T(8,128)(2,1)}, f32[768,768]{1,0:T(8,128)}, f32[1,768]{1,0:T(1,128)}, /*index=5*/f32[768,128]{1,0:T(8,128)}) custom-call(f32[1024,768]{1,0:T(8,128)} %get-tuple-element.53.h_ref, bf16[1024,768]{1,0:T(8,128)(2,1)} %get-tuple-element.54.a_ref, ...), custom_call_target="tpu_custom_call" | custom-call | flops 14495514624 | bytes 33554432 | tf_op jit(solution)/shard_map/combine/pallas_call | solution.py:797
  442.6 35.1 %attend_back.1 = (bf16[1024,768]{1,0:T(8,128)(2,1)}, bf16[1024,768]{1,0:T(8,128)(2,1)}, bf16[1024,768]{1,0:T(8,128)(2,1)}, f32[6,2,1024]{2,1,0:T(2,128)}) custom-call(bf16[1024,768]{1,0:T(8,128)(2,1)} %get-tuple-element.49.q_ref, bf16[1024,768]{1,0:T(8,128)(2,1)} %get-tuple-element.50.k_ref, bf16[1024,768]{1,0:T(8,128)(2,1)} %get-tuple-element.51.v_ref, ...), custom_call_target="tpu_custom_call" | custom-call | flops 16106127360 | bytes 25165824 | tf_op jit(solution)/shard_map/attend_back/pallas_call | solution.py:807
  477.6 16.7 %finish.1 = (bf16[1024,768]{1,0:T(8,128)(2,1)}, bf16[8,384,768]{2,1,0:T(8,128)(2,1)}, f32[1,768]{1,0:T(1,128)}) custom-call(bf16[1024,768]{1,0:T(8,128)(2,1)} %bitcast.50, bf16[1024,768]{1,0:T(8,128)(2,1)} %get-tuple-element.66.a_ref, bf16[1024,768]{1,0:T(8,128)(2,1)} %get-tuple-element.69.dq_ref, bf16[1024,768]{1,0:T(8,128)(2,1)} %get-tuple-element.70.dk_ref, ...), custom_call_target="tpu_custom_call" | custom-call | flops 7247757312 | bytes 25165824 | tf_op jit(solution)/shard_map/finish/pallas_call | solution.py:815
  495.1 3.3 collective-permute-start.4
  500.0 22.7 %reduce-scatter.10.cloned.1.call-done = bf16[1,2,384,768]{3,2,1,0:T(8,128)(2,1)} async-done(((bf16[8,2,384,768]{3,2,1,0:T(8,128)(2,1)}), bf16[1,2,384,768]{3,2,1,0:T(8,128)(2,1)}) %reduce-scatter.10.cloned.1.call-update) | async-done | bytes 1179664 | tf_op jit(solution)/shard_map/reduce_scatter | solution.py:796
  524.1 56.5 %reduce-scatter.6.cloned.1.call-done = bf16[1,384,768]{2,1,0:T(8,128)(2,1)} async-done(((bf16[8,384,768]{2,1,0:T(8,128)(2,1)}), bf16[1,384,768]{2,1,0:T(8,128)(2,1)}) %reduce-scatter.6.cloned.1.call-update) | async-done | bytes 589840 | tf_op jit(solution)/shard_map/reduce_scatter | solution.py:842
  580.7 80.9 %reduce-scatter.8.cloned.1.call-done = bf16[1,2,384,768]{3,2,1,0:T(8,128)(2,1)} async-done(((bf16[8,2,384,768]{3,2,1,0:T(8,128)(2,1)}), bf16[1,2,384,768]{3,2,1,0:T(8,128)(2,1)}) %reduce-scatter.8.cloned.1.call-update) | async-done | bytes 1179664 | tf_op jit(solution)/shard_map/reduce_scatter | solution.py:796
  662.6 3.7 fusion.3
  666.3 58.6 %all_to_all.38 = bf16[4,256,768]{2,1,0:T(8,128)(2,1)S(1)} all-to-all(bf16[4,256,768]{2,1,0:T(8,128)(2,1)S(1)} %bitcast.62), channel_id=1, replica_groups=mesh['dp'=8,'expert'=4] {'expert'}, dimensions={0} | all-to-all | bytes 3145728 | tf_op jit(solution)/shard_map/all_to_all | solution.py:825
  724.9 3.7 all-to-all-start.3
  733.3 52.8 %psum.14 = f32[8,624]{1,0:T(8,128)S(1)} all-reduce(f32[8,624]{1,0:T(8,128)S(1)} %pad_maximum_fusion.2), channel_id=1, replica_groups=mesh['dp'=8,'expert'=4] {'dp','expert'}, use_global_device_ids=true, to_apply=%region_0.1 | all-reduce | flops 4992 | bytes 39936 | tf_op jit(solution)/shard_map/psum | solution.py:847
  790.2 2.2 fusion.25
  792.4 11.5 %unpack.1 = (f32[1,768,3072]{2,1,0:T(8,128)}, f32[1,3072,768]{2,1,0:T(8,128)}) custom-call(bf16[8,2,384,768]{3,2,1,0:T(8,128)(2,1)} %bitcast.47), custom_call_target="tpu_custom_call" | custom-call | bytes 29360128 | tf_op jit(solution)/shard_map/unpack/pallas_call | solution.py:836
  (124 shorter events, 40.0 us)
Async XLA Ops:
  7.2 142.0 %copy-start = (s32[4,1024]{1,0:T(4,128)S(1)}, s32[4,1024]{1,0:T(4,128)}, u32[]{:S(2)}) copy-start(s32[4,1024]{1,0:T(4,128)} %param.18) | copy-start | bytes 49156
  7.2 185.0 %all-gather.11.cloned.1.call-start = ((), (), s32[]{:S(2)}) async-start(), calls=%async_computation.16 | async-start | bytes 5419008 | tf_op jit(solution)/shard_map/all_gather | solution.py:715
  17.2 229.8 %all-gather.15.cloned.1.call-start = ((), (), s32[]{:S(2)}) async-start(), calls=%async_computation.18 | async-start | bytes 10616832 | tf_op jit(solution)/shard_map/all_gather | solution.py:736
  19.9 55.3 %collective-permute-start.1 = (bf16[2,384,768]{2,1,0:T(8,128)(2,1)S(1)}, bf16[2,384,768]{2,1,0:T(8,128)(2,1)S(1)}, u32[]{:S(2)}, u32[]{:S(2)}) collective-permute-start(bf16[2,384,768]{2,1,0:T(8,128)(2,1)S(1)} %pad_maximum_fusion.1), channel_id=1, source_target_pairs={{2,0},{3,1},{0,2},{1,3},{6,4},{7,5},{4,6},{5,7},{10,8},{11,9},{8,1... | collective-permute-start | bytes 3538952 | tf_op jit(solution)/shard_map/ppermute | solution.py:735
  75.2 60.1 %copy-start.12 = (s32[4,256,2]{1,2,0:T(2,128)S(1)}, s32[4,256,2]{1,2,0:T(2,128)}, u32[]{:S(2)}) copy-start(s32[4,256,2]{1,2,0:T(2,128)} %param.17) | copy-start | bytes 24580
  76.2 208.6 %all-gather.17.cloned.1.call-start = ((), (), s32[]{:S(2)}) async-start(), calls=%async_computation.19 | async-start | bytes 10616832 | tf_op jit(solution)/shard_map/all_gather | solution.py:736
  76.3 29.7 %collective-permute-start.2 = (bf16[2,384,768]{2,1,0:T(8,128)(2,1)S(1)}, bf16[2,384,768]{2,1,0:T(8,128)(2,1)S(1)}, u32[]{:S(2)}, u32[]{:S(2)}) collective-permute-start(bf16[2,384,768]{2,1,0:T(8,128)(2,1)S(1)} %pad_maximum_fusion.1), channel_id=1, source_target_pairs={{3,0},{0,1},{1,2},{2,3},{7,4},{4,5},{5,6},{6,7},{11,8},{8,9},{9,10... | collective-permute-start | bytes 3538952 | tf_op jit(solution)/shard_map/ppermute | solution.py:735
  106.0 1.0 copy-start.6
  107.1 215.8 %all-gather.13.cloned.1.call-start = ((), (), s32[]{:S(2)}) async-start(), calls=%async_computation.17 | async-start | bytes 10616832 | tf_op jit(solution)/shard_map/all_gather | solution.py:736
  107.1 27.1 %collective-permute-start = (bf16[2,384,768]{2,1,0:T(8,128)(2,1)S(1)}, bf16[2,384,768]{2,1,0:T(8,128)(2,1)S(1)}, u32[]{:S(2)}, u32[]{:S(2)}) collective-permute-start(bf16[2,384,768]{2,1,0:T(8,128)(2,1)S(1)} %pad_maximum_fusion.1), channel_id=1, source_target_pairs={{1,0},{2,1},{3,2},{0,3},{5,4},{6,5},{7,6},{4,7},{9,8},{10,9},{11,1... | collective-permute-start | bytes 3538952 | tf_op jit(solution)/shard_map/ppermute | solution.py:735
  145.5 37.8 %all-to-all-start = ((bf16[4,256,768]{2,1,0:T(8,128)(2,1)}), bf16[4,256,768]{2,1,0:T(8,128)(2,1)S(1)}, u32[]{:S(2)}, u32[]{:S(2)}) async-start(bf16[4,256,768]{2,1,0:T(8,128)(2,1)} %param.15), calls=%async_computation | async-start | bytes 3145728 | tf_op jit(solution)/shard_map/all_to_all | solution.py:706
  150.2 54.5 %copy-start.14 = (s32[4]{0:T(128)}, s32[4]{0:T(128)S(1)}, u32[]{:S(2)}) copy-start(s32[4]{0:T(128)S(1)} %and_select_fusion) | copy-start | bytes 52
  151.2 37.6 %copy-start.2 = (s32[1024,2]{1,0:T(8,128)}, s32[1024,2]{1,0:T(8,128)S(1)}, u32[]{:S(2)}) copy-start(s32[1024,2]{1,0:T(8,128)S(1)} %add_select_fusion.routes_ref) | copy-start | bytes 24580
  183.3 1.1 copy-start.3
  184.4 62.5 %all-to-all-start.2 = ((bf16[4,256,768]{2,1,0:T(8,128)(2,1)}), bf16[4,256,768]{2,1,0:T(8,128)(2,1)}, u32[]{:S(2)}, u32[]{:S(2)}) async-start(bf16[4,256,768]{2,1,0:T(8,128)(2,1)} %param.16), calls=%async_computation.2 | async-start | bytes 3145728 | tf_op jit(solution)/shard_map/all_to_all | solution.py:706
  188.8 306.3 %reduce-scatter.12.cloned.1.call-start = ((), (), s32[]{:S(2)}) async-start(), calls=%async_computation.14 | async-start | bytes 10616832 | tf_op jit(solution)/shard_map/reduce_scatter | solution.py:796
  189.4 5.2 copy-start.10
  284.8 213.7 %reduce-scatter.14.cloned.1.call-start = ((), (), s32[]{:S(2)}) async-start(), calls=%async_computation.15 | async-start | bytes 10616832 | tf_op jit(solution)/shard_map/reduce_scatter | solution.py:796
  322.8 199.9 %reduce-scatter.10.cloned.1.call-start = ((), (), s32[]{:S(2)}) async-start(), calls=%async_computation.13 | async-start | bytes 10616832 | tf_op jit(solution)/shard_map/reduce_scatter | solution.py:796
  360.6 220.0 %reduce-scatter.6.cloned.1.call-start = ((), (), s32[]{:S(2)}) async-start(), calls=%async_computation.10 | async-start | bytes 5308416 | tf_op jit(solution)/shard_map/reduce_scatter | solution.py:842
  494.3 167.2 %reduce-scatter.8.cloned.1.call-start = ((), (), s32[]{:S(2)}) async-start(), calls=%async_computation.12 | async-start | bytes 10616832 | tf_op jit(solution)/shard_map/reduce_scatter | solution.py:796
  495.1 295.2 %all-reduce.9.cloned.1.call-start = ((), (), s32[]{:S(2)}) async-start(), calls=%async_computation.11 | async-start | bytes 1179648 | tf_op jit(solution)/shard_map/psum | solution.py:842
  495.1 166.4 %collective-permute-start.4 = (bf16[2,384,768]{2,1,0:T(8,128)(2,1)}, bf16[2,384,768]{2,1,0:T(8,128)(2,1)S(1)}, u32[]{:S(2)}, u32[]{:S(2)}) collective-permute-start(bf16[2,384,768]{2,1,0:T(8,128)(2,1)} %bitcast.72), channel_id=1, source_target_pairs={{0,2},{1,3},{2,0},{3,1},{4,6},{5,7},{6,4},{7,5},{8,10},{9,11},{10,... | collective-permute-start | bytes 3538952 | tf_op jit(solution)/shard_map/ppermute | solution.py:833
  498.5 163.1 %collective-permute-start.5 = (bf16[2,384,768]{2,1,0:T(8,128)(2,1)}, bf16[2,384,768]{2,1,0:T(8,128)(2,1)S(1)}, u32[]{:S(2)}, u32[]{:S(2)}) collective-permute-start(bf16[2,384,768]{2,1,0:T(8,128)(2,1)} %bitcast.73), channel_id=1, source_target_pairs={{0,3},{1,0},{2,1},{3,2},{4,7},{5,4},{6,5},{7,6},{8,11},{9,8},{10,9... | collective-permute-start | bytes 3538952 | tf_op jit(solution)/shard_map/ppermute | solution.py:833
  522.6 139.9 %collective-permute-start.3 = (bf16[2,384,768]{2,1,0:T(8,128)(2,1)}, bf16[2,384,768]{2,1,0:T(8,128)(2,1)}, u32[]{:S(2)}, u32[]{:S(2)}) collective-permute-start(bf16[2,384,768]{2,1,0:T(8,128)(2,1)} %bitcast.74), channel_id=1, source_target_pairs={{0,1},{1,2},{2,3},{3,0},{4,5},{5,6},{6,7},{7,4},{8,9},{9,10},{10,1... | collective-permute-start | bytes 3538952 | tf_op jit(solution)/shard_map/ppermute | solution.py:833
  580.6 211.8 %all-gather.19.cloned.1.call-start = ((), (), s32[]{:S(2)}) async-start(), calls=%async_computation.20 | async-start | bytes 10616832 | tf_op jit(solution)/shard_map/all_gather | solution.py:835
  662.6 3.7 copy-start.4
  724.9 3.7 copy-start.13
  724.9 4.4 copy-start.9
  724.9 4.4 copy-start.11
  724.9 65.4 %all-to-all-start.3 = ((bf16[4,256,768]{2,1,0:T(8,128)(2,1)}), bf16[4,256,768]{2,1,0:T(8,128)(2,1)S(1)}, u32[]{:S(2)}, u32[]{:S(2)}) async-start(bf16[4,256,768]{2,1,0:T(8,128)(2,1)} %bitcast.61), calls=%async_computation.3 | async-start | bytes 3145728 | tf_op jit(solution)/shard_map/all_to_all | solution.py:825
  803.9 1.1 copy-start.1
  (3 other events, 3.0 us)
Sparse Core Ops, SparseCore 0:
  17.3 42.0 all-gather.10
  76.4 60.0 all-gather.14
  138.3 58.8 all-gather.16
  199.5 58.8 all-gather.12
  284.9 77.8 reduce-scatter.11
  366.1 76.4 reduce-scatter.13
  446.1 76.4 reduce-scatter.9
  526.7 53.8 reduce-scatter.5
  585.1 76.4 reduce-scatter.7
  663.9 57.3 all-reduce.8
  723.9 58.1 all-gather.18

commit v2 on v1

--- a/solution.py
+++ b/solution.py
@@ -375,7 +375,8 @@
     return lax.dot_general(left, right, (((0,), (0,)), ((), ())), preferred_element_type=F32)
 
 
-def call(body, name, grid, ins, outs, out_shapes, scratch=(), flops=0, nbytes=0):
+def call(body, name, grid, ins, outs, out_shapes, scratch=(), flops=0, nbytes=0, collective=None):
+    extra = {} if collective is None else {"collective_id": collective, "has_side_effects": True}
     return pl.pallas_call(
         body,
         grid=grid,
@@ -384,7 +385,7 @@
         out_shape=out_shapes,
         scratch_shapes=list(scratch),
         compiler_params=pltpu.CompilerParams(
-            dimension_semantics=("arbitrary",) * len(grid), vmem_limit_bytes=VMEM_LIMIT
+            dimension_semantics=("arbitrary",) * len(grid), vmem_limit_bytes=VMEM_LIMIT, **extra
         ),
         cost_estimate=pl.CostEstimate(flops=flops, bytes_accessed=nbytes, transcendentals=0),
         name=name,
@@ -400,34 +401,349 @@
     return pl.BlockSpec((tile, width), lambda i: (i, 0))
 
 
+MESH = pl.DeviceIdType.MESH
+ANY = pl.BlockSpec(memory_space=pl.ANY)
+
+
+def neighbours():
+    me = lax.axis_index("dp")
+    core = me + 1 - 2 * (me % 2)
+    along_x = me + 2 - 4 * ((me // 2) % 2)
+    along_y = me + 4 - 8 * (me // 4)
+    across = along_x + 4 - 8 * (me // 4)
+    return me, core, along_x, along_y, across
+
+
+def meet(devices):
+    barrier = pltpu.get_barrier_semaphore()
+    for device in devices:
+        pl.semaphore_signal(barrier, inc=1, device_id=device, device_id_type=MESH)
+    pl.semaphore_wait(barrier, len(devices))
+
+
+def plane_devices():
+    place = lax.axis_index("expert")
+    _, core, along_x, along_y, _ = neighbours()
+    return [(core, place), (along_x, place), (along_y, place)]
+
+
+GATHER_COPIES = 14
+
+
+def gather_copies(first, second, source_first, source_second, send, recv, local):
+    place = lax.axis_index("expert")
+    me, core, along_x, along_y, across = neighbours()
+
+    def remote(index, source, target, device):
+        return pltpu.make_async_remote_copy(
+            src_ref=source,
+            dst_ref=target,
+            send_sem=send.at[index],
+            recv_sem=recv.at[index],
+            device_id=(device, place),
+            device_id_type=MESH,
+        )
+
+    own = [
+        pltpu.make_async_copy(source_first, first.at[me], local.at[0]),
+        pltpu.make_async_copy(source_second, second.at[me], local.at[1]),
+    ]
+    stage0 = [
+        remote(0, source_first, first.at[me], along_x),
+        remote(1, source_second, second.at[me], along_y),
+        remote(2, source_first, first.at[me], core),
+        remote(3, source_second, second.at[me], core),
+    ]
+    stage1 = [
+        remote(4, first.at[along_x], first.at[along_x], along_y),
+        remote(5, second.at[along_y], second.at[along_y], along_x),
+        remote(6, source_first, first.at[me], along_y),
+        remote(7, source_second, second.at[me], along_x),
+        remote(8, first.at[along_x], first.at[along_x], core),
+        remote(9, second.at[along_y], second.at[along_y], core),
+    ]
+    stage2 = [
+        remote(10, first.at[along_y], first.at[along_y], core),
+        remote(11, second.at[along_x], second.at[along_x], core),
+        remote(12, first.at[across], first.at[across], core),
+        remote(13, second.at[across], second.at[across], core),
+    ]
+
+    def start0():
+        for copy in stage0 + own:
+            copy.start()
+
+    def start1():
+        stage0[0].wait_recv()
+        stage0[1].wait_recv()
+        for copy in stage1:
+            copy.start()
+
+    def start2():
+        for copy in stage1[:4]:
+            copy.wait_recv()
+        for copy in stage2:
+            copy.start()
+
+    def finish():
+        for copy in own:
+            copy.wait()
+        for copy in stage0[2:] + stage1[4:] + stage2:
+            copy.wait_recv()
+        for copy in stage0 + stage1 + stage2:
+            copy.wait_send()
+
+    return start0, start1, start2, finish
+
+
+def gather_sems():
+    return [
+        pltpu.SemaphoreType.DMA((GATHER_COPIES,)),
+        pltpu.SemaphoreType.DMA((GATHER_COPIES,)),
+        pltpu.SemaphoreType.DMA((2,)),
+    ]
+
+
 def sds(shape, dtype):
     return jax.ShapeDtypeStruct(shape, dtype)
 
 
-def weight(wall_ref, index, share):
-    return wall_ref[:, index * share : (index + 1) * share, :].reshape(-1, D)
-
-
-def bias_kernel(bias_ref, table_ref):
-    row = bias_ref[0]
-    for delta in range(table_ref.shape[1]):
-        ahead = row[:, delta * TILE : (delta + 1) * TILE]
-        back = row[:, (delta - 1) * TILE : delta * TILE] if delta else jnp.zeros_like(ahead)
-        line = jnp.concatenate([ahead, back], axis=1)
-        grid = jnp.broadcast_to(line, (TILE, 2 * TILE))
-        grid = pltpu.roll(grid, 0, 1, stride=1, stride_axis=0)
-        table_ref[0, delta] = grid[:, :TILE].astype(BF16)
-
-
-def project_kernel(x_ref, gain_ref, wall_ref, a_ref, q_ref, k_ref, v_ref, *, share, scale):
-    x = x_ref[...].astype(F32)
-    inverse = lax.rsqrt(jnp.mean(x * x, axis=-1, keepdims=True) + EPSILON)
-    normed = (x * inverse * gain_ref[...]).astype(BF16)
-    a_ref[...] = normed
-    q = nn(normed, weight(wall_ref, 0, share)).astype(BF16)
-    q_ref[...] = (q.astype(F32) * scale).astype(BF16)
-    k_ref[...] = nn(normed, weight(wall_ref, 1, share)).astype(BF16)
-    v_ref[...] = nn(normed, weight(wall_ref, 2, share)).astype(BF16)
+def place_devices(group):
+    me = lax.axis_index("dp")
+    place = lax.axis_index("expert")
+    return [(me, lax.rem(place + k, group)) for k in range(1, group)]
+
+
+def along_axis(source, target, send, recv, place):
+    return pltpu.make_async_remote_copy(
+        src_ref=source,
+        dst_ref=target,
+        send_sem=send,
+        recv_sem=recv,
+        device_id=(lax.axis_index("dp"), place),
+        device_id_type=MESH,
+    )
+
+
+def swap_copies(source, target, send, recv, group):
+    place = lax.axis_index("expert")
+    copies = []
+    for k in range(1, group):
+        other = lax.rem(place + k, group)
+        copies.append(along_axis(source.at[other], target.at[place], send.at[k], recv.at[k], other))
+    return copies
+
+
+def slice_copies(w_in, w_out, target, send, recv, base, place):
+    me = lax.axis_index("dp")
+    chunk = target.shape[2]
+    rows_in = w_in.at[0, :, pl.ds(pl.multiple_of(me * chunk, 128), chunk)]
+    rows_out = pl.ds(pl.multiple_of(me * chunk, 128), chunk)
+    pieces = (
+        (rows_in, target.at[0]),
+        (w_out.at[0, rows_out, pl.ds(0, chunk)], target.at[1, pl.ds(0, chunk)]),
+        (w_out.at[0, rows_out, pl.ds(chunk, chunk)], target.at[1, pl.ds(chunk, chunk)]),
+    )
+    return [
+        along_axis(source, goal, send.at[base + i], recv.at[base + i], place)
+        for i, (source, goal) in enumerate(pieces)
+    ]
+
+
+REDUCE_COPIES = 10
+
+
+def reduce_copies(terms, own, pair, inbox, send, recv, local, emit):
+    place = lax.axis_index("expert")
+    me, core, along_x, along_y, across = neighbours()
+    targets = (across, along_x, along_y, me)
+
+    def remote(index, source, target, device):
+        return pltpu.make_async_remote_copy(
+            src_ref=source,
+            dst_ref=target,
+            send_sem=send.at[index],
+            recv_sem=recv.at[index],
+            device_id=(device, place),
+            device_id_type=MESH,
+        )
+
+    loads = [pltpu.make_async_copy(terms.at[t], own.at[q], local.at[q]) for q, t in enumerate(targets)]
+    pairs = [
+        remote(q, terms.at[t + 1 - 2 * lax.rem(t, 2)], pair.at[q], core) for q, t in enumerate(targets)
+    ]
+    far_first = remote(4, own.at[0, 0], inbox.at[0], along_x)
+    far_second = remote(5, own.at[0, 1], inbox.at[1], along_y)
+    near_first = remote(6, own.at[1, 0], inbox.at[2], along_x)
+    near_second = remote(7, own.at[2, 1], inbox.at[3], along_y)
+    late_first = remote(8, own.at[2, 0], inbox.at[4], along_y)
+    late_second = remote(9, own.at[1, 1], inbox.at[5], along_x)
+
+    def merge(q):
+        loads[q].wait()
+        pairs[q].wait_recv()
+        own[q] = own[q] + pair[q]
+
+    def start():
+        for copy in loads + pairs:
+            copy.start()
+
+    def far():
+        merge(0)
+        far_first.start()
+        far_second.start()
+
+    def near():
+        merge(1)
+        near_first.start()
+        merge(2)
+        near_second.start()
+
+    def late():
+        far_first.wait_recv()
+        own[2, 0] = own[2, 0] + inbox[0]
+        late_first.start()
+        far_second.wait_recv()
+        own[1, 1] = own[1, 1] + inbox[1]
+        late_second.start()
+
+    def finish():
+        merge(3)
+        for copy in (near_first, near_second, late_first, late_second):
+            copy.wait_recv()
+        emit(0, own[3, 0].astype(F32) + inbox[2].astype(F32) + inbox[4].astype(F32))
+        emit(1, own[3, 1].astype(F32) + inbox[3].astype(F32) + inbox[5].astype(F32))
+        for copy in pairs + [far_first, far_second, near_first, near_second, late_first, late_second]:
+            copy.wait_send()
+
+    return start, far, near, late, finish
+
+
+def reduce_scratch(shape):
+    half = shape[1:]
+    return [
+        pltpu.VMEM((4, *shape), BF16),
+        pltpu.VMEM((4, *shape), BF16),
+        pltpu.VMEM((6, *half), BF16),
+        pltpu.SemaphoreType.DMA((REDUCE_COPIES,)),
+        pltpu.SemaphoreType.DMA((REDUCE_COPIES,)),
+        pltpu.SemaphoreType.DMA((4,)),
+    ]
+
+
+def weight(slots_ref, index, share):
+    return slots_ref[:, index * share : (index + 1) * share, :].reshape(-1, D)
+
+
+def open_kernel(
+    x_ref, routes_ref, w_in_ref, w_out_ref, wq_ref, wk_ref, wv_ref, wo_ref, small_ref, buckets_ref, seg_ref,
+    x_out, piece_out, first_out, second_out, a_ref, q_ref, k_ref, v_ref, params_ref, line_ref, across_ref, down_ref,
+    land, routes_land, first, second, stage_first, stage_second,
+    x_send, x_recv, r_send, r_recv, p_send, p_recv, keep, own_local, send, recv, local,
+    *, group, share, heads, experts, scale
+):
+    me = lax.axis_index("dp")
+    place = lax.axis_index("expert")
+    pieces = [
+        (wq_ref, stage_first.at[pl.ds(0, share)]),
+        (wk_ref, stage_first.at[pl.ds(share, share)]),
+        (wv_ref, stage_second.at[pl.ds(0, share)]),
+        (wo_ref, stage_second.at[pl.ds(share, share)]),
+    ]
+    staged = [pltpu.make_async_copy(src, dst, own_local.at[i]) for i, (src, dst) in enumerate(pieces)]
+    for copy in staged:
+        copy.start()
+    small = small_ref[...].astype(F32)
+    line = lax.broadcasted_iota(jnp.int32, small.shape, 0)
+    placed = jnp.where(line < 16, pltpu.roll(small, me * share, 1), pltpu.roll(small, me * 4, 1))
+    stage_second[2 * share :, :] = placed.astype(BF16)
+    meet(plane_devices() + place_devices(group))
+    moves = swap_copies(routes_ref, routes_land, r_send, r_recv, group)
+    moves_x = swap_copies(x_ref, land, x_send, x_recv, group)
+    slices = slice_copies(w_in_ref, w_out_ref, piece_out, p_send, p_recv, 0, lax.rem(place + group - 1, group))
+    kept = [
+        pltpu.make_async_copy(routes_ref.at[place], routes_land.at[place], keep.at[0]),
+        pltpu.make_async_copy(x_ref.at[place], land.at[place], keep.at[1]),
+    ]
+    for copy in moves + moves_x + slices + kept:
+        copy.start()
+    for copy in staged:
+        copy.wait()
+    start0, start1, start2, finish = gather_copies(first, second, stage_first, stage_second, send, recv, local)
+    start0()
+
+    kept[0].wait()
+    for copy in moves:
+        copy.wait_recv()
+    seq = down_ref.shape[0]
+    row_id = lax.broadcasted_iota(jnp.int32, (8, routes_land.shape[2]), 0)
+    named = []
+    for p in range(group):
+        picks = []
+        for c in range(2):
+            pick = routes_land[p, c : c + 1, :] - place
+            picks.append(jnp.where(pick < 0, pick + experts, pick))
+        named.append(((picks[0] == row_id) | (picks[1] == row_id)).astype(F32))
+    named = jnp.concatenate(named, axis=1)
+    earlier = lax.broadcasted_iota(jnp.int32, (seq, seq), 0) < lax.broadcasted_iota(jnp.int32, (seq, seq), 1)
+    before = nn(named.astype(BF16), earlier.astype(F32).astype(BF16))
+    pos = jnp.where(named > 0, before, -1.0)
+    which = lax.broadcasted_iota(jnp.int32, seg_ref.shape, 0)
+    segs = jnp.where(which == place, seg_ref[...], 0).astype(F32).sum(axis=0, keepdims=True)
+    stack = jnp.concatenate([pos, jnp.broadcast_to(segs, (8, seq))], axis=0)
+    across_ref[...] = stack.astype(jnp.int32)
+    filled = jnp.concatenate([stack, jnp.full((112, seq), -1.0, F32)], axis=0)
+    down_ref[...] = filled.T.astype(jnp.int32)
+
+    start1()
+    start2()
+    finish()
+    out_copies = [
+        pltpu.make_async_copy(first, first_out, own_local.at[0]),
+        pltpu.make_async_copy(second, second_out, own_local.at[1]),
+    ]
+    for copy in out_copies:
+        copy.start()
+    params = second[0, 2 * share :, :].astype(F32)
+    for slot in range(1, second.shape[0]):
+        params = params + second[slot, 2 * share :, :].astype(F32)
+    turned = []
+    for k in range(experts):
+        wanted = lax.rem(place + k, experts)
+        picked = jnp.zeros((1, D), F32)
+        for e in range(experts):
+            picked = picked + params[8 + e : 9 + e, :] * jnp.where(wanted == e, 1.0, 0.0)
+        turned.append(picked)
+    params_ref[...] = params
+    for k in range(experts):
+        params_ref[8 + k : 9 + k, :] = turned[k]
+    hot = (lax.broadcasted_iota(jnp.int32, (128, seq), 0) == buckets_ref[...]).astype(F32).astype(BF16)
+    lines = nn(params[16:32, :128].astype(BF16), hot)
+    for h in range(heads):
+        line_ref[h] = lines[h : h + 1, :]
+
+    kept[1].wait()
+    for copy in moves_x:
+        copy.wait_recv()
+    out_copies.append(pltpu.make_async_copy(land, x_out, own_local.at[2]))
+    out_copies[-1].start()
+    part = land.shape[1]
+    for p in range(group):
+        here = slice(p * part, (p + 1) * part)
+        x = land[p].astype(F32)
+        inverse = lax.rsqrt(jnp.mean(x * x, axis=-1, keepdims=True) + EPSILON)
+        normed = (x * inverse * params[0:1, :]).astype(BF16)
+        a_ref[here, :] = normed
+        q = nn(normed, weight(first, 0, share)).astype(BF16)
+        q_ref[here, :] = (q.astype(F32) * scale).astype(BF16)
+        k_ref[here, :] = nn(normed, weight(first, 1, share)).astype(BF16)
+        v_ref[here, :] = nn(normed, weight(second, 0, share)).astype(BF16)
+    for copy in slices:
+        copy.wait_recv()
+    for copy in moves + moves_x + slices:
+        copy.wait_send()
+    for copy in out_copies:
+        copy.wait()
 
 
 def masked_scores(k, q, table_ref, head, i, j, seg_col, seg_row):
@@ -440,9 +756,44 @@
     return jnp.where(allowed, scores, MASKED)
 
 
-def attend_kernel(q_ref, k_ref, v_ref, table_ref, col_ref, row_ref, o_ref, lse_ref, *, width):
+def attend_kernel(
+    q_ref, k_ref, v_ref, line_ref, down_ref, across_ref, source, grad_ref, w_in_ref, w_out_ref,
+    o_ref, lse_ref, table_ref, grad_out, piece_out, gather_first, gather_second,
+    g_send, g_recv, p_send, p_recv, keep, send, recv, local, *, width, group
+):
+    step = pl.program_id(0)
+    last = pl.num_programs(0) - 1
+    place = lax.axis_index("expert")
+    start0, start1, start2, finish = gather_copies(
+        gather_first, gather_second, source.at[0], source.at[1], send, recv, local
+    )
+    moves = swap_copies(grad_ref, grad_out, g_send, g_recv, group)
+    slices = slice_copies(w_in_ref, w_out_ref, piece_out, p_send, p_recv, 0, lax.rem(place + 1, group))
+    kept = pltpu.make_async_copy(grad_ref.at[place], grad_out.at[place], keep.at[0])
+
+    @pl.when(step == 0)
+    def _():
+        meet(plane_devices() + place_devices(group))
+        start0()
+        for copy in moves + slices:
+            copy.start()
+        kept.start()
+
+    @pl.when(step == 3)
+    def _():
+        start1()
+
+    heads = q_ref.shape[1] // width
+    for h in range(heads):
+        row = line_ref[h]
+        for gap in range(table_ref.shape[1]):
+            ahead = row[:, gap * TILE : (gap + 1) * TILE]
+            back = row[:, (gap - 1) * TILE : gap * TILE] if gap else jnp.zeros_like(ahead)
+            grid = jnp.broadcast_to(jnp.concatenate([ahead, back], axis=1), (TILE, 2 * TILE))
+            grid = pltpu.roll(grid, 0, 1, stride=1, stride_axis=0)
+            table_ref[h, gap] = grid[:, :TILE].astype(BF16)
+
     blocks = q_ref.shape[0] // TILE
-    heads = q_ref.shape[1] // width
     turned = [v_ref[:, h * width : (h + 1) * width].T for h in range(heads)]
     for i in range(blocks):
         here = slice(i * TILE, (i + 1) * TILE)
@@ -455,7 +806,7 @@
                 there = slice(j * TILE, (j + 1) * TILE)
                 pieces.append(
                     masked_scores(
-                        k_ref[there, lanes], q, table_ref, h, i, j, col_ref[there, :], row_ref[:, here]
+                        k_ref[there, lanes], q, table_ref, h, i, j, down_ref[there, 8:9], across_ref[8:9, here]
                     )
                 )
             top = pieces[0].max(axis=0, keepdims=True)
@@ -471,11 +822,50 @@
             lse_ref[0, h : h + 1, here] = top + jnp.log(total)
         o_ref[here, :] = jnp.concatenate(outs, axis=0).T.astype(BF16)
 
+    @pl.when(step == last)
+    def _():
+        start2()
+        kept.wait()
+        for copy in moves + slices:
+            copy.wait_recv()
+        for copy in moves + slices:
+            copy.wait_send()
+        finish()
+
 
 def attend_back_kernel(
-    q_ref, k_ref, v_ref, do_ref, table_ref, col_ref, row_ref, lse_ref,
-    dq_ref, dk_ref, dv_ref, dist_ref, sum_ref, dk_sum, dv_sum, *, width, scale
+    q_ref, k_ref, v_ref, do_ref, table_ref, down_ref, across_ref, lse_ref, result_ref, terms,
+    dq_ref, dk_ref, dv_ref, dist_ref, sums_ref, result_out, sum_ref, dk_sum, dv_sum,
+    o_send, o_recv, keep, own, pair, inbox, send, recv, local, *, width, scale, group
 ):
+    step = pl.program_id(0)
+    last = pl.num_programs(0) - 1
+    place = lax.axis_index("expert")
+
+    def emit(half, value):
+        sums_ref[half] = value.astype(BF16)
+
+    start, far, near, late, finish = reduce_copies(terms, own, pair, inbox, send, recv, local, emit)
+    moves = swap_copies(result_ref, result_out, o_send, o_recv, group)
+    kept = pltpu.make_async_copy(result_ref.at[place], result_out.at[place], keep.at[0])
+
+    @pl.when(step == 0)
+    def _():
+        meet(plane_devices() + place_devices(group))
+        start()
+        for copy in moves:
+            copy.start()
+        kept.start()
+
+    @pl.when(step == 1)
+    def _():
+        far()
+        near()
+
+    @pl.when(step == 5)
+    def _():
+        late()
+
     blocks = q_ref.shape[0] // TILE
     heads = q_ref.shape[1] // width
     turned = [k_ref[:, h * width : (h + 1) * width].T for h in range(heads)]
@@ -492,7 +882,7 @@
             for j in range(i + 1):
                 there = slice(j * TILE, (j + 1) * TILE)
                 scores = masked_scores(
-                    k_ref[there, lanes], q, table_ref, h, i, j, col_ref[there, :], row_ref[:, here]
+                    k_ref[there, lanes], q, table_ref, h, i, j, down_ref[there, 8:9], across_ref[8:9, here]
                 )
                 p = jnp.exp(scores - lse)
                 dp = nt(v_ref[there, lanes], do)
@@ -531,69 +921,160 @@
     dk_ref[...] = dk_sum[...].astype(BF16)
     dv_ref[...] = dv_sum[...].astype(BF16)
 
+    @pl.when(step == last)
+    def _():
+        kept.wait()
+        for copy in moves:
+            copy.wait_recv()
+        for copy in moves:
+            copy.wait_send()
+        finish()
+
 
 def route_kernel(
-    x_ref, o_ref, wall_ref, gain_ref, router_ref, routes_ref, h_ref, a_ref, gate_ref, pr_ref,
-    *, share, experts
+    x_ref, o_ref, second_ref, params_ref, down_ref, h_ref, a_ref, gate_ref, pr_ref, *, share, experts
 ):
-    h1 = x_ref[...].astype(F32) + nn(o_ref[...], weight(wall_ref, 3, share))
+    h1 = x_ref[...].astype(F32) + nn(o_ref[...], weight(second_ref, 1, share))
     h_ref[...] = h1
     inverse = lax.rsqrt(jnp.mean(h1 * h1, axis=-1, keepdims=True) + EPSILON)
-    normed = (h1 * inverse * gain_ref[...]).astype(BF16)
+    normed = (h1 * inverse * params_ref[1:2, :]).astype(BF16)
     a_ref[...] = normed
-    logits = nn(normed, router_ref[...])
+    router = jnp.concatenate([params_ref[8:16, :], jnp.zeros((120, D), F32)], axis=0).astype(BF16)
+    logits = nt(normed, router)
     lane = lax.broadcasted_iota(jnp.int32, logits.shape, 1)
     logits = jnp.where(lane < experts, logits, MASKED)
     lifted = jnp.exp(logits - logits.max(axis=-1, keepdims=True))
     pr = lifted / lifted.sum(axis=-1, keepdims=True)
-    named = (routes_ref[:, 0:1] == lane) | (routes_ref[:, 1:2] == lane)
+    named = (down_ref[...] >= 0) & (lane < experts)
     picked = jnp.where(named, pr, 0.0)
     pr_ref[...] = pr
     gate_ref[...] = picked / picked.sum(axis=-1, keepdims=True)
 
 
-def expert_kernel(
-    a_ref, g_ref, gate_ref, pos_ref, w_ref, eo_ref, da_ref, dw_ref, rows_a, rows_d, eo_sum, da_sum,
-    *, index, capacity
-):
+def expert_kernel(a_ref, g_ref, gate_ref, across_ref, wi_ref, wo_ref, *refs, index, capacity, fetch, relay, reduce, pass_on, group):
+    refs = list(refs)
+    take = lambda count: [refs.pop(0) for _ in range(count)]
+    source = take(1) if fetch else None
+    relayed = take(2) if relay else None
+    terms = take(1) if reduce else None
+    passed = take(1) if pass_on else None
+    eo_ref, da_ref, dw_ref = take(3)
+    buffers = take(2) if fetch else None
+    relay_out = take(1) if relay else None
+    sums_ref = take(1)[0] if reduce else None
+    pass_out = take(1) if pass_on else None
+    rows_a, turned_a, rows_d, eo_sum, da_sum = take(5)
     step = pl.program_id(0)
+    last = pl.num_programs(0) - 1
+    place = lax.axis_index("expert")
+    at_start, at_end = [], []
+    at_step = {}
+    if fetch:
+        start0, start1, start2, finish = gather_copies(
+            *buffers, source[0].at[0], source[0].at[1], *take(3)
+        )
+        at_start.append(start0)
+        at_step[3] = [start1]
+        at_end += [start2, finish]
+    if relay:
+        send, recv = take(2)
+        down = along_axis(relayed[0], relay_out[0], send.at[0], recv.at[0], jnp.maximum(place - 1, 0))
+        up = along_axis(relayed[1], relay_out[0], send.at[1], recv.at[0], jnp.minimum(place + 1, group - 1))
+        middle = (place == 1) | (place == 2)
+
+        def start_relay():
+            @pl.when(middle)
+            def _():
+                down.start()
+                up.start()
+
+        def end_relay():
+            down.wait_recv()
+
+            @pl.when(middle)
+            def _():
+                down.wait_send()
+                up.wait_send()
+
+        at_start.append(start_relay)
+        at_end.append(end_relay)
+    if reduce:
+        scratch = take(6)
+
+        def emit(half, value):
+            sums_ref[half] = value.astype(BF16)
+
+        start, far, near, late, end_reduce = reduce_copies(terms[0], *scratch, emit)
+        at_start.append(start)
+        at_step[1] = [far]
+        at_step[2] = [near]
+        at_step[6 if fetch else 5] = [late]
+        at_end.append(end_reduce)
+    if pass_on:
+        send, recv = take(2)
+        hop = along_axis(passed[0], pass_out[0], send.at[0], recv.at[0], lax.rem(place + pass_on, group))
+        at_start.append(hop.start)
+        at_end.append(hop.wait)
+
+    if at_start:
+        @pl.when(step == 0)
+        def _():
+            far_devices = place_devices(group) if relay or pass_on else []
+            near_devices = plane_devices() if fetch or reduce else []
+            meet(near_devices + far_devices)
+            for action in at_start:
+                action()
+
+    for when, actions in at_step.items():
+        @pl.when(step == when)
+        def _(actions=actions):
+            for action in actions:
+                action()
 
     @pl.when(step == 0)
     def _():
         tokens = a_ref.shape[0]
         slot = lax.broadcasted_iota(jnp.int32, (capacity, tokens), 0)
-        pick = (pos_ref[index : index + 1, :] == slot).astype(BF16)
-        rows_a[...] = nn(pick, a_ref[...]).astype(BF16)
+        pick = (across_ref[index : index + 1, :] == slot).astype(BF16)
+        rows = nn(pick, a_ref[...]).astype(BF16)
+        rows_a[...] = rows
+        turned_a[...] = rows.T
         scaled = (gate_ref[:, index : index + 1] * g_ref[...].astype(F32)).astype(BF16)
         rows_d[...] = nn(pick, scaled).astype(BF16)
         eo_sum[...] = jnp.zeros_like(eo_sum)
         da_sum[...] = jnp.zeros_like(da_sum)
 
-    a = rows_a[...]
     d = rows_d[...]
-    w_in = w_ref[0, 0]
-    w_out = w_ref[0, 1]
-    u = nt(a, w_in)
-    cube = u * u
-    t = jnp.tanh(GELU_A * u * (1.0 + GELU_B * cube))
+    w_in = wi_ref[0]
+    w_out = wo_ref[0]
+    chunk = w_in.shape[1]
+    if index:
+        w_out = jnp.concatenate([w_out[:chunk], w_out[chunk:]], axis=1)
+    u = nn(rows_a[...], w_in)
+    square = u * u
+    t = jnp.tanh(GELU_A * u * (1.0 + GELU_B * square))
     half = 0.5 * (1.0 + t)
     z = (u * half).astype(BF16)
     eo_sum[...] += nn(z, w_out)
-    dw_ref[0, 1] = tn(z, d).astype(BF16)
-    slope = half + (0.5 * GELU_A) * u * (1.0 - t * t) * (1.0 + 3.0 * GELU_B * cube)
+    dw_out = tn(z, d).astype(BF16)
+    dw_ref[0, 1, :chunk] = dw_out[:, :chunk]
+    dw_ref[0, 1, chunk:] = dw_out[:, chunk:]
+    slope = half + (0.5 * GELU_A) * u * (1.0 - t * t) * (1.0 + 3.0 * GELU_B * square)
     du = (nt(d, w_out) * slope).astype(BF16)
-    da_sum[...] += nn(du, w_in)
-    dw_ref[0, 0] = tn(du, a).astype(BF16)
-
-    @pl.when(step == pl.num_programs(0) - 1)
+    da_sum[...] += nt(du, w_in)
+    dw_ref[0, 0] = nn(turned_a[...], du).astype(BF16)
+
+    @pl.when(step == last)
     def _():
         eo_ref[...] = eo_sum[...].astype(BF16)
         da_ref[...] = da_sum[...].astype(BF16)
+        for action in at_end:
+            action()
 
 
 def combine_kernel(
-    h_ref, a_ref, g_ref, o_ref, gate_ref, pr_ref, routes_ref, pos_ref, eo0, eo1, eo2, eo3,
-    da0, da1, da2, da3, wall_ref, gain_ref, router_ref,
+    h_ref, a_ref, g_ref, o_ref, gate_ref, pr_ref, pos_ref, eo0, eo1, eo2, eo3,
+    da0, da1, da2, da3, second_ref, params_ref,
     out_ref, dh_ref, do_ref, dw_ref, dgain_ref, drouter_ref, *, share, experts, capacity
 ):
     step = pl.program_id(0)
@@ -615,13 +1096,13 @@
     dgate = jnp.zeros_like(pr)
     da = jnp.zeros_like(h1)
     for k, (eo, back) in enumerate(((eo0, da0), (eo1, da1), (eo2, da2), (eo3, da3))):
-        place = (pos_ref[:, k : k + 1] == slot).astype(BF16)
-        got = nn(place, eo[...])
+        spot = (pos_ref[:, k : k + 1] == slot).astype(BF16)
+        got = nn(spot, eo[...])
         result = result + gates[:, k : k + 1] * got
         dgate = jnp.where(lane == k, jnp.sum(g * got, axis=-1, keepdims=True), dgate)
-        da = da + nn(place, back[...])
+        da = da + nn(spot, back[...])
     out_ref[...] = result.astype(BF16)
-    named = (routes_ref[:, 0:1] == lane) | (routes_ref[:, 1:2] == lane)
+    named = (pos_ref[...] >= 0) & (lane < experts)
     denom = jnp.sum(jnp.where(named, pr, 0.0), axis=-1, keepdims=True)
     weighted = jnp.sum(dgate * gates, axis=-1, keepdims=True)
     dpr = jnp.where(named, (dgate - weighted) / denom, 0.0)
@@ -629,57 +1110,161 @@
     high = dlog.astype(BF16)
     lost = (dlog - high.astype(F32)).astype(BF16)
     a = a_ref[...]
-    drouter_ref[...] += tn(a, high) + tn(a, lost)
+    drouter_ref[...] += (tn(high, a) + tn(lost, a))[: drouter_ref.shape[0]]
     for k in range(experts):
-        da = da + dlog[:, k : k + 1] * router_ref[k : k + 1, :]
+        da = da + dlog[:, k : k + 1] * params_ref[8 + k : 9 + k, :]
     inverse = lax.rsqrt(jnp.mean(h1 * h1, axis=-1, keepdims=True) + EPSILON)
     n2 = h1 * inverse
     dgain_ref[...] += jnp.sum(da * n2, axis=0, keepdims=True)
-    dn = da * gain_ref[...]
+    dn = da * params_ref[1:2, :]
     dh = g + inverse * (dn - n2 * jnp.mean(dn * n2, axis=-1, keepdims=True))
     dh_ref[...] = dh
     dy = dh.astype(BF16)
-    do_ref[...] = nt(dy, weight(wall_ref, 3, share)).astype(BF16)
+    do_ref[...] = nt(dy, weight(second_ref, 1, share)).astype(BF16)
     dw_ref[...] += tn(o_ref[...], dy)
 
 
-def finish_kernel(
-    x_ref, a_ref, dq_ref, dk_ref, dv_ref, dh_ref, wall_ref, gain_ref, dwo_ref,
-    din_ref, pack_ref, dgain_ref, sum_ref, *, share
+def close_kernel(
+    x_ref, a_ref, dq_ref, dk_ref, dv_ref, dh_ref, first_ref, second_ref, params_ref, dwo_ref, dgain_m_ref, drouter_ref,
+    dist_ref, buckets_ref, sum0, sum1, sum2, sum3,
+    din_out, gather_first, gather_second, dense_ref,
+    sum_ref, dgain, stage, total, pack, own, pair, inbox, r_send, r_recv, r_local, sends, recvs, keep,
+    z_in, z_total, z_final, z_send, z_recv, g_send, g_recv, g_local, *, share, group, experts
 ):
     step = pl.program_id(0)
+    last = pl.num_programs(0) - 1
+    me = lax.axis_index("dp")
+    place = lax.axis_index("expert")
+    start0, start1, start2, finish = gather_copies(
+        gather_first, gather_second, total.at[0], total.at[1], g_send, g_recv, g_local
+    )
+    tile = a_ref.shape[0]
+
+    def din_copy(p):
+        return along_axis(stage.at[p], din_out.at[place], sends.at[p], recvs.at[place], p)
+
+    def din_keep(p):
+        return pltpu.make_async_copy(stage.at[p], din_out.at[p], keep.at[0])
 
     @pl.when(step == 0)
     def _():
+        for half in range(2):
+            value = sum0[half].astype(F32) + sum1[half].astype(F32)
+            total[half] = (value + sum2[half].astype(F32) + sum3[half].astype(F32)).astype(BF16)
+        meet(plane_devices() + place_devices(group))
+        start0()
         sum_ref[...] = jnp.zeros_like(sum_ref)
-        dgain_ref[...] = jnp.zeros_like(dgain_ref)
+        dgain[...] = jnp.zeros_like(dgain)
 
     a = a_ref[...]
     da = jnp.zeros(dh_ref.shape, F32)
+    places = ((first_ref, 0), (first_ref, 1), (second_ref, 0))
     for index, grad_ref in enumerate((dq_ref, dk_ref, dv_ref)):
         grad = grad_ref[...]
         sum_ref[index] += tn(a, grad)
-        da = da + nt(grad, weight(wall_ref, index, share))
+        slots_ref, at = places[index]
+        da = da + nt(grad, weight(slots_ref, at, share))
     x = x_ref[...].astype(F32)
     inverse = lax.rsqrt(jnp.mean(x * x, axis=-1, keepdims=True) + EPSILON)
     n1 = x * inverse
-    dgain_ref[...] += jnp.sum(da * n1, axis=0, keepdims=True)
-    dn = da * gain_ref[...]
+    dgain[...] += jnp.sum(da * n1, axis=0, keepdims=True)
+    dn = da * params_ref[0:1, :]
     din = dh_ref[...] + inverse * (dn - n1 * jnp.mean(dn * n1, axis=-1, keepdims=True))
-    din_ref[...] = din.astype(BF16)
-
-    @pl.when(step == pl.num_programs(0) - 1)
+    for p in range(group):
+        @pl.when(step == p)
+        def _(p=p):
+            stage[p] = din.astype(BF16)
+
+            @pl.when(place == p)
+            def _():
+                din_keep(p).start()
+
+            @pl.when(place != p)
+            def _():
+                din_copy(p).start()
+
+    @pl.when(step == last)
     def _():
-        for index in range(3):
-            pack_ref[:, index * share : (index + 1) * share, :] = (
-                sum_ref[index].astype(BF16).reshape(-1, share, D)
-            )
-        pack_ref[:, 3 * share :, :] = dwo_ref[...].astype(BF16).reshape(-1, share, D)
-
-
-def unpack_kernel(w_ref, in_ref, out_ref):
-    in_ref[0] = w_ref[0, 0].astype(F32).T
-    out_ref[0] = w_ref[0, 1].astype(F32)
+        start1()
+        for index in range(2):
+            pack[:, 0, index * share : (index + 1) * share, :] = sum_ref[index].astype(BF16).reshape(-1, share, D)
+        pack[:, 1, :share, :] = sum_ref[2].astype(BF16).reshape(-1, share, D)
+        pack[:, 1, share : 2 * share, :] = dwo_ref[...].astype(BF16).reshape(-1, share, D)
+        seq = dist_ref.shape[1]
+        hot = (lax.broadcasted_iota(jnp.int32, (128, seq), 0) == buckets_ref[...]).astype(F32).astype(BF16)
+        left = dist_ref[...]
+        table = jnp.zeros((left.shape[0], 128), F32)
+        for _ in range(3):
+            part = left.astype(BF16)
+            left = left - part.astype(F32)
+            table = table + nt(part, hot)
+        rows_out = [dgain[...], dgain_m_ref[...], jnp.zeros((6, D), F32)]
+        for e in range(experts):
+            picked = jnp.zeros((1, D), F32)
+            for k in range(experts):
+                picked = picked + drouter_ref[k : k + 1, :] * jnp.where(lax.rem(place + k, experts) == e, 1.0, 0.0)
+            rows_out.append(picked)
+        rows_out.append(jnp.zeros((8 - experts, D), F32))
+        rows_out.append(jnp.concatenate([table, jnp.zeros((table.shape[0], D - 128), F32)], axis=1))
+        rows_out.append(jnp.zeros((16 - table.shape[0], D), F32))
+        small = jnp.concatenate(rows_out, axis=0).astype(BF16)
+        for slot in range(pack.shape[0]):
+            pack[slot, 0, 2 * share :, :] = small
+            pack[slot, 1, 2 * share :, :] = jnp.zeros_like(small)
+        quarter = pack.shape[2] // 2
+
+        def emit(half, value):
+            low = value.astype(BF16)
+            z_total[2 * half] = low[:quarter]
+            z_total[2 * half + 1] = low[quarter:]
+
+        start, far, near, late, end_reduce = reduce_copies(pack, own, pair, inbox, r_send, r_recv, r_local, emit)
+        start()
+        far()
+        near()
+        start2()
+        late()
+        end_reduce()
+        spread = [
+            along_axis(z_total.at[lax.rem(place + k, group)], z_in.at[k - 1], z_send.at[k], z_recv.at[k],
+                       lax.rem(place + k, group))
+            for k in range(1, group)
+        ]
+        for copy in spread:
+            copy.start()
+        for copy in spread:
+            copy.wait_recv()
+        value = z_total[place].astype(F32)
+        for k in range(group - 1):
+            value = value + z_in[k].astype(F32)
+        z_final[place] = value.astype(BF16)
+        share_out = [
+            along_axis(z_final.at[place], z_final.at[place], z_send.at[group + k], z_recv.at[group + k],
+                       lax.rem(place + k, group))
+            for k in range(1, group)
+        ]
+        for copy in share_out:
+            copy.start()
+        for copy in share_out:
+            copy.wait_recv()
+        for copy in spread + share_out:
+            copy.wait_send()
+        dense_ref[...] = z_final[...]
+        for k in range(1, group):
+            other = lax.rem(place + k, group)
+            along_axis(stage.at[other], din_out.at[other], sends.at[other], recvs.at[other], other).wait_recv()
+        for k in range(1, group):
+            other = lax.rem(place + k, group)
+            along_axis(stage.at[other], din_out.at[place], sends.at[other], recvs.at[place], other).wait_send()
+        pltpu.make_async_copy(stage.at[place], din_out.at[place], keep.at[0]).wait()
+        finish()
+
+
+def unpack_kernel(first_ref, second_ref, in_ref, out_ref):
+    chunk = first_ref.shape[2]
+    in_ref[0] = first_ref[0].astype(F32)
+    out_ref[0, :, :chunk] = second_ref[0, :chunk].astype(F32)
+    out_ref[0, :, chunk:] = second_ref[0, chunk:].astype(F32)
 
 
 def on_device_whole(
@@ -687,7 +1272,6 @@
     gain_moe, router, rel_bias, w_expert_in, w_expert_out,
 ):
     group = lax.axis_size("expert")
-    rank = lax.axis_index("expert")
     shards = lax.axis_size("dp")
     shard = lax.axis_index("dp")
     experts = router.shape[1]
@@ -699,169 +1283,164 @@
     ff = w_expert_in.shape[2]
     chunk = ff // shards
     blocks = seq // TILE
+    part = seq // group
     capacity = 3 * seq // group
     pairs = 128 // width
-
-    def across(values):
-        return lax.all_to_all(values, "expert", split_axis=0, concat_axis=1, tiled=True)[0]
-
-    x = across(layer_in)
-    routes_here = jnp.remainder(across(routes) - rank, experts)
-    g = across(out_grad)
-    row = lambda v: jnp.pad(v.reshape(1, -1), ((0, 0), (0, D - v.size)))
-    pack = jnp.concatenate(
-        [w_query, w_key, w_value, w_output, row(gain_attn), row(gain_moe), row(router), row(rel_bias),
-         jnp.zeros((4, D), BF16)], axis=0)
-    wall = lax.all_gather(pack, "dp", axis=0)
-    base = 4 * share
-    gain_a = wall[:, base, :share].reshape(1, D).astype(F32)
-    gain_m = wall[:, base + 1, :share].reshape(1, D).astype(F32)
-    router_all = wall[:, base + 2, : router.size].reshape(D, experts)
-    bias_all = wall[:, base + 3, : rel_bias.size].reshape(NB, heads)
-    turn = (jnp.arange(experts, dtype=jnp.int32)[:, None] == jnp.remainder(
-        jnp.arange(experts, dtype=jnp.int32)[None, :] + rank, experts)).astype(BF16)
-    router_rel = jnp.dot(router_all, turn, preferred_element_type=F32)
-    router_pad = jnp.pad(router_rel, ((0, 0), (0, 128 - experts))).astype(BF16)
-    router_turned = jnp.pad(router_rel.T, ((0, 8 - experts), (0, 0)))
-    own = jnp.stack([
-        lax.dynamic_slice_in_dim(w_expert_in[0], shard * chunk, chunk, axis=1).T,
-        lax.dynamic_slice_in_dim(w_expert_out[0], shard * chunk, chunk, axis=0),
-    ])
-    local = jnp.stack(
-        [w_expert_in[0].T.reshape(shards, chunk, D), w_expert_out[0].reshape(shards, chunk, D)], axis=1
-    )
-    weights = [local]
-    for k in range(1, experts):
-        moved = lax.ppermute(own, "expert", [((s + k) % group, s) for s in range(group)])
-        weights.append(lax.all_gather(moved, "dp", axis=0))
-    hot_buckets = (buckets[None, :] == jnp.arange(NB, dtype=jnp.int32)[:, None]).astype(BF16)
-    bias_line = lax.dot_general(
-        bias_all, hot_buckets, (((0,), (0,)), ((), ())), preferred_element_type=F32
-    ).reshape(heads, 1, seq)
-    table = call(
-        bias_kernel, "bias", (heads,),
-        [pl.BlockSpec((1, 1, seq), lambda i: (i, 0, 0))],
-        pl.BlockSpec((1, blocks, TILE, TILE), lambda i: (i, 0, 0, 0)),
-        sds((heads, blocks, TILE, TILE), BF16),
-    )(bias_line)
-    seg = lax.dynamic_slice_in_dim(segments, rank, 1, axis=0)
-    seg_row = seg.reshape(1, seq)
-    seg_col = seg.reshape(seq, 1)
-    expert_ids = jnp.arange(experts, dtype=jnp.int32)
-    named = (routes_here[:, 0:1] == expert_ids) | (routes_here[:, 1:2] == expert_ids)
-    at = jnp.arange(seq, dtype=jnp.int32)
-    before = jnp.dot(
-        (at[None, :] < at[:, None]).astype(BF16), named.astype(BF16), preferred_element_type=F32
-    ).astype(jnp.int32)
-    pos = jnp.where(named, before, -1)
-    pos_turned = jnp.pad(pos.T, ((0, 8 - experts), (0, 0)), constant_values=-1)
-
     tokens = (seq, D)
-    normed, q, k, v = call(
-        functools.partial(project_kernel, share=share, scale=scale), "project", (blocks,),
-        [rows(D), whole((1, D)), whole(wall.shape)],
-        [rows(D)] * 4, [sds(tokens, BF16)] * 4, flops=6 * seq * D * D, nbytes=12 * 2**20,
-    )(x, gain_a, wall)
+    slots = (capacity, D)
+    piece = (2, D, chunk)
+    buffer = sds((shards, D, chunk), BF16)
+    dma = pltpu.SemaphoreType.DMA
+    vmem = pl.BlockSpec(memory_space=pltpu.VMEM)
+
+    wide = lambda v, count: jnp.pad(v, ((0, count - v.shape[0]), (0, D - v.shape[1])))
+    small = jnp.concatenate([
+        wide(jnp.stack([gain_attn, gain_moe]), 8), wide(router.T, 8), wide(rel_bias.T, 16)])
+    routes_in = jnp.pad(routes.transpose(0, 2, 1), ((0, 0), (0, 6), (0, 0)))
+    bucket_row = buckets.reshape(1, seq)
+    second_rows = 2 * share + 32
+    x, moved, first, second, normed, q, k, v, params, lines, across, down = call(
+        functools.partial(open_kernel, group=group, share=share, heads=heads, experts=experts, scale=scale),
+        "open", (1,),
+        [ANY] * 8 + [vmem] * 3,
+        [ANY] * 4 + [vmem] * 8,
+        [sds((group, part, D), BF16), sds(piece, BF16), sds((shards, 2 * share, D), BF16),
+         sds((shards, second_rows, D), BF16)] + [sds(tokens, BF16)] * 4
+        + [sds((32, D), F32), sds((heads, 1, seq), F32), sds((16, seq), jnp.int32), sds((seq, 128), jnp.int32)],
+        [pltpu.VMEM((group, part, D), BF16), pltpu.VMEM((group, 8, part), jnp.int32),
+         pltpu.VMEM((shards, 2 * share, D), BF16), pltpu.VMEM((shards, second_rows, D), BF16),
+         pltpu.VMEM((2 * share, D), BF16), pltpu.VMEM((second_rows, D), BF16)]
+        + [dma((group,))] * 4 + [dma((3,))] * 2 + [dma((2,)), dma((4,))] + gather_sems(), collective=1,
+    )(layer_in, routes_in, w_expert_in, w_expert_out, w_query, w_key, w_value, w_output, small, bucket_row, segments)
+    x = x.reshape(tokens)
+
     cols = pl.BlockSpec((seq, 128), lambda i: (0, i))
     table_spec = pl.BlockSpec((pairs, blocks, TILE, TILE), lambda i: (i, 0, 0, 0))
-    line_spec = pl.BlockSpec((1, pairs, seq), lambda i: (i, 0, 0))
-    o, lse = call(
-        functools.partial(attend_kernel, width=width), "attend", (heads // pairs,),
-        [cols, cols, cols, table_spec, whole((seq, 1)), whole((1, seq))],
-        [cols, line_spec],
-        [sds(tokens, BF16), sds((heads // pairs, pairs, seq), F32)],
-        flops=8 * seq * seq * D, nbytes=16 * 2**20,
-    )(q, k, v, table, seg_col, seg_row)
+    lse_spec = pl.BlockSpec((1, pairs, seq), lambda i: (i, 0, 0))
+    o, lse, table, g, moved3, *buffers = call(
+        functools.partial(attend_kernel, width=width, group=group), "attend", (heads // pairs,),
+        [cols, cols, cols, pl.BlockSpec((pairs, 1, seq), lambda i: (i, 0, 0)), whole((seq, 128)), whole((16, seq))]
+        + [ANY] * 4,
+        [cols, lse_spec, table_spec] + [ANY] * 4,
+        [sds(tokens, BF16), sds((heads // pairs, pairs, seq), F32), sds((heads, blocks, TILE, TILE), BF16),
+         sds((group, part, D), BF16), sds(piece, BF16), buffer, buffer],
+        [dma((group,))] * 2 + [dma((3,))] * 2 + [dma((1,))] + gather_sems(),
+        flops=8 * seq * seq * D, nbytes=16 * 2**20, collective=2,
+    )(q, k, v, lines, down, across, moved, out_grad, w_expert_in, w_expert_out)
+    g = g.reshape(tokens)
     h1, normed_m, gates, pr = call(
         functools.partial(route_kernel, share=share, experts=experts), "route", (blocks,),
-        [rows(D), rows(D), whole(wall.shape), whole((1, D)), whole((D, 128)), rows(2)],
+        [rows(D), rows(D), whole(second.shape), whole((32, D)), rows(128)],
         [rows(D), rows(D), rows(128), rows(128)],
         [sds(tokens, F32), sds(tokens, BF16), sds((seq, 128), F32), sds((seq, 128), F32)],
         flops=2 * seq * D * D, nbytes=12 * 2**20,
-    )(x, o, wall, gain_m, router_pad, routes_here)
-    produced, returned, partial_sums = [], [], []
-    slots = (capacity, D)
-    for index in range(experts):
-        eo, da, dw = call(
-            functools.partial(expert_kernel, index=index, capacity=capacity), f"expert{index}", (shards,),
-            [whole(tokens), whole(tokens), whole((seq, 128)), whole((8, seq)),
-             pl.BlockSpec((1, 2, chunk, D), lambda i: (i, 0, 0, 0))],
-            [whole(slots), whole(slots), pl.BlockSpec((1, 2, chunk, D), lambda i: (i, 0, 0, 0))],
-            [sds(slots, BF16), sds(slots, BF16), sds((shards, 2, chunk, D), BF16)],
-            [pltpu.VMEM(slots, BF16), pltpu.VMEM(slots, BF16), pltpu.VMEM(slots, F32), pltpu.VMEM(slots, F32)],
-            flops=12 * capacity * D * ff, nbytes=24 * 2**20,
-        )(normed_m, g, gates, pos_turned, weights[index])
-        produced.append(eo)
-        returned.append(da)
-        partial_sums.append(lax.psum_scatter(dw, "dp", scatter_dimension=0, tiled=True)[0])
+    )(x, o, second, params, down)
+
+    def run_expert(index, buffers, collective, fetch=None, relay=None, reduce=None, pass_on=None, hop=0):
+        in_block, out_block = (1, D, chunk), (1, D, chunk)
+        in_map = out_map = lambda i: (i, 0, 0)
+        if index == 0:
+            buffers = (w_expert_in, w_expert_out)
+            out_block = (1, chunk, D)
+            in_map, out_map = (lambda i: (0, 0, i)), (lambda i: (0, i, 0))
+        extra_in, extra_out, shapes, scratch = [], [], [], []
+        if fetch is not None:
+            extra_in.append(fetch)
+            extra_out += [ANY] * 2
+            shapes += [buffer] * 2
+            scratch += gather_sems()
+        if relay is not None:
+            extra_in += relay
+            extra_out.append(ANY)
+            shapes.append(sds(piece, BF16))
+            scratch += [dma((2,)), dma((1,))]
+        if reduce is not None:
+            extra_in.append(reduce)
+            extra_out.append(whole(piece))
+            shapes.append(sds(piece, BF16))
+            scratch += reduce_scratch(piece)
+        if pass_on is not None:
+            extra_in.append(pass_on)
+            extra_out.append(ANY)
+            shapes.append(sds(piece, BF16))
+            scratch += [dma((1,)), dma((1,))]
+        return call(
+            functools.partial(
+                expert_kernel, index=index, capacity=capacity, fetch=fetch is not None, relay=relay is not None,
+                reduce=reduce is not None, pass_on=hop, group=group),
+            f"expert{index}", (shards,),
+            [whole(tokens), whole(tokens), whole((seq, 128)), whole((16, seq)),
+             pl.BlockSpec(in_block, in_map), pl.BlockSpec(out_block, out_map)] + [ANY] * len(extra_in),
+            [whole(slots), whole(slots), pl.BlockSpec((1, 2, D, chunk), lambda i: (i, 0, 0, 0))] + extra_out,
+            [sds(slots, BF16), sds(slots, BF16), sds((shards, *piece), BF16)] + shapes,
+            [pltpu.VMEM(slots, BF16), pltpu.VMEM((D, capacity), BF16), pltpu.VMEM(slots, BF16),
+             pltpu.VMEM(slots, F32), pltpu.VMEM(slots, F32)] + scratch,
+            flops=12 * capacity * D * ff, nbytes=24 * 2**20, collective=collective if extra_in else None,
+        )(normed_m, g, gates, across, *buffers, *extra_in)
+
+    eo1, da1, dw1, *rest = run_expert(1, buffers, 3, fetch=moved3, relay=[moved, moved3])
+    buffers, moved2 = rest[:2], rest[2]
+    eo3, da3, dw3, *rest = run_expert(3, buffers, 4, fetch=moved2, reduce=dw1)
+    buffers, sum1 = rest[:2], rest[2]
+    eo2, da2, dw2, sum3, sum1 = run_expert(2, buffers, 5, reduce=dw3, pass_on=sum1, hop=1)
+    eo0, da0, dw0, sum2, sum3 = run_expert(0, None, 6, reduce=dw2, pass_on=sum3, hop=3)
+    sum2 = lax.ppermute(sum2, "expert", [(s, (s + 2) % group) for s in range(group)])
     result, dh, do, grad_output, grad_gain_m, grad_router = call(
         functools.partial(combine_kernel, share=share, experts=experts, capacity=capacity), "combine",
         (blocks,),
-        [rows(D)] * 4 + [rows(128), rows(128), rows(2), rows(experts)] + [whole(slots)] * 8
-        + [whole(wall.shape), whole((1, D)), whole((8, D))],
-        [rows(D), rows(D), rows(D), whole((D, D)), whole((1, D)), whole((D, 128))],
+        [rows(D)] * 4 + [rows(128)] * 3 + [whole(slots)] * 8 + [whole(second.shape), whole((32, D))],
+        [rows(D), rows(D), rows(D), whole((D, D)), whole((1, D)), whole((8, D))],
         [sds(tokens, BF16), sds(tokens, F32), sds(tokens, BF16), sds((D, D), F32), sds((1, D), F32),
-         sds((D, 128), F32)],
+         sds((8, D), F32)],
         flops=24 * seq * D * D, nbytes=32 * 2**20,
-    )(h1, normed_m, g, o, gates, pr, routes_here, pos, *produced, *returned, wall, gain_m, router_turned)
-    dq, dk, dv, dist = call(
-        functools.partial(attend_back_kernel, width=width, scale=scale), "attend_back", (heads // pairs,),
-        [cols, cols, cols, cols, table_spec, whole((seq, 1)), whole((1, seq)), line_spec],
-        [cols, cols, cols, line_spec],
-        [sds(tokens, BF16)] * 3 + [sds((heads // pairs, pairs, seq), F32)],
-        [pltpu.VMEM((blocks, TILE, TILE), F32), pltpu.VMEM((seq, 128), F32), pltpu.VMEM((seq, 128), F32)],
-        flops=20 * seq * seq * D, nbytes=24 * 2**20,
-    )(q, k, v, do, table, seg_col, seg_row, lse)
-    din, dense, grad_gain_a = call(
-        functools.partial(finish_kernel, share=share), "finish", (blocks,),
-        [rows(D)] * 6 + [whole(wall.shape), whole((1, D)), whole((D, D))],
-        [rows(D), whole((shards, 4 * share, D)), whole((1, D))],
-        [sds(tokens, BF16), sds((shards, 4 * share, D), BF16), sds((1, D), F32)],
-        [pltpu.VMEM((3, D, D), F32)],
-        flops=12 * seq * D * D, nbytes=24 * 2**20,
-    )(x, normed, dq, dk, dv, dh, wall, gain_a, grad_output)
-
-    def back(values):
-        return lax.all_to_all(
-            values.reshape(group, seq // group, D), "expert", split_axis=0, concat_axis=0, tiled=True
-        )
-
-    layer_out = back(result)
-    grad_in = back(din).astype(F32)
-    total = partial_sums[0].astype(F32)
-    for k in range(1, experts):
-        moved = lax.ppermute(partial_sums[k], "expert", [(s, (s + k) % group) for s in range(group)])
-        total = total + moved.astype(F32)
-    gathered = lax.all_gather(total.astype(BF16), "dp", axis=0)
+    )(h1, normed_m, g, o, gates, pr, down, eo0, eo1, eo2, eo3, da0, da1, da2, da3, second, params)
+    dq, dk, dv, dist, sum0, layer_out = call(
+        functools.partial(attend_back_kernel, width=width, scale=scale, group=group), "attend_back",
+        (heads // pairs,),
+        [cols, cols, cols, cols, table_spec, whole((seq, 128)), whole((16, seq)), lse_spec, ANY, ANY],
+        [cols, cols, cols, lse_spec, whole(piece), ANY],
+        [sds(tokens, BF16)] * 3 + [sds((heads // pairs, pairs, seq), F32), sds(piece, BF16),
+                                   sds((group, part, D), BF16)],
+        [pltpu.VMEM((blocks, TILE, TILE), F32), pltpu.VMEM((seq, 128), F32), pltpu.VMEM((seq, 128), F32)]
+        + [dma((group,))] * 2 + [dma((1,))] + reduce_scratch(piece),
+        flops=20 * seq * seq * D, nbytes=24 * 2**20, collective=7,
+    )(q, k, v, do, table, down, across, lse, result.reshape(group, part, D), dw0)
+    dense_slot = (2, 2 * share + 32, D)
+    quarter = (dense_slot[1] // 2, D)
+    grad_in, *gathered, dense = call(
+        functools.partial(close_kernel, share=share, group=group, experts=experts), "close", (blocks,),
+        [rows(D)] * 6 + [whole(first.shape), whole(second.shape), whole((32, D)), whole((D, D)), whole((1, D)),
+                         whole((8, D)), whole((heads, seq)), whole((1, seq))] + [whole(piece)] * 4,
+        [ANY, ANY, ANY, whole((group, *quarter))],
+        [sds((group, part, D), BF16), buffer, buffer, sds((group, *quarter), BF16)],
+        [pltpu.VMEM((3, D, D), F32), pltpu.VMEM((1, D), F32), pltpu.VMEM((group, part, D), BF16),
+         pltpu.VMEM(piece, BF16), pltpu.VMEM((shards, *dense_slot), BF16)] + reduce_scratch(dense_slot)
+        + [dma((group,)), dma((group,)), dma((1,)), pltpu.VMEM((group - 1, *quarter), BF16),
+           pltpu.VMEM((group, *quarter), BF16), pltpu.VMEM((group, *quarter), BF16), dma((2 * group,)), dma((2 * group,))] + gather_sems(),
+        flops=12 * seq * D * D, nbytes=24 * 2**20, collective=8,
+    )(x, normed, dq, dk, dv, dh, first, second, params, grad_output, grad_gain_m, grad_router,
+      dist.reshape(heads, seq), bucket_row, sum0, sum1, sum2, sum3)
+    spec = pl.BlockSpec((1, D, chunk), lambda i: (i, 0, 0))
     expert_in, expert_out = call(
-        unpack_kernel, "unpack", (shards,),
-        [pl.BlockSpec((1, 2, chunk, D), lambda i: (i, 0, 0, 0))],
+        unpack_kernel, "unpack", (shards,), [spec, spec],
         [pl.BlockSpec((1, D, chunk), lambda i: (0, 0, i)), pl.BlockSpec((1, chunk, D), lambda i: (0, i, 0))],
         [sds(w_expert_in.shape, F32), sds(w_expert_out.shape, F32)], nbytes=28 * 2**20,
-    )(gathered)
-    dense = lax.psum(lax.psum_scatter(dense, "dp", scatter_dimension=0, tiled=True)[0], "expert").astype(F32)
-    grad_table = jnp.einsum(
-        "bx,hx->bh", hot_buckets.astype(F32), dist.reshape(heads, seq), precision=TOP_PRECISION
-    )
-    grad_router = jnp.dot(grad_router[:, :experts], turn.astype(F32).T, precision=TOP_PRECISION)
-    small = lax.psum(
-        jnp.concatenate([
-            grad_gain_a.reshape(shards, -1), grad_gain_m.reshape(shards, -1),
-            grad_router.reshape(shards, -1), grad_table.reshape(shards, -1)], axis=1),
-        ("dp", "expert"),
-    )
-    small = lax.dynamic_slice_in_dim(small, shard, 1, axis=0)[0]
+    )(*gathered)
+    dense = dense.reshape(dense_slot).astype(F32)
+    rest = dense[0, 2 * share :]
+    line = lax.dynamic_slice_in_dim(rest[:16], shard * share, share, axis=1)
+    grad_table = lax.dynamic_slice_in_dim(rest[16 : 16 + heads], shard * rel_bias.shape[0], rel_bias.shape[0], axis=1)
     return (
         layer_out,
-        grad_in,
-        small[:share],
-        dense[:share],
-        dense[share : 2 * share],
-        dense[2 * share : 3 * share],
-        dense[3 * share :],
-        small[share : 2 * share],
-        small[2 * share : 2 * share + router.size].reshape(router.shape),
-        small[2 * share + router.size :].reshape(rel_bias.shape),
+        grad_in.astype(F32),
+        line[0],
+        dense[0, :share],
+        dense[0, share : 2 * share],
+        dense[1, :share],
+        dense[1, share : 2 * share],
+        line[1],
+        line[8 : 8 + experts].T,
+        grad_table.T,
         expert_in,
         expert_out,
     )

time: 817 us -> 613 us (0.75)
  Pallas kernels: 290 us -> 589 us
  waiting for transfers between devices: 299 us -> 0.01 us
  blocking collectives: 122 us -> 0 us
  local copies, waits for them, and re-layouts: 40.4 us -> 9.51 us
  starting transfers between devices: 25.1 us -> 1.55 us
  between operations: 14.6 us -> 1.24 us
  other arithmetic: 18.1 us -> 5.11 us
    pallas_call x10 -> x9, Pallas kernels: 255 us -> 555 us  [the longest x4 251 us: run_expert(): call(functools.partial(expert_kernel, index=index, capacity=capacity, fet...]
    reduce_scatter x5 -> x0, waiting for transfers between devices: 160 us -> none  [the longest x4 104 us: on_device_whole(): lax.psum_scatter(dw, 'dp', scatter_dimension=0, tiled=True)[0]]
    ppermute x6 -> x1, waiting for transfers between devices: 106 us -> 0.01 us  [on_device_whole(): lax.ppermute(sum2, 'expert', [(s, (s + 2) % group) for s in range(group)])]
    all_to_all x2 -> x0, blocking collectives: 68.8 us -> none  [the longest x1 58.6 us: back(): lax.all_to_all(values.reshape(group, seq // group, D), 'expert', split_ax...]
    psum x1 -> x0, blocking collectives: 52.8 us -> none  [on_device_whole(): lax.psum(jnp.concatenate([grad_gain_a.reshape(shards, -1), grad_gain_m.re...]
    all_to_all x3 -> x0, waiting for transfers between devices: 32 us -> none  [the longest x2 32 us: across(): lax.all_to_all(values, 'expert', split_axis=0, concat_axis=1, tiled=True)[0]]
    all_to_all x3 -> x0, starting transfers between devices: 11.7 us -> none  [the longest x2 8.02 us: across(): lax.all_to_all(values, 'expert', split_axis=0, concat_axis=1, tiled=True)[0]]
    ppermute x6 -> x1, starting transfers between devices: 13 us -> 1.55 us  [on_device_whole(): lax.ppermute(sum2, 'expert', [(s, (s + 2) % group) for s in range(group)])]
  transfers between devices with their start and end apart: 20 -> 1, of which waited for: 7 -> 0; matrix products, arithmetic and copies ran while one was open for 6% -> 0% of each run, Pallas kernels for 34% -> 13%
where the time goes in v2:
time: 613 us; the launch traced here: 606 us
  Pallas kernels  589 us (96%)
  local copies, waits for them, and re-layouts  9.51 us (2%)
    pallas_call x4, Pallas kernels, run_expert(): call(functools.partial(expert_kernel, index=index, capacity=capacity, fet...  251 us
    pallas_call x1, Pallas kernels, on_device_whole(): call(functools.partial(close_kernel, share=share, group=group, experts=ex...  108 us
    pallas_call x1, Pallas kernels, on_device_whole(): call(functools.partial(attend_kernel, width=width, group=group), 'attend'...  70.3 us
    pallas_call x1, Pallas kernels, on_device_whole(): call(functools.partial(open_kernel, group=group, share=share, heads=heads...  61.8 us
    pallas_call x1, Pallas kernels, on_device_whole(): call(functools.partial(attend_back_kernel, width=width, scale=scale, grou...  53.6 us
    pallas_call x1, Pallas kernels, on_device_whole(): call(functools.partial(combine_kernel, share=share, experts=experts, capa...  25.4 us
  transfers between devices with their start and end apart: 1, of which 0 were waited for; matrix products, arithmetic and copies ran while one was open for 0% of the time, Pallas kernels for 13%

profile of v2, /device:TPU:0, one launch (start us, length us, event | category | flops | bytes accessed | tf_op | source)
XLA Modules:
  0.0 606.1 jit_solution(10956615857679865392)
XLA Ops:
  0.6 0.8 copy.27
  1.4 1.3 pad.16.routes_ref
  2.7 0.7 fusion.10
  3.4 1.3 fusion.4.small_ref
  4.7 61.8 %open.1 = (bf16[4,256,768]{2,1,0:T(8,128)(2,1)}, bf16[2,768,384]{2,1,0:T(8,128)(2,1)}, bf16[8,192,768]{2,1,0:T(8,128)(2,1)}, bf16[8,224,768]{2,1,0:T(8,128)(2,1)...) custom-call(bf16[4,256,768]{2,1,0:T(8,128)(2,1)} %x_ref.1, ...), custom_call_target="tpu_custom_call" | custom-call | tf_op jit(solution)/shard_map/open/pallas_call | solution.py:1302
  66.5 70.3 %attend.1 = (bf16[1024,768]{1,0:T(8,128)(2,1)}, f32[6,2,1024]{2,1,0:T(2,128)}, bf16[12,4,256,256]{3,2,1,0:T(8,128)(2,1)}, bf16[4,256,768]{2,1,0:T(8,128)(2,1)}, ...) custom-call(bf16[1024,768]{1,0:T(8,128)(2,1)} %get-tuple-element.75.q_ref, ...), custom_call_target="tpu_custom_call" | custom-call | flops 6442450944 | bytes 16777216 | tf_op jit(solution)/shard_map/attend/pallas_call | solution.py:1320
  136.8 7.8 %route.1 = (f32[1024,768]{1,0:T(8,128)}, bf16[1024,768]{1,0:T(8,128)(2,1)}, f32[1024,128]{1,0:T(8,128)}, f32[1024,128]{1,0:T(8,128)}) custom-call(bf16[1024,768]{1,0:T(8,128)(2,1)} %bitcast.32, bf16[1024,768]{1,0:T(8,128)(2,1)} %get-tuple-element.83.o_ref, bf16[8,224,768]{2,1,0:T(8,128)(2,1)} %get-tuple-element.84.second_ref, ...), custom_call_target="tpu_custom_call" | custom-call | flops 1207959552 | bytes 12582912 | tf_op jit(solution)/shard_map/route/pallas_call | solution.py:1331
  144.6 58.4 %expert1.1 = (bf16[768,768]{1,0:T(8,128)(2,1)}, bf16[768,768]{1,0:T(8,128)(2,1)}, bf16[8,2,768,384]{3,2,1,0:T(8,128)(2,1)}, bf16[8,768,384]{2,1,0:T(8,128)(2,1)}...) custom-call(bf16[1024,768]{1,0:T(8,128)(2,1)} %get-tuple-element.87.a_ref, bf16[1024,768]{1,0:T(8,128)(2,1)} %bitcast.43, ...), custom_call_target="tpu_custom_call" | custom-call | flops 21743271936 | bytes 25165824 | tf_op jit(solution)/shard_map/expert1/pallas_call | solution.py:1367
  203.0 85.1 %expert3.1 = (bf16[768,768]{1,0:T(8,128)(2,1)}, bf16[768,768]{1,0:T(8,128)(2,1)}, bf16[8,2,768,384]{3,2,1,0:T(8,128)(2,1)}, bf16[8,768,384]{2,1,0:T(8,128)(2,1)}...) custom-call(bf16[1024,768]{1,0:T(8,128)(2,1)} %get-tuple-element.87.a_ref, bf16[1024,768]{1,0:T(8,128)(2,1)} %bitcast.44, ...), custom_call_target="tpu_custom_call" | custom-call | flops 21743271936 | bytes 25165824 | tf_op jit(solution)/shard_map/expert3/pallas_call | solution.py:1367
  288.1 54.6 %expert2.1 = (bf16[768,768]{1,0:T(8,128)(2,1)}, bf16[768,768]{1,0:T(8,128)(2,1)}, bf16[8,2,768,384]{3,2,1,0:T(8,128)(2,1)}, bf16[2,768,384]{2,1,0:T(8,128)(2,1)}, bf16[2,768,384]{2,1,0:T(8,128)(2,1)}) custom-call(bf16[1024,768]{1,0:T(8,128)(2,1)} %get-tuple-element.87.a_ref, bf16[1024,768]{1,0:T(8,128)(2,1)} %bitcast.45, ...), custom_call_target="tpu_custom_call" | custom-call | flops 21743271936 | bytes 25165824 | tf_op jit(solution)/shard_map/expert2/pallas_call | solution.py:1367
  342.8 52.4 %expert0.1 = (bf16[768,768]{1,0:T(8,128)(2,1)}, bf16[768,768]{1,0:T(8,128)(2,1)}, bf16[8,2,768,384]{3,2,1,0:T(8,128)(2,1)}, bf16[2,768,384]{2,1,0:T(8,128)(2,1)}, bf16[2,768,384]{2,1,0:T(8,128)(2,1)}) custom-call(bf16[1024,768]{1,0:T(8,128)(2,1)} %get-tuple-element.87.a_ref, bf16[1024,768]{1,0:T(8,128)(2,1)} %bitcast.46, ...), custom_call_target="tpu_custom_call" | custom-call | flops 21743271936 | bytes 25165824 | tf_op jit(solution)/shard_map/expert0/pallas_call | solution.py:1367
  395.2 1.6 collective-permute-start
  396.8 25.4 %combine.1 = (bf16[1024,768]{1,0:T(8,128)(2,1)}, f32[1024,768]{1,0:T(8,128)}, bf16[1024,768]{1,0:T(8,128)(2,1)}, f32[768,768]{1,0:T(8,128)}, f32[1,768]{1,0:T(1,128)}, /*index=5*/f32[8,768]{1,0:T(8,128)}) custom-call(f32[1024,768]{1,0:T(8,128)} %get-tuple-element.86.h_ref, bf16[1024,768]{1,0:T(8,128)(2,1)} %get-tuple-element.87.a_ref, ...), custom_call_target="tpu_custom_call" | custom-call | flops 14495514624 | bytes 33554432 | tf_op jit(solution)/shard_map/combine/pallas_call | solution.py:1388
  422.2 53.6 %attend_back.1 = (bf16[1024,768]{1,0:T(8,128)(2,1)}, bf16[1024,768]{1,0:T(8,128)(2,1)}, bf16[1024,768]{1,0:T(8,128)(2,1)}, f32[6,2,1024]{2,1,0:T(2,128)}, bf16[2...) custom-call(bf16[1024,768]{1,0:T(8,128)(2,1)} %get-tuple-element.75.q_ref, ...), custom_call_target="tpu_custom_call" | custom-call | flops 16106127360 | bytes 25165824 | tf_op jit(solution)/shard_map/attend_back/pallas_call | solution.py:1397
  475.8 1.5 reshape.55.dist_ref
  477.3 0.0 collective-permute-done.sum2
  477.3 0.0 copy-start.2
  477.3 1.0 copy-done.2
  478.3 107.9 %close.1 = (bf16[4,256,768]{2,1,0:T(8,128)(2,1)}, bf16[8,768,384]{2,1,0:T(8,128)(2,1)}, bf16[8,768,384]{2,1,0:T(8,128)(2,1)}, bf16[4,112,768]{2,1,0:T(8,128)(2,1)}) custom-call(bf16[1024,768]{1,0:T(8,128)(2,1)} %bitcast.33, bf16[1024,768]{1,0:T(8,128)(2,1)} %get-tuple-element.118.a_ref, bf16[1024,768]{1,0:T(8,128)(2,1)} %get-tuple-element.119.dq_ref, ...), custom_call_target="tpu_custom_call" | custom-call | flops 7247757312 | bytes 25165824 | tf_op jit(solution)/shard_map/close/pallas_call | solution.py:1410
  586.2 1.2 bitcast_convert_fusion
  587.4 0.0 copy-start.1
  587.4 1.0 slice_bitcast_fusion
  588.4 0.8 copy-done.1
  589.2 1.9 convert_element_type.15
  591.2 0.6 fusion.12
  591.7 0.7 dynamic-slice_bitcast_fusion
  592.4 0.1 constant_dynamic-slice_fusion.2
  592.5 0.7 copy.28
  593.1 0.0 copy-start
  593.1 11.3 %unpack.1 = (f32[1,768,3072]{2,1,0:T(8,128)}, f32[1,3072,768]{2,1,0:T(8,128)}) custom-call(bf16[8,768,384]{2,1,0:T(8,128)(2,1)} %get-tuple-element.134.first_ref, bf16[8,768,384]{2,1,0:T(8,128)(2,1)} %get-tuple-element.135.second_ref), custom_call_target="tpu_custom_call" | custom-call | bytes 29360128 | tf_op jit(solution)/shard_map/unpack/pallas_call | solution.py:1424
  604.5 0.0 copy-done
  604.5 1.1 copy.30
  (2 shorter events, 0.0 us)
Async XLA Ops:
  395.2 82.0 %collective-permute-start = (bf16[2,768,384]{2,1,0:T(8,128)(2,1)}, bf16[2,768,384]{2,1,0:T(8,128)(2,1)S(1)}, u32[]{:S(2)}, u32[]{:S(2)}) collective-permute-start(bf16[2,768,384]{2,1,0:T(8,128)(2,1)} %get-tuple-element.130), channel_id=1, source_target_pairs={{0,2},{1,3},{2,0},{3,1},{4,6},{5,7},{6,4},{7,5},{8,10},{9,11},{10,... | collective-permute-start | bytes 3538952 | tf_op jit(solution)/shard_map/ppermute | solution.py:1387
  477.3 1.0 copy-start.2
  587.4 1.8 copy-start.1
  593.1 11.3 %copy-start = (bf16[4,256,768]{2,1,0:T(8,128)(2,1)S(1)}, bf16[4,256,768]{2,1,0:T(8,128)(2,1)}, u32[]{:S(2)}) copy-start(bf16[4,256,768]{2,1,0:T(8,128)(2,1)} %get-tuple-element.156) | copy-start | bytes 4718596

commit v3 on v2

--- a/solution.py
+++ b/solution.py
@@ -448,49 +448,56 @@
         pltpu.make_async_copy(source_first, first.at[me], local.at[0]),
         pltpu.make_async_copy(source_second, second.at[me], local.at[1]),
     ]
-    stage0 = [
+    near = [
         remote(0, source_first, first.at[me], along_x),
         remote(1, source_second, second.at[me], along_y),
-        remote(2, source_first, first.at[me], core),
-        remote(3, source_second, second.at[me], core),
+        remote(2, source_first, first.at[me], along_y),
+        remote(3, source_second, second.at[me], along_x),
     ]
-    stage1 = [
-        remote(4, first.at[along_x], first.at[along_x], along_y),
-        remote(5, second.at[along_y], second.at[along_y], along_x),
-        remote(6, source_first, first.at[me], along_y),
-        remote(7, source_second, second.at[me], along_x),
+    paired = [
+        remote(4, source_first, first.at[me], core),
+        remote(5, source_second, second.at[me], core),
+    ]
+    far = [
+        remote(6, first.at[along_x], first.at[along_x], along_y),
+        remote(7, second.at[along_y], second.at[along_y], along_x),
+    ]
+    paired_near = [
         remote(8, first.at[along_x], first.at[along_x], core),
         remote(9, second.at[along_y], second.at[along_y], core),
-    ]
-    stage2 = [
         remote(10, first.at[along_y], first.at[along_y], core),
         remote(11, second.at[along_x], second.at[along_x], core),
+    ]
+    paired_far = [
         remote(12, first.at[across], first.at[across], core),
         remote(13, second.at[across], second.at[across], core),
     ]
 
     def start0():
-        for copy in stage0 + own:
+        for copy in near + paired + own:
             copy.start()
 
     def start1():
-        stage0[0].wait_recv()
-        stage0[1].wait_recv()
-        for copy in stage1:
+        near[0].wait_recv()
+        far[0].start()
+        near[1].wait_recv()
+        far[1].start()
+        near[2].wait_recv()
+        near[3].wait_recv()
+        for copy in paired_near:
             copy.start()
 
     def start2():
-        for copy in stage1[:4]:
+        for copy, onward in zip(far, paired_far):
             copy.wait_recv()
-        for copy in stage2:
-            copy.start()
+            onward.start()
 
     def finish():
         for copy in own:
             copy.wait()
-        for copy in stage0[2:] + stage1[4:] + stage2:
+        for copy in paired + paired_near + paired_far:
             copy.wait_recv()
-        for copy in stage0 + stage1 + stage2:
+        for copy in near + paired + far + paired_near + paired_far:
             copy.wait_send()
 
     return start0, start1, start2, finish
@@ -506,6 +513,13 @@
 
 def sds(shape, dtype):
     return jax.ShapeDtypeStruct(shape, dtype)
+
+
+def partner(place, k):
+    return 2 * lax.rem(place // 2 + k // 2, 2) + lax.rem(lax.rem(place, 2) + k % 2, 2)
+
+
+ORDER = (1, 0, 3, 2)
 
 
 def place_devices(group):
@@ -534,16 +548,17 @@
     return copies
 
 
-def slice_copies(w_in, w_out, target, send, recv, base, place):
+def slice_copies(w_in, w_out, first, second, send, recv, base, place):
     me = lax.axis_index("dp")
-    chunk = target.shape[2]
-    rows_in = w_in.at[0, :, pl.ds(pl.multiple_of(me * chunk, 128), chunk)]
-    rows_out = pl.ds(pl.multiple_of(me * chunk, 128), chunk)
-    pieces = (
-        (rows_in, target.at[0]),
-        (w_out.at[0, rows_out, pl.ds(0, chunk)], target.at[1, pl.ds(0, chunk)]),
-        (w_out.at[0, rows_out, pl.ds(chunk, chunk)], target.at[1, pl.ds(chunk, chunk)]),
-    )
+    chunk = (first if second is None else second).shape[1]
+    here = pl.ds(pl.multiple_of(me * chunk, 128), chunk)
+    pieces = []
+    if first is not None:
+        pieces.append((w_in.at[0, :, here], first))
+    if second is not None:
+        pieces += [
+            (w_out.at[0, here, pl.ds(at, chunk)], second.at[pl.ds(at, chunk)]) for at in (0, chunk)
+        ]
     return [
         along_axis(source, goal, send.at[base + i], recv.at[base + i], place)
         for i, (source, goal) in enumerate(pieces)
@@ -585,13 +600,16 @@
         own[q] = own[q] + pair[q]
 
     def start():
-        for copy in loads + pairs:
+        pairs[0].start()
+        for copy in loads:
             copy.start()
 
     def far():
         merge(0)
         far_first.start()
         far_second.start()
+        for copy in pairs[1:]:
+            copy.start()
 
     def near():
         merge(1)
@@ -635,12 +653,15 @@
     return slots_ref[:, index * share : (index + 1) * share, :].reshape(-1, D)
 
 
-def open_kernel(
-    x_ref, routes_ref, w_in_ref, w_out_ref, wq_ref, wk_ref, wv_ref, wo_ref, small_ref, buckets_ref, seg_ref,
-    x_out, piece_out, first_out, second_out, a_ref, q_ref, k_ref, v_ref, params_ref, line_ref, across_ref, down_ref,
+def front_kernel(
+    x_ref, grad_ref, routes_ref, w_in_ref, w_out_ref, wq_ref, wk_ref, wv_ref, wo_ref, small_ref, buckets_ref, seg_ref,
+    x_out, grad_out, c0_out, c1_out, first_out, second_out, a_out, q_out, k_out, v_out, o_out, table_out,
+    h_out, n_out, gate_out, pr_out, gather_first, gather_second, piece_out, params_ref, across_ref, down_ref, lse_ref,
     land, routes_land, first, second, stage_first, stage_second,
-    x_send, x_recv, r_send, r_recv, p_send, p_recv, keep, own_local, send, recv, local,
-    *, group, share, heads, experts, scale
+    a_ref, q_ref, k_ref, v_ref, o_ref, table_ref, h_ref, n_ref, gate_ref, pr_ref, line_ref,
+    x_send, x_recv, r_send, r_recv, g_send, g_recv, p_send, p_recv, keep, own_local, out_sem,
+    send, recv, local, send_w, recv_w, local_w,
+    *, group, share, heads, experts, scale, width
 ):
     me = lax.axis_index("dp")
     place = lax.axis_index("expert")
@@ -660,12 +681,15 @@
     meet(plane_devices() + place_devices(group))
     moves = swap_copies(routes_ref, routes_land, r_send, r_recv, group)
     moves_x = swap_copies(x_ref, land, x_send, x_recv, group)
-    slices = slice_copies(w_in_ref, w_out_ref, piece_out, p_send, p_recv, 0, lax.rem(place + group - 1, group))
+    moves_g = swap_copies(grad_ref, grad_out, g_send, g_recv, group)
+    slices = slice_copies(w_in_ref, w_out_ref, piece_out.at[0], piece_out.at[1], p_send, p_recv, 0, partner(place, 1))
+    distant = slice_copies(w_in_ref, w_out_ref, c0_out, c1_out, p_send, p_recv, 3, partner(place, 3))
     kept = [
         pltpu.make_async_copy(routes_ref.at[place], routes_land.at[place], keep.at[0]),
         pltpu.make_async_copy(x_ref.at[place], land.at[place], keep.at[1]),
+        pltpu.make_async_copy(grad_ref.at[place], grad_out.at[place], keep.at[2]),
     ]
-    for copy in moves + moves_x + slices + kept:
+    for copy in moves + moves_x + kept:
         copy.start()
     for copy in staged:
         copy.wait()
@@ -677,13 +701,13 @@
         copy.wait_recv()
     seq = down_ref.shape[0]
     row_id = lax.broadcasted_iota(jnp.int32, (8, routes_land.shape[2]), 0)
+    holder = jnp.full(row_id.shape, -1, jnp.int32)
+    for k in range(experts):
+        holder = jnp.where(row_id == k, partner(place, ORDER[k]), holder)
     named = []
     for p in range(group):
-        picks = []
-        for c in range(2):
-            pick = routes_land[p, c : c + 1, :] - place
-            picks.append(jnp.where(pick < 0, pick + experts, pick))
-        named.append(((picks[0] == row_id) | (picks[1] == row_id)).astype(F32))
+        picks = [routes_land[p, c : c + 1, :] == holder for c in range(2)]
+        named.append((picks[0] | picks[1]).astype(F32))
     named = jnp.concatenate(named, axis=1)
     earlier = lax.broadcasted_iota(jnp.int32, (seq, seq), 0) < lax.broadcasted_iota(jnp.int32, (seq, seq), 1)
     before = nn(named.astype(BF16), earlier.astype(F32).astype(BF16))
@@ -698,18 +722,20 @@
     start1()
     start2()
     finish()
-    out_copies = [
-        pltpu.make_async_copy(first, first_out, own_local.at[0]),
-        pltpu.make_async_copy(second, second_out, own_local.at[1]),
-    ]
-    for copy in out_copies:
-        copy.start()
+    out_copies = []
+
+    def put(source, target):
+        out_copies.append(pltpu.make_async_copy(source, target, out_sem.at[len(out_copies)]))
+        out_copies[-1].start()
+
+    put(first, first_out)
+    put(second, second_out)
     params = second[0, 2 * share :, :].astype(F32)
     for slot in range(1, second.shape[0]):
         params = params + second[slot, 2 * share :, :].astype(F32)
     turned = []
     for k in range(experts):
-        wanted = lax.rem(place + k, experts)
+        wanted = partner(place, ORDER[k])
         picked = jnp.zeros((1, D), F32)
         for e in range(experts):
             picked = picked + params[8 + e : 9 + e, :] * jnp.where(wanted == e, 1.0, 0.0)
@@ -725,8 +751,9 @@
     kept[1].wait()
     for copy in moves_x:
         copy.wait_recv()
-    out_copies.append(pltpu.make_async_copy(land, x_out, own_local.at[2]))
-    out_copies[-1].start()
+    for copy in slices + distant + moves_g:
+        copy.start()
+    put(land, x_out)
     part = land.shape[1]
     for p in range(group):
         here = slice(p * part, (p + 1) * part)
@@ -738,10 +765,52 @@
         q_ref[here, :] = (q.astype(F32) * scale).astype(BF16)
         k_ref[here, :] = nn(normed, weight(first, 1, share)).astype(BF16)
         v_ref[here, :] = nn(normed, weight(second, 0, share)).astype(BF16)
-    for copy in slices:
+    for source, target in ((a_ref, a_out), (q_ref, q_out), (k_ref, k_out), (v_ref, v_out)):
+        put(source, target)
+    gather = gather_copies(
+        gather_first, gather_second, piece_out.at[0], piece_out.at[1], send_w, recv_w, local_w
+    )
+    pairs = 128 // width
+    count = heads // pairs
+
+    def table_copy(n):
+        heads_here = pl.ds(n * pairs, pairs)
+        return pltpu.make_async_copy(table_ref.at[heads_here], table_out.at[heads_here], keep.at[3 + n])
+
+    def attend(n, carry):
+        @pl.when(n == 4)
+        def _():
+            for copy in slices:
+                copy.wait_recv()
+            gather[0]()
+
+        attend_pair(n, q_ref, k_ref, v_ref, line_ref, table_ref, down_ref, across_ref, o_ref, lse_ref, width)
+        table_copy(n).start()
+        return carry
+
+    lax.fori_loop(0, count, attend, 0)
+    put(o_ref, o_out)
+
+    def route(i, carry):
+        here = pl.ds(pl.multiple_of(i * TILE, TILE), TILE)
+        route_rows(
+            land[i], o_ref[here, :], second, params_ref, down_ref, h_ref, n_ref, gate_ref, pr_ref, here, share, experts
+        )
+        return carry
+
+    lax.fori_loop(0, group, route, 0)
+    for source, target in ((h_ref, h_out), (n_ref, n_out), (gate_ref, gate_out), (pr_ref, pr_out)):
+        put(source, target)
+    gather[1]()
+    gather[2]()
+    kept[2].wait()
+    for copy in distant + moves_g:
         copy.wait_recv()
-    for copy in moves + moves_x + slices:
+    for copy in moves + moves_x + slices + distant + moves_g:
         copy.wait_send()
+    gather[3]()
+    for n in range(count):
+        table_copy(n).wait()
     for copy in out_copies:
         copy.wait()
 
@@ -756,57 +825,51 @@
     return jnp.where(allowed, scores, MASKED)
 
 
-def attend_kernel(
-    q_ref, k_ref, v_ref, line_ref, down_ref, across_ref, source, grad_ref, w_in_ref, w_out_ref,
-    o_ref, lse_ref, table_ref, grad_out, piece_out, gather_first, gather_second,
-    g_send, g_recv, p_send, p_recv, keep, send, recv, local, *, width, group
-):
-    step = pl.program_id(0)
-    last = pl.num_programs(0) - 1
-    place = lax.axis_index("expert")
-    start0, start1, start2, finish = gather_copies(
-        gather_first, gather_second, source.at[0], source.at[1], send, recv, local
-    )
-    moves = swap_copies(grad_ref, grad_out, g_send, g_recv, group)
-    slices = slice_copies(w_in_ref, w_out_ref, piece_out, p_send, p_recv, 0, lax.rem(place + 1, group))
-    kept = pltpu.make_async_copy(grad_ref.at[place], grad_out.at[place], keep.at[0])
-
-    @pl.when(step == 0)
-    def _():
-        meet(plane_devices() + place_devices(group))
-        start0()
-        for copy in moves + slices:
-            copy.start()
-        kept.start()
-
-    @pl.when(step == 3)
-    def _():
-        start1()
-
-    heads = q_ref.shape[1] // width
+def route_rows(x, o, second_ref, params_ref, down_ref, h_ref, a_ref, gate_ref, pr_ref, here, share, experts):
+    h1 = x.astype(F32) + nn(o, weight(second_ref, 1, share))
+    h_ref[here, :] = h1
+    inverse = lax.rsqrt(jnp.mean(h1 * h1, axis=-1, keepdims=True) + EPSILON)
+    normed = (h1 * inverse * params_ref[1:2, :]).astype(BF16)
+    a_ref[here, :] = normed
+    router = jnp.concatenate([params_ref[8:16, :], jnp.zeros((120, D), F32)], axis=0).astype(BF16)
+    logits = nt(normed, router)
+    lane = lax.broadcasted_iota(jnp.int32, logits.shape, 1)
+    logits = jnp.where(lane < experts, logits, MASKED)
+    lifted = jnp.exp(logits - logits.max(axis=-1, keepdims=True))
+    pr = lifted / lifted.sum(axis=-1, keepdims=True)
+    named = (down_ref[here, :] >= 0) & (lane < experts)
+    picked = jnp.where(named, pr, 0.0)
+    pr_ref[here, :] = pr
+    gate_ref[here, :] = picked / picked.sum(axis=-1, keepdims=True)
+
+
+def attend_pair(n, q_ref, k_ref, v_ref, line_ref, table_ref, down_ref, across_ref, o_ref, lse_ref, width):
+    columns = pl.ds(pl.multiple_of(n * 128, 128), 128)
+    heads = 128 // width
     for h in range(heads):
-        row = line_ref[h]
+        row = line_ref[n * heads + h]
         for gap in range(table_ref.shape[1]):
             ahead = row[:, gap * TILE : (gap + 1) * TILE]
             back = row[:, (gap - 1) * TILE : gap * TILE] if gap else jnp.zeros_like(ahead)
             grid = jnp.broadcast_to(jnp.concatenate([ahead, back], axis=1), (TILE, 2 * TILE))
             grid = pltpu.roll(grid, 0, 1, stride=1, stride_axis=0)
-            table_ref[h, gap] = grid[:, :TILE].astype(BF16)
-
-    blocks = q_ref.shape[0] // TILE
-    turned = [v_ref[:, h * width : (h + 1) * width].T for h in range(heads)]
+            table_ref[n * heads + h, gap] = grid[:, :TILE].astype(BF16)
+    q_all, k_all, v_all = q_ref[:, columns], k_ref[:, columns], v_ref[:, columns]
+    blocks = q_all.shape[0] // TILE
+    turned = [v_all[:, h * width : (h + 1) * width].T for h in range(heads)]
     for i in range(blocks):
         here = slice(i * TILE, (i + 1) * TILE)
         outs = []
         for h in range(heads):
             lanes = slice(h * width, (h + 1) * width)
-            q = q_ref[here, lanes]
+            q = q_all[here, lanes]
             pieces = []
             for j in range(i + 1):
                 there = slice(j * TILE, (j + 1) * TILE)
                 pieces.append(
                     masked_scores(
-                        k_ref[there, lanes], q, table_ref, h, i, j, down_ref[there, 8:9], across_ref[8:9, here]
+                        k_all[there, lanes], q, table_ref, n * heads + h, i, j, down_ref[there, 8:9],
+                        across_ref[8:9, here]
                     )
                 )
             top = pieces[0].max(axis=0, keepdims=True)
@@ -819,24 +882,14 @@
                 total = total + lifted.sum(axis=0, keepdims=True)
                 acc = acc + nn(turned[h][:, j * TILE : (j + 1) * TILE], lifted.astype(BF16))
             outs.append(acc / total)
-            lse_ref[0, h : h + 1, here] = top + jnp.log(total)
-        o_ref[here, :] = jnp.concatenate(outs, axis=0).T.astype(BF16)
-
-    @pl.when(step == last)
-    def _():
-        start2()
-        kept.wait()
-        for copy in moves + slices:
-            copy.wait_recv()
-        for copy in moves + slices:
-            copy.wait_send()
-        finish()
+            lse_ref[n, h : h + 1, here] = top + jnp.log(total)
+        o_ref[here, columns] = jnp.concatenate(outs, axis=0).T.astype(BF16)
 
 
 def attend_back_kernel(
-    q_ref, k_ref, v_ref, do_ref, table_ref, down_ref, across_ref, lse_ref, result_ref, terms,
-    dq_ref, dk_ref, dv_ref, dist_ref, sums_ref, result_out, sum_ref, dk_sum, dv_sum,
-    o_send, o_recv, keep, own, pair, inbox, send, recv, local, *, width, scale, group
+    q_ref, k_ref, v_ref, do_ref, table_ref, down_ref, across_ref, lse_ref, a_ref, passed, terms,
+    dq_ref, dk_ref, dv_ref, dist_ref, dwq_ref, dwk_ref, dwv_ref, sums_ref, pass_out,
+    sum_ref, dk_sum, dv_sum, turned_a, p_send, p_recv, own, pair, inbox, send, recv, local, *, width, scale, group
 ):
     step = pl.program_id(0)
     last = pl.num_programs(0) - 1
@@ -845,24 +898,19 @@
     def emit(half, value):
         sums_ref[half] = value.astype(BF16)
 
-    start, far, near, late, finish = reduce_copies(terms, own, pair, inbox, send, recv, local, emit)
-    moves = swap_copies(result_ref, result_out, o_send, o_recv, group)
-    kept = pltpu.make_async_copy(result_ref.at[place], result_out.at[place], keep.at[0])
+    start, far, near, late, finish = reduce_copies(terms.at[1], own, pair, inbox, send, recv, local, emit)
+    hop = along_axis(passed, pass_out, p_send.at[0], p_recv.at[0], partner(place, 2))
 
     @pl.when(step == 0)
     def _():
-        meet(plane_devices() + place_devices(group))
+        meet(plane_devices() + [(lax.axis_index("dp"), partner(place, 2))])
         start()
-        for copy in moves:
-            copy.start()
-        kept.start()
-
-    @pl.when(step == 1)
-    def _():
+        hop.start()
         far()
+        turned_a[...] = a_ref[...].T
         near()
 
-    @pl.when(step == 5)
+    @pl.when(step == 3)
     def _():
         late()
 
@@ -915,169 +963,255 @@
             while half:
                 part = part[:half] + pltpu.roll(part[half : 2 * half], 2 * TILE - half, 1)
                 half //= 2
-            dist_ref[0, h : h + 1, gap * TILE : (gap + 1) * TILE] += part[:, :TILE]
+            dist_ref[h, :, gap * TILE : (gap + 1) * TILE] += part[:, :TILE]
             if gap:
-                dist_ref[0, h : h + 1, (gap - 1) * TILE : gap * TILE] += part[:, TILE:]
+                dist_ref[h, :, (gap - 1) * TILE : gap * TILE] += part[:, TILE:]
     dk_ref[...] = dk_sum[...].astype(BF16)
     dv_ref[...] = dv_sum[...].astype(BF16)
 
+    grads = jnp.concatenate([dq_ref[...], dk_ref[...], dv_ref[...]], axis=1)
+    sums = nn(turned_a[...], grads).astype(BF16)
+    for index, dw_ref in enumerate((dwq_ref, dwk_ref, dwv_ref)):
+        dw_ref[...] = sums[:, index * 128 : (index + 1) * 128]
+
     @pl.when(step == last)
     def _():
-        kept.wait()
-        for copy in moves:
-            copy.wait_recv()
-        for copy in moves:
-            copy.wait_send()
         finish()
-
-
-def route_kernel(
-    x_ref, o_ref, second_ref, params_ref, down_ref, h_ref, a_ref, gate_ref, pr_ref, *, share, experts
+        hop.wait()
+
+
+def experts_kernel(
+    a_ref, g_ref, gate_ref, across_ref, first_a, second_a, piece_c0, piece_c1, w_in_ref, w_out_ref,
+    eo_ref, da_ref, dw_out, sum_a, sum_c, piece_b, first_c, second_c, first_b, second_b,
+    rows_a, turned_a, rows_d, eo_sum, da_sum, w_in_two, w_out_two, dw_two, total_a,
+    w_sem, dw_sem, hop_send, hop_recv, save, free, own, pair, inbox, send_a, recv_a, local_a,
+    send_c, recv_c, local_c, *gather, capacity, group, shards
 ):
-    h1 = x_ref[...].astype(F32) + nn(o_ref[...], weight(second_ref, 1, share))
-    h_ref[...] = h1
-    inverse = lax.rsqrt(jnp.mean(h1 * h1, axis=-1, keepdims=True) + EPSILON)
-    normed = (h1 * inverse * params_ref[1:2, :]).astype(BF16)
-    a_ref[...] = normed
-    router = jnp.concatenate([params_ref[8:16, :], jnp.zeros((120, D), F32)], axis=0).astype(BF16)
-    logits = nt(normed, router)
-    lane = lax.broadcasted_iota(jnp.int32, logits.shape, 1)
-    logits = jnp.where(lane < experts, logits, MASKED)
-    lifted = jnp.exp(logits - logits.max(axis=-1, keepdims=True))
-    pr = lifted / lifted.sum(axis=-1, keepdims=True)
-    named = (down_ref[...] >= 0) & (lane < experts)
-    picked = jnp.where(named, pr, 0.0)
-    pr_ref[...] = pr
-    gate_ref[...] = picked / picked.sum(axis=-1, keepdims=True)
-
-
-def expert_kernel(a_ref, g_ref, gate_ref, across_ref, wi_ref, wo_ref, *refs, index, capacity, fetch, relay, reduce, pass_on, group):
-    refs = list(refs)
-    take = lambda count: [refs.pop(0) for _ in range(count)]
-    source = take(1) if fetch else None
-    relayed = take(2) if relay else None
-    terms = take(1) if reduce else None
-    passed = take(1) if pass_on else None
-    eo_ref, da_ref, dw_ref = take(3)
-    buffers = take(2) if fetch else None
-    relay_out = take(1) if relay else None
-    sums_ref = take(1)[0] if reduce else None
-    pass_out = take(1) if pass_on else None
-    rows_a, turned_a, rows_d, eo_sum, da_sum = take(5)
     step = pl.program_id(0)
     last = pl.num_programs(0) - 1
+    steps = shards // 2
+    turn = step // steps
+    slot = lax.rem(step, 2)
     place = lax.axis_index("expert")
-    at_start, at_end = [], []
-    at_step = {}
-    if fetch:
-        start0, start1, start2, finish = gather_copies(
-            *buffers, source[0].at[0], source[0].at[1], *take(3)
-        )
-        at_start.append(start0)
-        at_step[3] = [start1]
-        at_end += [start2, finish]
-    if relay:
-        send, recv = take(2)
-        down = along_axis(relayed[0], relay_out[0], send.at[0], recv.at[0], jnp.maximum(place - 1, 0))
-        up = along_axis(relayed[1], relay_out[0], send.at[1], recv.at[0], jnp.minimum(place + 1, group - 1))
-        middle = (place == 1) | (place == 2)
-
-        def start_relay():
-            @pl.when(middle)
-            def _():
-                down.start()
-                up.start()
-
-        def end_relay():
-            down.wait_recv()
-
-            @pl.when(middle)
-            def _():
-                down.wait_send()
-                up.wait_send()
-
-        at_start.append(start_relay)
-        at_end.append(end_relay)
-    if reduce:
-        scratch = take(6)
-
-        def emit(half, value):
-            sums_ref[half] = value.astype(BF16)
-
-        start, far, near, late, end_reduce = reduce_copies(terms[0], *scratch, emit)
-        at_start.append(start)
-        at_step[1] = [far]
-        at_step[2] = [near]
-        at_step[6 if fetch else 5] = [late]
-        at_end.append(end_reduce)
-    if pass_on:
-        send, recv = take(2)
-        hop = along_axis(passed[0], pass_out[0], send.at[0], recv.at[0], lax.rem(place + pass_on, group))
-        at_start.append(hop.start)
-        at_end.append(hop.wait)
-
-    if at_start:
-        @pl.when(step == 0)
-        def _():
-            far_devices = place_devices(group) if relay or pass_on else []
-            near_devices = plane_devices() if fetch or reduce else []
-            meet(near_devices + far_devices)
-            for action in at_start:
-                action()
-
-    for when, actions in at_step.items():
+    chunk = w_in_two.shape[3]
+
+    def loads(at, which):
+        c = lax.rem(at, steps)
+        two = lax.rem(at, 2)
+        if which != 1:
+            first, second = {0: (first_a, second_a), 2: (first_c, second_c), 3: (first_b, second_b)}[which]
+            both = pl.ds(2 * c, 2)
+            return [
+                pltpu.make_async_copy(first.at[both], w_in_two.at[two], w_sem.at[0, two]),
+                pltpu.make_async_copy(second.at[both], w_out_two.at[two], w_sem.at[1, two]),
+            ]
+        copies = []
+        for h in range(2):
+            cols = pl.ds(pl.multiple_of((2 * c + h) * chunk, 128), chunk)
+            copies.append(
+                pltpu.make_async_copy(w_in_ref.at[0, :, cols], w_in_two.at[two, h], w_sem.at[3 * h, two])
+            )
+            for l in range(2):
+                lanes = pl.ds(l * chunk, chunk)
+                copies.append(
+                    pltpu.make_async_copy(
+                        w_out_ref.at[0, cols, lanes], w_out_two.at[two, h, lanes], w_sem.at[3 * h + 1 + l, two]
+                    )
+                )
+        return copies
+
+    def each_turn(at, action):
+        for which in range(group):
+            @pl.when(at // steps == which)
+            def _(which=which):
+                for copy in loads(at, which):
+                    action(copy)
+
+    def saved(at):
+        two = lax.rem(at, 2)
+        return pltpu.make_async_copy(
+            dw_two.at[two], dw_out.at[at // steps, pl.ds(2 * lax.rem(at, steps), 2)], dw_sem.at[two]
+        )
+
+    gather_c = gather_copies(first_c, second_c, piece_c0, piece_c1, *gather[:3])
+    gather_b = gather_copies(first_b, second_b, piece_b.at[0], piece_b.at[1], *gather[3:])
+    relays = [
+        along_axis(piece, piece_b.at[i], hop_send.at[2 * i], hop_recv.at[2 * i], partner(place, 1))
+        for i, piece in enumerate((piece_c0, piece_c1))
+    ]
+    hop = along_axis(total_a, sum_a, hop_send.at[1], hop_recv.at[1], partner(place, 1))
+    keep = pltpu.make_async_copy(own.at[3], sum_c, save.at[0])
+
+    def emit_a(half, value):
+        total_a[half] = value.astype(BF16)
+
+    def emit_c(half, value):
+        own[3, half] = value.astype(BF16)
+
+    reduce_a = reduce_copies(dw_out.at[0], own, pair, inbox, send_a, recv_a, local_a, emit_a)
+    reduce_c = reduce_copies(dw_out.at[2], own, pair, inbox, send_c, recv_c, local_c, emit_c)
+
+    @pl.when(step == 0)
+    def _():
+        meet(plane_devices() + [(lax.axis_index("dp"), partner(place, 1))])
+        gather_c[0]()
+        for copy in relays:
+            copy.start()
+        each_turn(step, lambda copy: copy.start())
+
+    def release():
+        for device in plane_devices():
+            pl.semaphore_signal(free, inc=1, device_id=device, device_id_type=MESH)
+
+    def claim():
+        pl.semaphore_wait(free, len(plane_devices()))
+
+    schedule = {
+        3: [gather_c[1]],
+        6: [gather_c[2], gather_c[3], relays[0].wait, relays[1].wait, gather_b[0]],
+        9: [gather_b[1], reduce_a[0], reduce_a[1]],
+        10: [reduce_a[2]],
+        12: [reduce_a[3]],
+        14: [reduce_a[4], release, hop.start, claim, reduce_c[0], reduce_c[1]],
+        15: [reduce_c[2]],
+    }
+    for when, actions in schedule.items():
         @pl.when(step == when)
         def _(actions=actions):
             for action in actions:
                 action()
 
-    @pl.when(step == 0)
+    @pl.when(lax.rem(step, steps) == 0)
     def _():
         tokens = a_ref.shape[0]
-        slot = lax.broadcasted_iota(jnp.int32, (capacity, tokens), 0)
-        pick = (across_ref[index : index + 1, :] == slot).astype(BF16)
+        places = lax.broadcasted_iota(jnp.int32, (capacity, tokens), 0)
+        pick = (across_ref[pl.ds(turn, 1), :] == places).astype(BF16)
         rows = nn(pick, a_ref[...]).astype(BF16)
         rows_a[...] = rows
         turned_a[...] = rows.T
-        scaled = (gate_ref[:, index : index + 1] * g_ref[...].astype(F32)).astype(BF16)
-        rows_d[...] = nn(pick, scaled).astype(BF16)
+        lane = lax.broadcasted_iota(jnp.int32, gate_ref.shape, 1)
+        gate = jnp.sum(jnp.where(lane == turn, gate_ref[...], 0.0), axis=-1, keepdims=True)
+        rows_d[...] = nn(pick, (gate * g_ref[...].astype(F32)).astype(BF16)).astype(BF16)
         eo_sum[...] = jnp.zeros_like(eo_sum)
         da_sum[...] = jnp.zeros_like(da_sum)
 
+    each_turn(step, lambda copy: copy.wait())
+    ahead = step + 1
+
+    @pl.when((step < last) & (ahead != 3 * steps))
+    def _():
+        each_turn(ahead, lambda copy: copy.start())
+
+    @pl.when(step > 1)
+    def _():
+        saved(step - 2).wait()
+
     d = rows_d[...]
-    w_in = wi_ref[0]
-    w_out = wo_ref[0]
-    chunk = w_in.shape[1]
-    if index:
-        w_out = jnp.concatenate([w_out[:chunk], w_out[chunk:]], axis=1)
+    w_in = jnp.concatenate([w_in_two[slot, h] for h in range(2)], axis=1)
+    w_out = jnp.concatenate(
+        [
+            jnp.concatenate([w_out_two[slot, h, :chunk], w_out_two[slot, h, chunk:]], axis=1)
+            for h in range(2)
+        ],
+        axis=0,
+    )
     u = nn(rows_a[...], w_in)
     square = u * u
     t = jnp.tanh(GELU_A * u * (1.0 + GELU_B * square))
     half = 0.5 * (1.0 + t)
     z = (u * half).astype(BF16)
     eo_sum[...] += nn(z, w_out)
-    dw_out = tn(z, d).astype(BF16)
-    dw_ref[0, 1, :chunk] = dw_out[:, :chunk]
-    dw_ref[0, 1, chunk:] = dw_out[:, chunk:]
+    dw_last = tn(z, d).astype(BF16)
     slope = half + (0.5 * GELU_A) * u * (1.0 - t * t) * (1.0 + 3.0 * GELU_B * square)
     du = (nt(d, w_out) * slope).astype(BF16)
     da_sum[...] += nt(du, w_in)
-    dw_ref[0, 0] = nn(turned_a[...], du).astype(BF16)
+    dw_first = nn(turned_a[...], du).astype(BF16)
+    for h in range(2):
+        here = slice(h * chunk, (h + 1) * chunk)
+        dw_two[slot, h, 0] = dw_first[:, here]
+        dw_two[slot, h, 1, :chunk] = dw_last[here, :chunk]
+        dw_two[slot, h, 1, chunk:] = dw_last[here, chunk:]
+    saved(step).start()
+
+    @pl.when(lax.rem(ahead, steps) == 0)
+    def _():
+        eo_ref[0] = eo_sum[...].astype(BF16)
+        da_ref[0] = da_sum[...].astype(BF16)
+
+    @pl.when(ahead == 3 * steps)
+    def _():
+        gather_b[2]()
+        gather_b[3]()
+        each_turn(ahead, lambda copy: copy.start())
 
     @pl.when(step == last)
     def _():
-        eo_ref[...] = eo_sum[...].astype(BF16)
-        da_ref[...] = da_sum[...].astype(BF16)
-        for action in at_end:
-            action()
+        saved(step - 1).wait()
+        saved(step).wait()
+        reduce_c[3]()
+        reduce_c[4]()
+        keep.start()
+        hop.wait()
+        keep.wait()
+
+
+def send_rows(step, value, stage, target, sends, recvs, keep, group):
+    place = lax.axis_index("expert")
+    for p in range(group):
+        @pl.when(step == p)
+        def _(p=p):
+            stage[p] = value
+
+            @pl.when(place == p)
+            def _():
+                pltpu.make_async_copy(stage.at[p], target.at[p], keep.at[0]).start()
+
+            @pl.when(place != p)
+            def _():
+                along_axis(stage.at[p], target.at[place], sends.at[p], recvs.at[place], p).start()
+
+
+def end_rows(stage, target, sends, recvs, keep, group):
+    place = lax.axis_index("expert")
+    for k in range(1, group):
+        other = lax.rem(place + k, group)
+        along_axis(stage.at[other], target.at[other], sends.at[other], recvs.at[other], other).wait_recv()
+    for k in range(1, group):
+        other = lax.rem(place + k, group)
+        along_axis(stage.at[other], target.at[place], sends.at[other], recvs.at[place], other).wait_send()
+    pltpu.make_async_copy(stage.at[place], target.at[place], keep.at[0]).wait()
 
 
 def combine_kernel(
-    h_ref, a_ref, g_ref, o_ref, gate_ref, pr_ref, pos_ref, eo0, eo1, eo2, eo3,
-    da0, da1, da2, da3, second_ref, params_ref,
-    out_ref, dh_ref, do_ref, dw_ref, dgain_ref, drouter_ref, *, share, experts, capacity
+    h_ref, a_ref, g_ref, o_ref, gate_ref, pr_ref, pos_ref, eo_ref, back_ref, second_ref, params_ref, terms, passed,
+    out_all, dh_ref, do_ref, dw_ref, dgain_ref, drouter_ref, sums_ref,
+    stage, landed, p_send, p_recv, sends, recvs, keep, own, pair, inbox, send, recv, local,
+    *, share, experts, capacity, group
 ):
     step = pl.program_id(0)
+    last = pl.num_programs(0) - 1
+    place = lax.axis_index("expert")
+
+    def emit(half, value):
+        sums_ref[half] = (value + landed[half].astype(F32)).astype(BF16)
+
+    start, far, near, late, finish = reduce_copies(terms.at[3], own, pair, inbox, send, recv, local, emit)
+    hop = along_axis(passed, landed, p_send.at[0], p_recv.at[0], partner(place, 1))
+
+    @pl.when(step == 0)
+    def _():
+        meet(plane_devices() + place_devices(group))
+        start()
+        hop.start()
+        far()
+
+    @pl.when(step == 1)
+    def _():
+        near()
+
+    @pl.when(step == 3)
+    def _():
+        late()
 
     @pl.when(step == 0)
     def _():
@@ -1095,13 +1229,13 @@
     result = h1
     dgate = jnp.zeros_like(pr)
     da = jnp.zeros_like(h1)
-    for k, (eo, back) in enumerate(((eo0, da0), (eo1, da1), (eo2, da2), (eo3, da3))):
+    for k in range(experts):
         spot = (pos_ref[:, k : k + 1] == slot).astype(BF16)
-        got = nn(spot, eo[...])
+        got = nn(spot, eo_ref[k])
         result = result + gates[:, k : k + 1] * got
         dgate = jnp.where(lane == k, jnp.sum(g * got, axis=-1, keepdims=True), dgate)
-        da = da + nn(spot, back[...])
-    out_ref[...] = result.astype(BF16)
+        da = da + nn(spot, back_ref[k])
+    send_rows(step, result.astype(BF16), stage, out_all, sends, recvs, keep, group)
     named = (pos_ref[...] >= 0) & (lane < experts)
     denom = jnp.sum(jnp.where(named, pr, 0.0), axis=-1, keepdims=True)
     weighted = jnp.sum(dgate * gates, axis=-1, keepdims=True)
@@ -1123,86 +1257,53 @@
     do_ref[...] = nt(dy, weight(second_ref, 1, share)).astype(BF16)
     dw_ref[...] += tn(o_ref[...], dy)
 
+    @pl.when(step == last)
+    def _():
+        hop.wait()
+        finish()
+        end_rows(stage, out_all, sends, recvs, keep, group)
+
 
 def close_kernel(
-    x_ref, a_ref, dq_ref, dk_ref, dv_ref, dh_ref, first_ref, second_ref, params_ref, dwo_ref, dgain_m_ref, drouter_ref,
-    dist_ref, buckets_ref, sum0, sum1, sum2, sum3,
+    x_ref, dq_ref, dk_ref, dv_ref, dh_ref, first_ref, second_ref, params_ref, dwq_ref, dwk_ref, dwv_ref, dwo_ref,
+    dgain_m_ref, drouter_ref, dist_ref, buckets_ref, sum0, sum1, sum2,
     din_out, gather_first, gather_second, dense_ref,
-    sum_ref, dgain, stage, total, pack, own, pair, inbox, r_send, r_recv, r_local, sends, recvs, keep,
+    stage, total, pack, own, pair, inbox, r_send, r_recv, r_local, sends, recvs, keep,
     z_in, z_total, z_final, z_send, z_recv, g_send, g_recv, g_local, *, share, group, experts
 ):
     step = pl.program_id(0)
     last = pl.num_programs(0) - 1
-    me = lax.axis_index("dp")
     place = lax.axis_index("expert")
     start0, start1, start2, finish = gather_copies(
         gather_first, gather_second, total.at[0], total.at[1], g_send, g_recv, g_local
     )
-    tile = a_ref.shape[0]
-
-    def din_copy(p):
-        return along_axis(stage.at[p], din_out.at[place], sends.at[p], recvs.at[place], p)
-
-    def din_keep(p):
-        return pltpu.make_async_copy(stage.at[p], din_out.at[p], keep.at[0])
+    quarter = pack.shape[2] // 2
+
+    def emit(half, value):
+        low = value.astype(BF16)
+        z_total[2 * half] = low[:quarter]
+        z_total[2 * half + 1] = low[quarter:]
+
+    start, far, near, late, end_reduce = reduce_copies(pack, own, pair, inbox, r_send, r_recv, r_local, emit)
 
     @pl.when(step == 0)
     def _():
-        for half in range(2):
-            value = sum0[half].astype(F32) + sum1[half].astype(F32)
-            total[half] = (value + sum2[half].astype(F32) + sum3[half].astype(F32)).astype(BF16)
-        meet(plane_devices() + place_devices(group))
-        start0()
-        sum_ref[...] = jnp.zeros_like(sum_ref)
-        dgain[...] = jnp.zeros_like(dgain)
-
-    a = a_ref[...]
-    da = jnp.zeros(dh_ref.shape, F32)
-    places = ((first_ref, 0), (first_ref, 1), (second_ref, 0))
-    for index, grad_ref in enumerate((dq_ref, dk_ref, dv_ref)):
-        grad = grad_ref[...]
-        sum_ref[index] += tn(a, grad)
-        slots_ref, at = places[index]
-        da = da + nt(grad, weight(slots_ref, at, share))
-    x = x_ref[...].astype(F32)
-    inverse = lax.rsqrt(jnp.mean(x * x, axis=-1, keepdims=True) + EPSILON)
-    n1 = x * inverse
-    dgain[...] += jnp.sum(da * n1, axis=0, keepdims=True)
-    dn = da * params_ref[0:1, :]
-    din = dh_ref[...] + inverse * (dn - n1 * jnp.mean(dn * n1, axis=-1, keepdims=True))
-    for p in range(group):
-        @pl.when(step == p)
-        def _(p=p):
-            stage[p] = din.astype(BF16)
-
-            @pl.when(place == p)
-            def _():
-                din_keep(p).start()
-
-            @pl.when(place != p)
-            def _():
-                din_copy(p).start()
-
-    @pl.when(step == last)
-    def _():
-        start1()
-        for index in range(2):
-            pack[:, 0, index * share : (index + 1) * share, :] = sum_ref[index].astype(BF16).reshape(-1, share, D)
-        pack[:, 1, :share, :] = sum_ref[2].astype(BF16).reshape(-1, share, D)
-        pack[:, 1, share : 2 * share, :] = dwo_ref[...].astype(BF16).reshape(-1, share, D)
-        seq = dist_ref.shape[1]
+        places = ((0, 0, dwq_ref), (0, share, dwk_ref), (1, 0, dwv_ref), (1, share, dwo_ref))
+        for half, at, grad_ref in places:
+            pack[:, half, at : at + share, :] = grad_ref[...].astype(BF16).reshape(-1, share, D)
+        seq = dist_ref.shape[2]
         hot = (lax.broadcasted_iota(jnp.int32, (128, seq), 0) == buckets_ref[...]).astype(F32).astype(BF16)
-        left = dist_ref[...]
+        left = jnp.concatenate([dist_ref[h] for h in range(dist_ref.shape[0])], axis=0)
         table = jnp.zeros((left.shape[0], 128), F32)
         for _ in range(3):
-            part = left.astype(BF16)
-            left = left - part.astype(F32)
-            table = table + nt(part, hot)
-        rows_out = [dgain[...], dgain_m_ref[...], jnp.zeros((6, D), F32)]
+            low = left.astype(BF16)
+            left = left - low.astype(F32)
+            table = table + nt(low, hot)
+        rows_out = [jnp.zeros((1, D), F32), dgain_m_ref[...], jnp.zeros((6, D), F32)]
         for e in range(experts):
             picked = jnp.zeros((1, D), F32)
             for k in range(experts):
-                picked = picked + drouter_ref[k : k + 1, :] * jnp.where(lax.rem(place + k, experts) == e, 1.0, 0.0)
+                picked = picked + drouter_ref[k : k + 1, :] * jnp.where(partner(place, ORDER[k]) == e, 1.0, 0.0)
             rows_out.append(picked)
         rows_out.append(jnp.zeros((8 - experts, D), F32))
         rows_out.append(jnp.concatenate([table, jnp.zeros((table.shape[0], D - 128), F32)], axis=1))
@@ -1211,19 +1312,36 @@
         for slot in range(pack.shape[0]):
             pack[slot, 0, 2 * share :, :] = small
             pack[slot, 1, 2 * share :, :] = jnp.zeros_like(small)
-        quarter = pack.shape[2] // 2
-
-        def emit(half, value):
-            low = value.astype(BF16)
-            z_total[2 * half] = low[:quarter]
-            z_total[2 * half + 1] = low[quarter:]
-
-        start, far, near, late, end_reduce = reduce_copies(pack, own, pair, inbox, r_send, r_recv, r_local, emit)
+        meet(plane_devices() + place_devices(group))
         start()
         far()
         near()
-        start2()
+        for half in range(2):
+            value = sum0[half].astype(F32) + sum1[half].astype(F32)
+            total[half] = (value + sum2[half].astype(F32)).astype(BF16)
+
+    @pl.when(step == 1)
+    def _():
+        start0()
+
+    @pl.when(step == 2)
+    def _():
         late()
+
+    da = jnp.zeros(dh_ref.shape, F32)
+    places = ((first_ref, 0), (first_ref, 1), (second_ref, 0))
+    for index, grad_ref in enumerate((dq_ref, dk_ref, dv_ref)):
+        slots_ref, at = places[index]
+        da = da + nt(grad_ref[...], weight(slots_ref, at, share))
+    x = x_ref[...].astype(F32)
+    inverse = lax.rsqrt(jnp.mean(x * x, axis=-1, keepdims=True) + EPSILON)
+    n1 = x * inverse
+    dn = da * params_ref[0:1, :]
+    din = dh_ref[...] + inverse * (dn - n1 * jnp.mean(dn * n1, axis=-1, keepdims=True))
+    send_rows(step, din.astype(BF16), stage, din_out, sends, recvs, keep, group)
+
+    @pl.when(step == last)
+    def _():
         end_reduce()
         spread = [
             along_axis(z_total.at[lax.rem(place + k, group)], z_in.at[k - 1], z_send.at[k], z_recv.at[k],
@@ -1232,6 +1350,7 @@
         ]
         for copy in spread:
             copy.start()
+        start1()
         for copy in spread:
             copy.wait_recv()
         value = z_total[place].astype(F32)
@@ -1245,26 +1364,37 @@
         ]
         for copy in share_out:
             copy.start()
+        start2()
         for copy in share_out:
             copy.wait_recv()
         for copy in spread + share_out:
             copy.wait_send()
         dense_ref[...] = z_final[...]
-        for k in range(1, group):
-            other = lax.rem(place + k, group)
-            along_axis(stage.at[other], din_out.at[other], sends.at[other], recvs.at[other], other).wait_recv()
-        for k in range(1, group):
-            other = lax.rem(place + k, group)
-            along_axis(stage.at[other], din_out.at[place], sends.at[other], recvs.at[place], other).wait_send()
-        pltpu.make_async_copy(stage.at[place], din_out.at[place], keep.at[0]).wait()
+        end_rows(stage, din_out, sends, recvs, keep, group)
         finish()
 
 
-def unpack_kernel(first_ref, second_ref, in_ref, out_ref):
+def unpack_kernel(
+    first_ref, second_ref, din_ref, dense_ref, wq_ref, wk_ref, wv_ref, gain_ref,
+    in_ref, out_ref, grad_ref, dq_ref, dk_ref, dv_ref, do_ref, gain_out, small_ref, *, share
+):
     chunk = first_ref.shape[2]
     in_ref[0] = first_ref[0].astype(F32)
     out_ref[0, :, :chunk] = second_ref[0, :chunk].astype(F32)
     out_ref[0, :, chunk:] = second_ref[0, chunk:].astype(F32)
+    grad_ref[...] = din_ref[...].astype(F32)
+
+    @pl.when(pl.program_id(0) == 0)
+    def _():
+        grads = []
+        for grad, half, at in ((dq_ref, 0, 0), (dk_ref, 0, share), (dv_ref, 1, 0), (do_ref, 1, share)):
+            value = dense_ref[half, at : at + share, :].astype(F32)
+            grad[...] = value
+            grads.append(value)
+        moved = grads[0] * wq_ref[...].astype(F32) + grads[1] * wk_ref[...].astype(F32)
+        moved = moved + grads[2] * wv_ref[...].astype(F32)
+        gain_out[...] = jnp.sum(moved, axis=-1, keepdims=True) / gain_ref[...].astype(F32)
+        small_ref[...] = dense_ref[0, 2 * share :, :].astype(F32)
 
 
 def on_device_whole(
@@ -1299,145 +1429,113 @@
     routes_in = jnp.pad(routes.transpose(0, 2, 1), ((0, 0), (0, 6), (0, 0)))
     bucket_row = buckets.reshape(1, seq)
     second_rows = 2 * share + 32
-    x, moved, first, second, normed, q, k, v, params, lines, across, down = call(
-        functools.partial(open_kernel, group=group, share=share, heads=heads, experts=experts, scale=scale),
-        "open", (1,),
-        [ANY] * 8 + [vmem] * 3,
-        [ANY] * 4 + [vmem] * 8,
-        [sds((group, part, D), BF16), sds(piece, BF16), sds((shards, 2 * share, D), BF16),
-         sds((shards, second_rows, D), BF16)] + [sds(tokens, BF16)] * 4
-        + [sds((32, D), F32), sds((heads, 1, seq), F32), sds((16, seq), jnp.int32), sds((seq, 128), jnp.int32)],
+    tok16, tok32, wide32 = sds(tokens, BF16), sds(tokens, F32), sds((seq, 128), F32)
+    block = sds((group, part, D), BF16)
+    table_shape = (heads, blocks, TILE, TILE)
+    v16, v32 = pltpu.VMEM(tokens, BF16), pltpu.VMEM(tokens, F32)
+    (x, g, far_first, far_second, first, second, normed, q, k, v, o, table, h1, normed_m, gates, pr, near_first,
+     near_second, _, params, across, down, lse) = call(
+        functools.partial(
+            front_kernel, group=group, share=share, heads=heads, experts=experts, scale=scale, width=width),
+        "front", (1,),
+        [ANY] * 9 + [vmem] * 3,
+        [ANY] * 19 + [vmem] * 4,
+        [block, block, sds((D, chunk), BF16), sds((D, chunk), BF16), sds((shards, 2 * share, D), BF16),
+         sds((shards, second_rows, D), BF16)] + [tok16] * 5
+        + [sds(table_shape, BF16), tok32, tok16, wide32, wide32, buffer, buffer, sds(piece, BF16),
+           sds((32, D), F32), sds((16, seq), jnp.int32), sds((seq, 128), jnp.int32),
+           sds((heads // pairs, pairs, seq), F32)],
         [pltpu.VMEM((group, part, D), BF16), pltpu.VMEM((group, 8, part), jnp.int32),
          pltpu.VMEM((shards, 2 * share, D), BF16), pltpu.VMEM((shards, second_rows, D), BF16),
-         pltpu.VMEM((2 * share, D), BF16), pltpu.VMEM((second_rows, D), BF16)]
-        + [dma((group,))] * 4 + [dma((3,))] * 2 + [dma((2,)), dma((4,))] + gather_sems(), collective=1,
-    )(layer_in, routes_in, w_expert_in, w_expert_out, w_query, w_key, w_value, w_output, small, bucket_row, segments)
+         pltpu.VMEM((2 * share, D), BF16), pltpu.VMEM((second_rows, D), BF16)] + [v16] * 5
+        + [pltpu.VMEM(table_shape, BF16), v32, v16, pltpu.VMEM((seq, 128), F32), pltpu.VMEM((seq, 128), F32),
+           pltpu.VMEM((heads, 1, seq), F32)]
+        + [dma((group,))] * 6 + [dma((6,))] * 2 + [dma((3 + heads // pairs,)), dma((4,)), dma((12,))]
+        + gather_sems() * 2, collective=1, flops=6 * seq * D * D,
+    )(layer_in, out_grad, routes_in, w_expert_in, w_expert_out, w_query, w_key, w_value, w_output, small, bucket_row,
+      segments)
     x = x.reshape(tokens)
-
+    g = g.reshape(tokens)
+    buffers = [near_first, near_second]
     cols = pl.BlockSpec((seq, 128), lambda i: (0, i))
     table_spec = pl.BlockSpec((pairs, blocks, TILE, TILE), lambda i: (i, 0, 0, 0))
     lse_spec = pl.BlockSpec((1, pairs, seq), lambda i: (i, 0, 0))
-    o, lse, table, g, moved3, *buffers = call(
-        functools.partial(attend_kernel, width=width, group=group), "attend", (heads // pairs,),
-        [cols, cols, cols, pl.BlockSpec((pairs, 1, seq), lambda i: (i, 0, 0)), whole((seq, 128)), whole((16, seq))]
-        + [ANY] * 4,
-        [cols, lse_spec, table_spec] + [ANY] * 4,
-        [sds(tokens, BF16), sds((heads // pairs, pairs, seq), F32), sds((heads, blocks, TILE, TILE), BF16),
-         sds((group, part, D), BF16), sds(piece, BF16), buffer, buffer],
-        [dma((group,))] * 2 + [dma((3,))] * 2 + [dma((1,))] + gather_sems(),
-        flops=8 * seq * seq * D, nbytes=16 * 2**20, collective=2,
-    )(q, k, v, lines, down, across, moved, out_grad, w_expert_in, w_expert_out)
-    g = g.reshape(tokens)
-    h1, normed_m, gates, pr = call(
-        functools.partial(route_kernel, share=share, experts=experts), "route", (blocks,),
-        [rows(D), rows(D), whole(second.shape), whole((32, D)), rows(128)],
-        [rows(D), rows(D), rows(128), rows(128)],
-        [sds(tokens, F32), sds(tokens, BF16), sds((seq, 128), F32), sds((seq, 128), F32)],
-        flops=2 * seq * D * D, nbytes=12 * 2**20,
-    )(x, o, second, params, down)
-
-    def run_expert(index, buffers, collective, fetch=None, relay=None, reduce=None, pass_on=None, hop=0):
-        in_block, out_block = (1, D, chunk), (1, D, chunk)
-        in_map = out_map = lambda i: (i, 0, 0)
-        if index == 0:
-            buffers = (w_expert_in, w_expert_out)
-            out_block = (1, chunk, D)
-            in_map, out_map = (lambda i: (0, 0, i)), (lambda i: (0, i, 0))
-        extra_in, extra_out, shapes, scratch = [], [], [], []
-        if fetch is not None:
-            extra_in.append(fetch)
-            extra_out += [ANY] * 2
-            shapes += [buffer] * 2
-            scratch += gather_sems()
-        if relay is not None:
-            extra_in += relay
-            extra_out.append(ANY)
-            shapes.append(sds(piece, BF16))
-            scratch += [dma((2,)), dma((1,))]
-        if reduce is not None:
-            extra_in.append(reduce)
-            extra_out.append(whole(piece))
-            shapes.append(sds(piece, BF16))
-            scratch += reduce_scratch(piece)
-        if pass_on is not None:
-            extra_in.append(pass_on)
-            extra_out.append(ANY)
-            shapes.append(sds(piece, BF16))
-            scratch += [dma((1,)), dma((1,))]
-        return call(
-            functools.partial(
-                expert_kernel, index=index, capacity=capacity, fetch=fetch is not None, relay=relay is not None,
-                reduce=reduce is not None, pass_on=hop, group=group),
-            f"expert{index}", (shards,),
-            [whole(tokens), whole(tokens), whole((seq, 128)), whole((16, seq)),
-             pl.BlockSpec(in_block, in_map), pl.BlockSpec(out_block, out_map)] + [ANY] * len(extra_in),
-            [whole(slots), whole(slots), pl.BlockSpec((1, 2, D, chunk), lambda i: (i, 0, 0, 0))] + extra_out,
-            [sds(slots, BF16), sds(slots, BF16), sds((shards, *piece), BF16)] + shapes,
-            [pltpu.VMEM(slots, BF16), pltpu.VMEM((D, capacity), BF16), pltpu.VMEM(slots, BF16),
-             pltpu.VMEM(slots, F32), pltpu.VMEM(slots, F32)] + scratch,
-            flops=12 * capacity * D * ff, nbytes=24 * 2**20, collective=collective if extra_in else None,
-        )(normed_m, g, gates, across, *buffers, *extra_in)
-
-    eo1, da1, dw1, *rest = run_expert(1, buffers, 3, fetch=moved3, relay=[moved, moved3])
-    buffers, moved2 = rest[:2], rest[2]
-    eo3, da3, dw3, *rest = run_expert(3, buffers, 4, fetch=moved2, reduce=dw1)
-    buffers, sum1 = rest[:2], rest[2]
-    eo2, da2, dw2, sum3, sum1 = run_expert(2, buffers, 5, reduce=dw3, pass_on=sum1, hop=1)
-    eo0, da0, dw0, sum2, sum3 = run_expert(0, None, 6, reduce=dw2, pass_on=sum3, hop=3)
-    sum2 = lax.ppermute(sum2, "expert", [(s, (s + 2) % group) for s in range(group)])
-    result, dh, do, grad_output, grad_gain_m, grad_router = call(
-        functools.partial(combine_kernel, share=share, experts=experts, capacity=capacity), "combine",
+
+    once = lambda shape: pl.BlockSpec(shape, lambda *_: (0,) * len(shape), pipeline_mode=pl.Buffered(1))
+    turned = pl.BlockSpec((1, *slots), lambda i: (i // (shards // 2), 0, 0))
+    eo, da, dw, sum1, sum3, _, _, _, _, _ = call(
+        functools.partial(experts_kernel, capacity=capacity, group=group, shards=shards), "experts",
+        (experts * shards // 2,),
+        [once(tokens), once(tokens), once((seq, 128)), once((16, seq))] + [ANY] * 6,
+        [turned, turned] + [ANY] * 8,
+        [sds((experts, *slots), BF16)] * 2 + [sds((experts, shards, *piece), BF16)] + [sds(piece, BF16)] * 3
+        + [buffer] * 4,
+        [pltpu.VMEM(slots, BF16), pltpu.VMEM((D, capacity), BF16), pltpu.VMEM(slots, BF16),
+         pltpu.VMEM(slots, F32), pltpu.VMEM(slots, F32), pltpu.VMEM((2, 2, D, chunk), BF16),
+         pltpu.VMEM((2, 2, D, chunk), BF16), pltpu.VMEM((2, 2, *piece), BF16), pltpu.VMEM(piece, BF16),
+         dma((6, 2)), dma((2,)), dma((3,)), dma((3,)), dma((1,)), pltpu.SemaphoreType.REGULAR]
+        + reduce_scratch(piece) + reduce_scratch(piece)[3:] + gather_sems() * 2,
+        flops=48 * capacity * D * ff, nbytes=96 * 2**20, collective=3,
+    )(normed_m, g, gates, across, *buffers, far_first, far_second, w_expert_in, w_expert_out)
+    layer_out, dh, do, grad_output, grad_gain_m, grad_router, sum2 = call(
+        functools.partial(combine_kernel, share=share, experts=experts, capacity=capacity, group=group), "combine",
         (blocks,),
-        [rows(D)] * 4 + [rows(128)] * 3 + [whole(slots)] * 8 + [whole(second.shape), whole((32, D))],
-        [rows(D), rows(D), rows(D), whole((D, D)), whole((1, D)), whole((8, D))],
-        [sds(tokens, BF16), sds(tokens, F32), sds(tokens, BF16), sds((D, D), F32), sds((1, D), F32),
-         sds((8, D), F32)],
-        flops=24 * seq * D * D, nbytes=32 * 2**20,
-    )(h1, normed_m, g, o, gates, pr, down, eo0, eo1, eo2, eo3, da0, da1, da2, da3, second, params)
-    dq, dk, dv, dist, sum0, layer_out = call(
+        [rows(D)] * 4 + [rows(128)] * 3 + [once((experts, *slots))] * 2 + [once(second.shape), whole((32, D)), ANY, ANY],
+        [ANY, rows(D), rows(D), whole((D, D)), whole((1, D)), whole((8, D)), whole(piece)],
+        [sds((group, part, D), BF16), sds(tokens, F32), sds(tokens, BF16), sds((D, D), F32), sds((1, D), F32),
+         sds((8, D), F32), sds(piece, BF16)],
+        [pltpu.VMEM((group, part, D), BF16), pltpu.VMEM(piece, BF16), dma((1,)), dma((1,)), dma((group,)),
+         dma((group,)), dma((1,))] + reduce_scratch(piece),
+        flops=24 * seq * D * D, nbytes=32 * 2**20, collective=7,
+    )(h1, normed_m, g, o, gates, pr, down, eo, da, second, params, dw, sum3)
+    dist_spec = pl.BlockSpec((pairs, 1, seq), lambda i: (i, 0, 0))
+    dq, dk, dv, dist, grad_query, grad_key, grad_value, sum0, sum2 = call(
         functools.partial(attend_back_kernel, width=width, scale=scale, group=group), "attend_back",
         (heads // pairs,),
-        [cols, cols, cols, cols, table_spec, whole((seq, 128)), whole((16, seq)), lse_spec, ANY, ANY],
-        [cols, cols, cols, lse_spec, whole(piece), ANY],
-        [sds(tokens, BF16)] * 3 + [sds((heads // pairs, pairs, seq), F32), sds(piece, BF16),
-                                   sds((group, part, D), BF16)],
-        [pltpu.VMEM((blocks, TILE, TILE), F32), pltpu.VMEM((seq, 128), F32), pltpu.VMEM((seq, 128), F32)]
-        + [dma((group,))] * 2 + [dma((1,))] + reduce_scratch(piece),
-        flops=20 * seq * seq * D, nbytes=24 * 2**20, collective=7,
-    )(q, k, v, do, table, down, across, lse, result.reshape(group, part, D), dw0)
+        [cols, cols, cols, cols, table_spec, whole((seq, 128)), whole((16, seq)), lse_spec, whole(tokens), ANY, ANY],
+        [cols, cols, cols, dist_spec] + [pl.BlockSpec((D, 128), lambda i: (0, i))] * 3 + [whole(piece), ANY],
+        [sds(tokens, BF16)] * 3 + [sds((heads, 1, seq), F32)] + [sds((D, D), BF16)] * 3
+        + [sds(piece, BF16), sds(piece, BF16)],
+        [pltpu.VMEM((blocks, TILE, TILE), F32), pltpu.VMEM((seq, 128), F32), pltpu.VMEM((seq, 128), F32),
+         pltpu.VMEM((D, seq), BF16)]
+        + [dma((1,))] * 2 + reduce_scratch(piece),
+        flops=20 * seq * seq * D, nbytes=24 * 2**20, collective=8,
+    )(q, k, v, do, table, down, across, lse, normed, sum2, dw)
     dense_slot = (2, 2 * share + 32, D)
     quarter = (dense_slot[1] // 2, D)
     grad_in, *gathered, dense = call(
         functools.partial(close_kernel, share=share, group=group, experts=experts), "close", (blocks,),
-        [rows(D)] * 6 + [whole(first.shape), whole(second.shape), whole((32, D)), whole((D, D)), whole((1, D)),
-                         whole((8, D)), whole((heads, seq)), whole((1, seq))] + [whole(piece)] * 4,
+        [rows(D)] * 5 + [whole(first.shape), whole(second.shape), whole((32, D))] + [whole((D, D))] * 4
+        + [whole((1, D)), whole((8, D)), whole((heads, 1, seq)), whole((1, seq))] + [whole(piece)] * 3,
         [ANY, ANY, ANY, whole((group, *quarter))],
         [sds((group, part, D), BF16), buffer, buffer, sds((group, *quarter), BF16)],
-        [pltpu.VMEM((3, D, D), F32), pltpu.VMEM((1, D), F32), pltpu.VMEM((group, part, D), BF16),
-         pltpu.VMEM(piece, BF16), pltpu.VMEM((shards, *dense_slot), BF16)] + reduce_scratch(dense_slot)
+        [pltpu.VMEM((group, part, D), BF16), pltpu.VMEM(piece, BF16), pltpu.VMEM((shards, *dense_slot), BF16)]
+        + reduce_scratch(dense_slot)
         + [dma((group,)), dma((group,)), dma((1,)), pltpu.VMEM((group - 1, *quarter), BF16),
-           pltpu.VMEM((group, *quarter), BF16), pltpu.VMEM((group, *quarter), BF16), dma((2 * group,)), dma((2 * group,))] + gather_sems(),
-        flops=12 * seq * D * D, nbytes=24 * 2**20, collective=8,
-    )(x, normed, dq, dk, dv, dh, first, second, params, grad_output, grad_gain_m, grad_router,
-      dist.reshape(heads, seq), bucket_row, sum0, sum1, sum2, sum3)
+           pltpu.VMEM((group, *quarter), BF16), pltpu.VMEM((group, *quarter), BF16), dma((2 * group,)),
+           dma((2 * group,))] + gather_sems(),
+        flops=12 * seq * D * D, nbytes=24 * 2**20, collective=9,
+    )(x, dq, dk, dv, dh, first, second, params, grad_query, grad_key, grad_value, grad_output, grad_gain_m, grad_router,
+      dist, bucket_row, sum0, sum1, sum2)
     spec = pl.BlockSpec((1, D, chunk), lambda i: (i, 0, 0))
-    expert_in, expert_out = call(
-        unpack_kernel, "unpack", (shards,), [spec, spec],
-        [pl.BlockSpec((1, D, chunk), lambda i: (0, 0, i)), pl.BlockSpec((1, chunk, D), lambda i: (0, i, 0))],
-        [sds(w_expert_in.shape, F32), sds(w_expert_out.shape, F32)], nbytes=28 * 2**20,
-    )(*gathered)
-    dense = dense.reshape(dense_slot).astype(F32)
-    rest = dense[0, 2 * share :]
-    line = lax.dynamic_slice_in_dim(rest[:16], shard * share, share, axis=1)
-    grad_table = lax.dynamic_slice_in_dim(rest[16 : 16 + heads], shard * rel_bias.shape[0], rel_bias.shape[0], axis=1)
+    line_rows = pl.BlockSpec((seq // shards, D), lambda i: (i, 0))
+    expert_in, expert_out, grad_in, *dense_grads, grad_gain, smalls = call(
+        functools.partial(unpack_kernel, share=share), "unpack", (shards,),
+        [spec, spec, line_rows, whole(dense_slot)] + [whole((share, D))] * 3 + [whole((share, 1))],
+        [pl.BlockSpec((1, D, chunk), lambda i: (0, 0, i)), pl.BlockSpec((1, chunk, D), lambda i: (0, i, 0)), line_rows]
+        + [whole((share, D))] * 4 + [whole((share, 1)), whole((32, D))],
+        [sds(w_expert_in.shape, F32), sds(w_expert_out.shape, F32), sds(tokens, F32)]
+        + [sds((share, D), F32)] * 4 + [sds((share, 1), F32), sds((32, D), F32)],
+        nbytes=34 * 2**20,
+    )(*gathered, grad_in.reshape(tokens), dense.reshape(dense_slot), w_query, w_key, w_value,
+      gain_attn.reshape(share, 1))
+    line = lax.dynamic_slice_in_dim(smalls[:16], shard * share, share, axis=1)
+    grad_table = lax.dynamic_slice_in_dim(smalls[16 : 16 + heads], shard * rel_bias.shape[0], rel_bias.shape[0], axis=1)
     return (
         layer_out,
-        grad_in.astype(F32),
-        line[0],
-        dense[0, :share],
-        dense[0, share : 2 * share],
-        dense[1, :share],
-        dense[1, share : 2 * share],
+        grad_in.reshape(group, part, D),
+        grad_gain.reshape(share),
+        *dense_grads,
         line[1],
         line[8 : 8 + experts].T,
         grad_table.T,

time: 613 us -> 580 us (0.946)
  Pallas kernels: 589 us -> 566 us
    pallas_call x8 -> x3, Pallas kernels: 402 us -> 343 us  [the longest x1 184 us: on_device_whole(): call(functools.partial(experts_kernel, capacity=capacity, group=group, sh...]
    pallas_call x1, Pallas kernels: 25.4 us -> 74.5 us  [on_device_whole(): call(functools.partial(combine_kernel, share=share, experts=experts, capa...]
    pallas_call x1, Pallas kernels: 108 us -> 89.8 us  [on_device_whole(): call(functools.partial(close_kernel, share=share, group=group, experts=ex...]
  transfers between devices with their start and end apart: 1 -> 0, of which waited for: 0 -> 0; matrix products, arithmetic and copies ran while one was open for 0% -> 0% of each run, Pallas kernels for 13% -> 0%
where the time goes in v3:
time: 580 us; the launch traced here: 578 us
  Pallas kernels  566 us (98%)
  local copies, waits for them, and re-layouts  7.54 us (1%)
    pallas_call x1, Pallas kernels, on_device_whole(): call(functools.partial(experts_kernel, capacity=capacity, group=group, sh...  184 us
    pallas_call x1, Pallas kernels, on_device_whole(): call(functools.partial(front_kernel, group=group, share=share, heads=head...  146 us
    pallas_call x1, Pallas kernels, on_device_whole(): call(functools.partial(close_kernel, share=share, group=group, experts=ex...  89.8 us
    pallas_call x1, Pallas kernels, on_device_whole(): call(functools.partial(combine_kernel, share=share, experts=experts, capa...  74.5 us
    pallas_call x1, Pallas kernels, on_device_whole(): call(functools.partial(attend_back_kernel, width=width, scale=scale, grou...  58.9 us
    pallas_call x1, Pallas kernels, on_device_whole(): call(functools.partial(unpack_kernel, share=share), 'unpack', (shards,),...  13.8 us

profile of v3, /device:TPU:0, one launch (start us, length us, event | category | flops | bytes accessed | tf_op | source)
XLA Modules:
  0.0 578.1 jit_solution(7498243711016677782)
XLA Ops:
  0.6 0.7 fusion.10
  1.3 0.8 copy.30
  2.1 1.3 fusion.4.small_ref
  3.4 1.3 pad.16.routes_ref
  4.7 145.5 %front.1 = (bf16[4,256,768]{2,1,0:T(8,128)(2,1)}, bf16[4,256,768]{2,1,0:T(8,128)(2,1)}, bf16[768,384]{1,0:T(8,128)(2,1)}, bf16[768,384]{1,0:T(8,128)(2,1)}, bf16...) custom-call(bf16[4,256,768]{2,1,0:T(8,128)(2,1)} %x_ref.1, ...), custom_call_target="tpu_custom_call" | custom-call | flops 3623878656 | tf_op jit(solution)/shard_map/front/pallas_call | solution.py:1437
  150.2 183.8 %experts.1 = (bf16[4,768,768]{2,1,0:T(8,128)(2,1)}, bf16[4,768,768]{2,1,0:T(8,128)(2,1)}, bf16[4,8,2,768,384]{4,3,2,1,0:T(8,128)(2,1)}, bf16[2,768,384]{2,1,0:T(...) custom-call(bf16[1024,768]{1,0:T(8,128)(2,1)} %get-tuple-element.69., ...), custom_call_target="tpu_custom_call" | custom-call | flops 86973087744 | bytes 100663296 | tf_op jit(solution)/shard_map/experts/pallas_call | solution.py:1466
  334.1 74.5 %combine.1 = (bf16[4,256,768]{2,1,0:T(8,128)(2,1)}, f32[1024,768]{1,0:T(8,128)}, bf16[1024,768]{1,0:T(8,128)(2,1)}, f32[768,768]{1,0:T(8,128)}, f32[1,768]{1,0:T...) custom-call(f32[1024,768]{1,0:T(8,128)} %get-tuple-element.68.h_ref, bf16[1024,768]{1,0:T(8,128)(2,1)} %get-tuple-element.69.a_ref, ...), custom_call_target="tpu_custom_call" | custom-call | flops 14495514624 | bytes 33554432 | tf_op jit(solution)/shard_map/combine/pallas_call | solution.py:1480
  408.5 58.9 %attend_back.1 = (bf16[1024,768]{1,0:T(8,128)(2,1)}, bf16[1024,768]{1,0:T(8,128)(2,1)}, bf16[1024,768]{1,0:T(8,128)(2,1)}, f32[12,1,1024]{2,1,0:T(1,128)}, bf16[...) custom-call(bf16[1024,768]{1,0:T(8,128)(2,1)} %get-tuple-element.88., ...), custom_call_target="tpu_custom_call" | custom-call | flops 16106127360 | bytes 25165824 | tf_op jit(solution)/shard_map/attend_back/pallas_call | solution.py:1492
  467.4 0.0 copy-start.1
  467.4 89.8 %close.1 = (bf16[4,256,768]{2,1,0:T(8,128)(2,1)}, bf16[8,768,384]{2,1,0:T(8,128)(2,1)}, bf16[8,768,384]{2,1,0:T(8,128)(2,1)}, bf16[4,112,768]{2,1,0:T(8,128)(2,1)}) custom-call(bf16[1024,768]{1,0:T(8,128)(2,1)} %bitcast.31, bf16[1024,768]{1,0:T(8,128)(2,1)} %get-tuple-element.96.dq_ref, bf16[1024,768]{1,0:T(8,128)(2,1)} %get-tuple-element.97.dk_ref, ...), custom_call_target="tpu_custom_call" | custom-call | flops 7247757312 | bytes 25165824 | tf_op jit(solution)/shard_map/close/pallas_call | solution.py:1506
  557.2 0.0 copy-done.1
  557.2 0.7 copy.31.gain_ref
  558.0 0.0 copy-start
  558.0 13.8 %unpack.1 = (f32[1,768,3072]{2,1,0:T(8,128)}, f32[1,3072,768]{2,1,0:T(8,128)}, f32[1024,768]{1,0:T(8,128)}, f32[96,768]{1,0:T(8,128)}, f32[96,768]{1,0:T(8,128)}...) custom-call(bf16[8,768,384]{2,1,0:T(8,128)(2,1)} %get-tuple-element.111.first_ref, ...), custom_call_target="tpu_custom_call" | custom-call | bytes 35651584 | tf_op jit(solution)/shard_map/unpack/pallas_call | solution.py:1522
  571.7 0.8 slice.15
  572.5 0.1 dynamic-slice_bitcast_fusion
  572.6 0.7 copy.32
  573.3 0.8 slice.12
  574.1 0.7 dynamic-slice_bitcast_fusion.1
  574.7 0.6 dynamic-slice_bitcast_fusion.2
  575.3 1.4 reduce
  576.7 0.0 copy-done
  576.7 1.1 copy.34
Async XLA Ops:
  467.4 89.8 %copy-start.1 = (bf16[96]{0:T(256)(128)(2,1)S(1)}, bf16[96]{0:T(256)(128)(2,1)}, u32[]{:S(2)}) copy-start(bf16[96]{0:T(256)(128)(2,1)} %param.20) | copy-start | bytes 580
  558.0 18.8 %copy-start = (bf16[4,256,768]{2,1,0:T(8,128)(2,1)S(1)}, bf16[4,256,768]{2,1,0:T(8,128)(2,1)}, u32[]{:S(2)}) copy-start(bf16[4,256,768]{2,1,0:T(8,128)(2,1)} %get-tuple-element.160) | copy-start | bytes 4718596

commit v4 on v3

--- a/solution.py
+++ b/solution.py
@@ -519,7 +519,7 @@
     return 2 * lax.rem(place // 2 + k // 2, 2) + lax.rem(lax.rem(place, 2) + k % 2, 2)
 
 
-ORDER = (1, 0, 3, 2)
+ORDER = (1, 0, 2, 3)
 
 
 def place_devices(group):
@@ -683,7 +683,7 @@
     moves_x = swap_copies(x_ref, land, x_send, x_recv, group)
     moves_g = swap_copies(grad_ref, grad_out, g_send, g_recv, group)
     slices = slice_copies(w_in_ref, w_out_ref, piece_out.at[0], piece_out.at[1], p_send, p_recv, 0, partner(place, 1))
-    distant = slice_copies(w_in_ref, w_out_ref, c0_out, c1_out, p_send, p_recv, 3, partner(place, 3))
+    distant = slice_copies(w_in_ref, w_out_ref, c0_out, c1_out, p_send, p_recv, 3, partner(place, 2))
     kept = [
         pltpu.make_async_copy(routes_ref.at[place], routes_land.at[place], keep.at[0]),
         pltpu.make_async_copy(x_ref.at[place], land.at[place], keep.at[1]),
@@ -751,7 +751,7 @@
     kept[1].wait()
     for copy in moves_x:
         copy.wait_recv()
-    for copy in slices + distant + moves_g:
+    for copy in slices + distant:
         copy.start()
     put(land, x_out)
     part = land.shape[1]
@@ -783,6 +783,8 @@
             for copy in slices:
                 copy.wait_recv()
             gather[0]()
+            for copy in moves_g:
+                copy.start()
 
         attend_pair(n, q_ref, k_ref, v_ref, line_ref, table_ref, down_ref, across_ref, o_ref, lse_ref, width)
         table_copy(n).start()
@@ -887,9 +889,10 @@
 
 
 def attend_back_kernel(
-    q_ref, k_ref, v_ref, do_ref, table_ref, down_ref, across_ref, lse_ref, a_ref, passed, terms,
-    dq_ref, dk_ref, dv_ref, dist_ref, dwq_ref, dwk_ref, dwv_ref, sums_ref, pass_out,
-    sum_ref, dk_sum, dv_sum, turned_a, p_send, p_recv, own, pair, inbox, send, recv, local, *, width, scale, group
+    q_ref, k_ref, v_ref, do_ref, table_ref, down_ref, across_ref, lse_ref, a_ref, dwo_ref, dgain_m_ref, drouter_ref, buckets_ref,
+    passed, terms,
+    dq_ref, dk_ref, dv_ref, pack, sums_ref, pass_out,
+    dist_ref, grads_ref, sum_ref, dk_sum, dv_sum, turned_a, p_send, p_recv, own, pair, inbox, send, recv, local, *, width, scale, group, share, experts
 ):
     step = pl.program_id(0)
     last = pl.num_programs(0) - 1
@@ -899,11 +902,11 @@
         sums_ref[half] = value.astype(BF16)
 
     start, far, near, late, finish = reduce_copies(terms.at[1], own, pair, inbox, send, recv, local, emit)
-    hop = along_axis(passed, pass_out, p_send.at[0], p_recv.at[0], partner(place, 2))
+    hop = along_axis(passed, pass_out, p_send.at[0], p_recv.at[0], partner(place, 3))
 
     @pl.when(step == 0)
     def _():
-        meet(plane_devices() + [(lax.axis_index("dp"), partner(place, 2))])
+        meet(plane_devices() + [(lax.axis_index("dp"), partner(place, 3))])
         start()
         hop.start()
         far()
@@ -917,7 +920,8 @@
     blocks = q_ref.shape[0] // TILE
     heads = q_ref.shape[1] // width
     turned = [k_ref[:, h * width : (h + 1) * width].T for h in range(heads)]
-    dist_ref[...] = jnp.zeros_like(dist_ref)
+    for h in range(heads):
+        dist_ref[step * heads + h] = jnp.zeros(dist_ref.shape[1:], F32)
     for h in range(heads):
         lanes = slice(h * width, (h + 1) * width)
         for i in range(blocks):
@@ -963,19 +967,45 @@
             while half:
                 part = part[:half] + pltpu.roll(part[half : 2 * half], 2 * TILE - half, 1)
                 half //= 2
-            dist_ref[h, :, gap * TILE : (gap + 1) * TILE] += part[:, :TILE]
+            dist_ref[step * heads + h, :, gap * TILE : (gap + 1) * TILE] += part[:, :TILE]
             if gap:
-                dist_ref[h, :, (gap - 1) * TILE : gap * TILE] += part[:, TILE:]
+                dist_ref[step * heads + h, :, (gap - 1) * TILE : gap * TILE] += part[:, TILE:]
     dk_ref[...] = dk_sum[...].astype(BF16)
     dv_ref[...] = dv_sum[...].astype(BF16)
 
     grads = jnp.concatenate([dq_ref[...], dk_ref[...], dv_ref[...]], axis=1)
     sums = nn(turned_a[...], grads).astype(BF16)
-    for index, dw_ref in enumerate((dwq_ref, dwk_ref, dwv_ref)):
-        dw_ref[...] = sums[:, index * 128 : (index + 1) * 128]
+    for index in range(3):
+        grads_ref[step, :, index * 128 : (index + 1) * 128] = sums[:, index * 128 : (index + 1) * 128]
 
     @pl.when(step == last)
     def _():
+        for index, (half, at) in enumerate(((0, 0), (0, share), (1, 0))):
+            for n in range(grads_ref.shape[0]):
+                part = grads_ref[n, :, index * 128 : (index + 1) * 128]
+                pack[:, half, at : at + share, n * 128 : (n + 1) * 128] = part.reshape(-1, share, 128)
+        pack[:, 1, share : 2 * share, :] = dwo_ref[...].astype(BF16).reshape(-1, share, D)
+        seq = dist_ref.shape[2]
+        hot = (lax.broadcasted_iota(jnp.int32, (128, seq), 0) == buckets_ref[...]).astype(F32).astype(BF16)
+        left = jnp.concatenate([dist_ref[h] for h in range(dist_ref.shape[0])], axis=0)
+        table = jnp.zeros((left.shape[0], 128), F32)
+        for _ in range(3):
+            low = left.astype(BF16)
+            left = left - low.astype(F32)
+            table = table + nt(low, hot)
+        rows_out = [jnp.zeros((1, D), F32), dgain_m_ref[...], jnp.zeros((6, D), F32)]
+        for e in range(experts):
+            picked = jnp.zeros((1, D), F32)
+            for k in range(experts):
+                picked = picked + drouter_ref[k : k + 1, :] * jnp.where(partner(place, ORDER[k]) == e, 1.0, 0.0)
+            rows_out.append(picked)
+        rows_out.append(jnp.zeros((8 - experts, D), F32))
+        rows_out.append(jnp.concatenate([table, jnp.zeros((table.shape[0], D - 128), F32)], axis=1))
+        rows_out.append(jnp.zeros((16 - table.shape[0], D), F32))
+        small = jnp.concatenate(rows_out, axis=0).astype(BF16)
+        for slot in range(pack.shape[0]):
+            pack[slot, 0, 2 * share :, :] = small
+            pack[slot, 1, 2 * share :, :] = jnp.zeros_like(small)
         finish()
         hop.wait()
 
@@ -1068,12 +1098,13 @@
 
     schedule = {
         3: [gather_c[1]],
-        6: [gather_c[2], gather_c[3], relays[0].wait, relays[1].wait, gather_b[0]],
-        9: [gather_b[1], reduce_a[0], reduce_a[1]],
-        10: [reduce_a[2]],
+        5: [relays[0].wait, relays[1].wait, gather_b[0]],
+        6: [gather_c[2]],
+        7: [gather_c[3], reduce_a[0]],
+        8: [gather_b[1], reduce_a[1]],
+        9: [reduce_a[2]],
         12: [reduce_a[3]],
-        14: [reduce_a[4], release, hop.start, claim, reduce_c[0], reduce_c[1]],
-        15: [reduce_c[2]],
+        15: [reduce_a[4], release, hop.start, claim, reduce_c[0], reduce_c[1], reduce_c[2]],
     }
     for when, actions in schedule.items():
         @pl.when(step == when)
@@ -1155,20 +1186,21 @@
         keep.wait()
 
 
-def send_rows(step, value, stage, target, sends, recvs, keep, group):
+def own_last(step, group):
+    return lax.rem(lax.axis_index("expert") + 1 + step, group)
+
+
+def send_rows(p, value, stage, target, sends, recvs, keep):
     place = lax.axis_index("expert")
-    for p in range(group):
-        @pl.when(step == p)
-        def _(p=p):
-            stage[p] = value
-
-            @pl.when(place == p)
-            def _():
-                pltpu.make_async_copy(stage.at[p], target.at[p], keep.at[0]).start()
-
-            @pl.when(place != p)
-            def _():
-                along_axis(stage.at[p], target.at[place], sends.at[p], recvs.at[place], p).start()
+    stage[p] = value
+
+    @pl.when(p == place)
+    def _():
+        pltpu.make_async_copy(stage.at[place], target.at[place], keep.at[0]).start()
+
+    @pl.when(p != place)
+    def _():
+        along_axis(stage.at[p], target.at[place], sends.at[p], recvs.at[place], p).start()
 
 
 def end_rows(stage, target, sends, recvs, keep, group):
@@ -1235,7 +1267,7 @@
         result = result + gates[:, k : k + 1] * got
         dgate = jnp.where(lane == k, jnp.sum(g * got, axis=-1, keepdims=True), dgate)
         da = da + nn(spot, back_ref[k])
-    send_rows(step, result.astype(BF16), stage, out_all, sends, recvs, keep, group)
+    send_rows(step, result.astype(BF16), stage, out_all, sends, recvs, keep)
     named = (pos_ref[...] >= 0) & (lane < experts)
     denom = jnp.sum(jnp.where(named, pr, 0.0), axis=-1, keepdims=True)
     weighted = jnp.sum(dgate * gates, axis=-1, keepdims=True)
@@ -1265,10 +1297,9 @@
 
 
 def close_kernel(
-    x_ref, dq_ref, dk_ref, dv_ref, dh_ref, first_ref, second_ref, params_ref, dwq_ref, dwk_ref, dwv_ref, dwo_ref,
-    dgain_m_ref, drouter_ref, dist_ref, buckets_ref, sum0, sum1, sum2,
+    x_ref, dq_ref, dk_ref, dv_ref, dh_ref, first_ref, second_ref, params_ref, pack, sum0, sum1, sum2,
     din_out, gather_first, gather_second, dense_ref,
-    stage, total, pack, own, pair, inbox, r_send, r_recv, r_local, sends, recvs, keep,
+    stage, total, own, pair, inbox, r_send, r_recv, r_local, sends, recvs, keep,
     z_in, z_total, z_final, z_send, z_recv, g_send, g_recv, g_local, *, share, group, experts
 ):
     step = pl.program_id(0)
@@ -1288,30 +1319,6 @@
 
     @pl.when(step == 0)
     def _():
-        places = ((0, 0, dwq_ref), (0, share, dwk_ref), (1, 0, dwv_ref), (1, share, dwo_ref))
-        for half, at, grad_ref in places:
-            pack[:, half, at : at + share, :] = grad_ref[...].astype(BF16).reshape(-1, share, D)
-        seq = dist_ref.shape[2]
-        hot = (lax.broadcasted_iota(jnp.int32, (128, seq), 0) == buckets_ref[...]).astype(F32).astype(BF16)
-        left = jnp.concatenate([dist_ref[h] for h in range(dist_ref.shape[0])], axis=0)
-        table = jnp.zeros((left.shape[0], 128), F32)
-        for _ in range(3):
-            low = left.astype(BF16)
-            left = left - low.astype(F32)
-            table = table + nt(low, hot)
-        rows_out = [jnp.zeros((1, D), F32), dgain_m_ref[...], jnp.zeros((6, D), F32)]
-        for e in range(experts):
-            picked = jnp.zeros((1, D), F32)
-            for k in range(experts):
-                picked = picked + drouter_ref[k : k + 1, :] * jnp.where(partner(place, ORDER[k]) == e, 1.0, 0.0)
-            rows_out.append(picked)
-        rows_out.append(jnp.zeros((8 - experts, D), F32))
-        rows_out.append(jnp.concatenate([table, jnp.zeros((table.shape[0], D - 128), F32)], axis=1))
-        rows_out.append(jnp.zeros((16 - table.shape[0], D), F32))
-        small = jnp.concatenate(rows_out, axis=0).astype(BF16)
-        for slot in range(pack.shape[0]):
-            pack[slot, 0, 2 * share :, :] = small
-            pack[slot, 1, 2 * share :, :] = jnp.zeros_like(small)
         meet(plane_devices() + place_devices(group))
         start()
         far()
@@ -1322,11 +1329,8 @@
 
     @pl.when(step == 1)
     def _():
+        late()
         start0()
-
-    @pl.when(step == 2)
-    def _():
-        late()
 
     da = jnp.zeros(dh_ref.shape, F32)
     places = ((first_ref, 0), (first_ref, 1), (second_ref, 0))
@@ -1338,7 +1342,7 @@
     n1 = x * inverse
     dn = da * params_ref[0:1, :]
     din = dh_ref[...] + inverse * (dn - n1 * jnp.mean(dn * n1, axis=-1, keepdims=True))
-    send_rows(step, din.astype(BF16), stage, din_out, sends, recvs, keep, group)
+    send_rows(own_last(step, group), din.astype(BF16), stage, din_out, sends, recvs, keep)
 
     @pl.when(step == last)
     def _():
@@ -1350,7 +1354,6 @@
         ]
         for copy in spread:
             copy.start()
-        start1()
         for copy in spread:
             copy.wait_recv()
         value = z_total[place].astype(F32)
@@ -1364,6 +1367,7 @@
         ]
         for copy in share_out:
             copy.start()
+        start1()
         start2()
         for copy in share_out:
             copy.wait_recv()
@@ -1461,6 +1465,7 @@
     table_spec = pl.BlockSpec((pairs, blocks, TILE, TILE), lambda i: (i, 0, 0, 0))
     lse_spec = pl.BlockSpec((1, pairs, seq), lambda i: (i, 0, 0))
 
+    turned_rows = lambda width: pl.BlockSpec((TILE, width), lambda i: (own_last(i, group), 0))
     once = lambda shape: pl.BlockSpec(shape, lambda *_: (0,) * len(shape), pipeline_mode=pl.Buffered(1))
     turned = pl.BlockSpec((1, *slots), lambda i: (i // (shards // 2), 0, 0))
     eo, da, dw, sum1, sum3, _, _, _, _, _ = call(
@@ -1488,35 +1493,34 @@
          dma((group,)), dma((1,))] + reduce_scratch(piece),
         flops=24 * seq * D * D, nbytes=32 * 2**20, collective=7,
     )(h1, normed_m, g, o, gates, pr, down, eo, da, second, params, dw, sum3)
-    dist_spec = pl.BlockSpec((pairs, 1, seq), lambda i: (i, 0, 0))
-    dq, dk, dv, dist, grad_query, grad_key, grad_value, sum0, sum2 = call(
-        functools.partial(attend_back_kernel, width=width, scale=scale, group=group), "attend_back",
-        (heads // pairs,),
-        [cols, cols, cols, cols, table_spec, whole((seq, 128)), whole((16, seq)), lse_spec, whole(tokens), ANY, ANY],
-        [cols, cols, cols, dist_spec] + [pl.BlockSpec((D, 128), lambda i: (0, i))] * 3 + [whole(piece), ANY],
-        [sds(tokens, BF16)] * 3 + [sds((heads, 1, seq), F32)] + [sds((D, D), BF16)] * 3
-        + [sds(piece, BF16), sds(piece, BF16)],
-        [pltpu.VMEM((blocks, TILE, TILE), F32), pltpu.VMEM((seq, 128), F32), pltpu.VMEM((seq, 128), F32),
+    dense_slot = (2, 2 * share + 32, D)
+    dq, dk, dv, pack, sum0, sum2 = call(
+        functools.partial(
+            attend_back_kernel, width=width, scale=scale, group=group, share=share, experts=experts),
+        "attend_back", (heads // pairs,),
+        [cols, cols, cols, cols, table_spec, whole((seq, 128)), whole((16, seq)), lse_spec, once(tokens), once((D, D)),
+         whole((1, D)), whole((8, D)), whole((1, seq)), ANY, ANY],
+        [cols, cols, cols, once((shards, *dense_slot)), whole(piece), ANY],
+        [sds(tokens, BF16)] * 3 + [sds((shards, *dense_slot), BF16), sds(piece, BF16), sds(piece, BF16)],
+        [pltpu.VMEM((heads, 1, seq), F32), pltpu.VMEM((heads // pairs, D, 3 * 128), BF16),
+         pltpu.VMEM((blocks, TILE, TILE), F32), pltpu.VMEM((seq, 128), F32), pltpu.VMEM((seq, 128), F32),
          pltpu.VMEM((D, seq), BF16)]
         + [dma((1,))] * 2 + reduce_scratch(piece),
         flops=20 * seq * seq * D, nbytes=24 * 2**20, collective=8,
-    )(q, k, v, do, table, down, across, lse, normed, sum2, dw)
-    dense_slot = (2, 2 * share + 32, D)
+    )(q, k, v, do, table, down, across, lse, normed, grad_output, grad_gain_m, grad_router, bucket_row, sum2, dw)
     quarter = (dense_slot[1] // 2, D)
     grad_in, *gathered, dense = call(
         functools.partial(close_kernel, share=share, group=group, experts=experts), "close", (blocks,),
-        [rows(D)] * 5 + [whole(first.shape), whole(second.shape), whole((32, D))] + [whole((D, D))] * 4
-        + [whole((1, D)), whole((8, D)), whole((heads, 1, seq)), whole((1, seq))] + [whole(piece)] * 3,
+        [turned_rows(D)] * 5 + [once(first.shape), once(second.shape), whole((32, D)), ANY] + [once(piece)] * 3,
         [ANY, ANY, ANY, whole((group, *quarter))],
         [sds((group, part, D), BF16), buffer, buffer, sds((group, *quarter), BF16)],
-        [pltpu.VMEM((group, part, D), BF16), pltpu.VMEM(piece, BF16), pltpu.VMEM((shards, *dense_slot), BF16)]
+        [pltpu.VMEM((group, part, D), BF16), pltpu.VMEM(piece, BF16)]
         + reduce_scratch(dense_slot)
         + [dma((group,)), dma((group,)), dma((1,)), pltpu.VMEM((group - 1, *quarter), BF16),
            pltpu.VMEM((group, *quarter), BF16), pltpu.VMEM((group, *quarter), BF16), dma((2 * group,)),
            dma((2 * group,))] + gather_sems(),
         flops=12 * seq * D * D, nbytes=24 * 2**20, collective=9,
-    )(x, dq, dk, dv, dh, first, second, params, grad_query, grad_key, grad_value, grad_output, grad_gain_m, grad_router,
-      dist, bucket_row, sum0, sum1, sum2)
+    )(x, dq, dk, dv, dh, first, second, params, pack, sum0, sum1, sum2)
     spec = pl.BlockSpec((1, D, chunk), lambda i: (i, 0, 0))
     line_rows = pl.BlockSpec((seq // shards, D), lambda i: (i, 0))
     expert_in, expert_out, grad_in, *dense_grads, grad_gain, smalls = call(

time: 580 us -> 561 us (0.967)
  Pallas kernels: 566 us -> 546 us
    pallas_call x1, Pallas kernels: 146 us -> 138 us  [on_device_whole(): call(functools.partial(front_kernel, group=group, share=share, heads=head...]
    pallas_call x1, Pallas kernels: 89.8 us -> 83.6 us  [on_device_whole(): call(functools.partial(close_kernel, share=share, group=group, experts=ex...]
where the time goes in v4:
time: 561 us; the launch traced here: 558 us
  Pallas kernels  546 us (97%)
  local copies, waits for them, and re-layouts  7.53 us (1%)
    pallas_call x1, Pallas kernels, on_device_whole(): call(functools.partial(experts_kernel, capacity=capacity, group=group, sh...  181 us
    pallas_call x1, Pallas kernels, on_device_whole(): call(functools.partial(front_kernel, group=group, share=share, heads=head...  138 us
    pallas_call x1, Pallas kernels, on_device_whole(): call(functools.partial(close_kernel, share=share, group=group, experts=ex...  83.6 us
    pallas_call x1, Pallas kernels, on_device_whole(): call(functools.partial(combine_kernel, share=share, experts=experts, capa...  73.8 us
    pallas_call x1, Pallas kernels, on_device_whole(): call(functools.partial(attend_back_kernel, width=width, scale=scale, grou...  56.1 us
    pallas_call x1, Pallas kernels, on_device_whole(): call(functools.partial(unpack_kernel, share=share), 'unpack', (shards,),...  13.8 us

profile of v4, /device:TPU:0, one launch (start us, length us, event | category | flops | bytes accessed | tf_op | source)
XLA Modules:
  0.0 558.2 jit_solution(7583460735628319493)
XLA Ops:
  0.6 0.7 fusion.10
  1.3 0.8 copy.30
  2.1 1.3 fusion.4.small_ref
  3.4 1.3 pad.16.routes_ref
  4.7 138.5 %front.1 = (bf16[4,256,768]{2,1,0:T(8,128)(2,1)}, bf16[4,256,768]{2,1,0:T(8,128)(2,1)}, bf16[768,384]{1,0:T(8,128)(2,1)}, bf16[768,384]{1,0:T(8,128)(2,1)}, bf16...) custom-call(bf16[4,256,768]{2,1,0:T(8,128)(2,1)} %x_ref.1, ...), custom_call_target="tpu_custom_call" | custom-call | flops 3623878656 | tf_op jit(solution)/shard_map/front/pallas_call | solution.py:1441
  143.2 180.6 %experts.1 = (bf16[4,768,768]{2,1,0:T(8,128)(2,1)}, bf16[4,768,768]{2,1,0:T(8,128)(2,1)}, bf16[4,8,2,768,384]{4,3,2,1,0:T(8,128)(2,1)}, bf16[2,768,384]{2,1,0:T(...) custom-call(bf16[1024,768]{1,0:T(8,128)(2,1)} %get-tuple-element.66., ...), custom_call_target="tpu_custom_call" | custom-call | flops 86973087744 | bytes 100663296 | tf_op jit(solution)/shard_map/experts/pallas_call | solution.py:1471
  323.8 73.8 %combine.1 = (bf16[4,256,768]{2,1,0:T(8,128)(2,1)}, f32[1024,768]{1,0:T(8,128)}, bf16[1024,768]{1,0:T(8,128)(2,1)}, f32[768,768]{1,0:T(8,128)}, f32[1,768]{1,0:T...) custom-call(f32[1024,768]{1,0:T(8,128)} %get-tuple-element.65.h_ref, bf16[1024,768]{1,0:T(8,128)(2,1)} %get-tuple-element.66.a_ref, ...), custom_call_target="tpu_custom_call" | custom-call | flops 14495514624 | bytes 33554432 | tf_op jit(solution)/shard_map/combine/pallas_call | solution.py:1485
  397.6 56.1 %attend_back.1 = (bf16[1024,768]{1,0:T(8,128)(2,1)}, bf16[1024,768]{1,0:T(8,128)(2,1)}, bf16[1024,768]{1,0:T(8,128)(2,1)}, bf16[8,2,224,768]{3,2,1,0:T(8,128)(2,...) custom-call(bf16[1024,768]{1,0:T(8,128)(2,1)} %get-tuple-element.85.q_ref, ...), custom_call_target="tpu_custom_call" | custom-call | flops 16106127360 | bytes 25165824 | tf_op jit(solution)/shard_map/attend_back/pallas_call | solution.py:1497
  453.8 0.0 copy-start.1
  453.8 83.6 %close.1 = (bf16[4,256,768]{2,1,0:T(8,128)(2,1)}, bf16[8,768,384]{2,1,0:T(8,128)(2,1)}, bf16[8,768,384]{2,1,0:T(8,128)(2,1)}, bf16[4,112,768]{2,1,0:T(8,128)(2,1)}) custom-call(bf16[1024,768]{1,0:T(8,128)(2,1)} %bitcast.31, bf16[1024,768]{1,0:T(8,128)(2,1)} %get-tuple-element.96.dq_ref, bf16[1024,768]{1,0:T(8,128)(2,1)} %get-tuple-element.97.dk_ref, ...), custom_call_target="tpu_custom_call" | custom-call | flops 7247757312 | bytes 25165824 | tf_op jit(solution)/shard_map/close/pallas_call | solution.py:1512
  537.3 0.0 copy-done.1
  537.3 0.7 copy.31.gain_ref
  538.1 0.0 copy-start
  538.1 13.8 %unpack.1 = (f32[1,768,3072]{2,1,0:T(8,128)}, f32[1,3072,768]{2,1,0:T(8,128)}, f32[1024,768]{1,0:T(8,128)}, f32[96,768]{1,0:T(8,128)}, f32[96,768]{1,0:T(8,128)}...) custom-call(bf16[8,768,384]{2,1,0:T(8,128)(2,1)} %get-tuple-element.105.first_ref, ...), custom_call_target="tpu_custom_call" | custom-call | bytes 35651584 | tf_op jit(solution)/shard_map/unpack/pallas_call | solution.py:1526
  551.8 0.8 slice.15
  552.6 0.1 dynamic-slice_bitcast_fusion
  552.7 0.7 copy.32
  553.4 0.8 slice.12
  554.2 0.7 dynamic-slice_bitcast_fusion.1
  554.8 0.6 dynamic-slice_bitcast_fusion.2
  555.4 1.4 reduce
  556.8 0.0 copy-done
  556.9 1.1 copy.34
Async XLA Ops:
  453.8 83.6 %copy-start.1 = (bf16[96]{0:T(256)(128)(2,1)S(1)}, bf16[96]{0:T(256)(128)(2,1)}, u32[]{:S(2)}) copy-start(bf16[96]{0:T(256)(128)(2,1)} %param.20) | copy-start | bytes 580
  538.1 18.8 %copy-start = (bf16[4,256,768]{2,1,0:T(8,128)(2,1)S(1)}, bf16[4,256,768]{2,1,0:T(8,128)(2,1)}, u32[]{:S(2)}) copy-start(bf16[4,256,768]{2,1,0:T(8,128)(2,1)} %get-tuple-element.154) | copy-start | bytes 4718596

commit v5 on v4

--- a/solution.py
+++ b/solution.py
@@ -519,7 +519,7 @@
     return 2 * lax.rem(place // 2 + k // 2, 2) + lax.rem(lax.rem(place, 2) + k % 2, 2)
 
 
-ORDER = (1, 0, 2, 3)
+ORDER = (1, 2, 0, 3)
 
 
 def place_devices(group):
@@ -901,7 +901,7 @@
     def emit(half, value):
         sums_ref[half] = value.astype(BF16)
 
-    start, far, near, late, finish = reduce_copies(terms.at[1], own, pair, inbox, send, recv, local, emit)
+    start, far, near, late, finish = reduce_copies(terms.at[2], own, pair, inbox, send, recv, local, emit)
     hop = along_axis(passed, pass_out, p_send.at[0], p_recv.at[0], partner(place, 3))
 
     @pl.when(step == 0)
@@ -1028,8 +1028,8 @@
     def loads(at, which):
         c = lax.rem(at, steps)
         two = lax.rem(at, 2)
-        if which != 1:
-            first, second = {0: (first_a, second_a), 2: (first_c, second_c), 3: (first_b, second_b)}[which]
+        if which != 2:
+            first, second = {0: (first_a, second_a), 1: (first_c, second_c), 3: (first_b, second_b)}[which]
             both = pl.ds(2 * c, 2)
             return [
                 pltpu.make_async_copy(first.at[both], w_in_two.at[two], w_sem.at[0, two]),
@@ -1079,7 +1079,7 @@
         own[3, half] = value.astype(BF16)
 
     reduce_a = reduce_copies(dw_out.at[0], own, pair, inbox, send_a, recv_a, local_a, emit_a)
-    reduce_c = reduce_copies(dw_out.at[2], own, pair, inbox, send_c, recv_c, local_c, emit_c)
+    reduce_c = reduce_copies(dw_out.at[1], own, pair, inbox, send_c, recv_c, local_c, emit_c)
 
     @pl.when(step == 0)
     def _():
@@ -1098,13 +1098,12 @@
 
     schedule = {
         3: [gather_c[1]],
-        5: [relays[0].wait, relays[1].wait, gather_b[0]],
-        6: [gather_c[2]],
-        7: [gather_c[3], reduce_a[0]],
-        8: [gather_b[1], reduce_a[1]],
-        9: [reduce_a[2]],
-        12: [reduce_a[3]],
-        15: [reduce_a[4], release, hop.start, claim, reduce_c[0], reduce_c[1], reduce_c[2]],
+        4: [relays[0].wait, relays[1].wait, gather_b[0]],
+        6: [reduce_a[0]],
+        7: [gather_b[1], reduce_a[1]],
+        8: [reduce_a[2]],
+        11: [reduce_a[3]],
+        13: [reduce_a[4], release, hop.start, claim, reduce_c[0], reduce_c[1], reduce_c[2]],
     }
     for when, actions in schedule.items():
         @pl.when(step == when)
@@ -1129,7 +1128,7 @@
     each_turn(step, lambda copy: copy.wait())
     ahead = step + 1
 
-    @pl.when((step < last) & (ahead != 3 * steps))
+    @pl.when((step < last) & (ahead != steps) & (ahead != 3 * steps))
     def _():
         each_turn(ahead, lambda copy: copy.start())
 
@@ -1168,6 +1167,12 @@
     def _():
         eo_ref[0] = eo_sum[...].astype(BF16)
         da_ref[0] = da_sum[...].astype(BF16)
+
+    @pl.when(ahead == steps)
+    def _():
+        gather_c[2]()
+        gather_c[3]()
+        each_turn(ahead, lambda copy: copy.start())
 
     @pl.when(ahead == 3 * steps)
     def _():

time: 561 us -> 554 us (0.988)
  Pallas kernels: 546 us -> 540 us
    pallas_call x1, Pallas kernels: 181 us -> 174 us  [on_device_whole(): call(functools.partial(experts_kernel, capacity=capacity, group=group, sh...]
where the time goes in v5:
time: 554 us; the launch traced here: 551 us
  Pallas kernels  540 us (97%)
  local copies, waits for them, and re-layouts  7.53 us (1%)
    pallas_call x1, Pallas kernels, on_device_whole(): call(functools.partial(experts_kernel, capacity=capacity, group=group, sh...  174 us
    pallas_call x1, Pallas kernels, on_device_whole(): call(functools.partial(front_kernel, group=group, share=share, heads=head...  138 us
    pallas_call x1, Pallas kernels, on_device_whole(): call(functools.partial(close_kernel, share=share, group=group, experts=ex...  83.3 us
    pallas_call x1, Pallas kernels, on_device_whole(): call(functools.partial(combine_kernel, share=share, experts=experts, capa...  73.7 us
    pallas_call x1, Pallas kernels, on_device_whole(): call(functools.partial(attend_back_kernel, width=width, scale=scale, grou...  56.2 us
    pallas_call x1, Pallas kernels, on_device_whole(): call(functools.partial(unpack_kernel, share=share), 'unpack', (shards,),...  13.8 us

profile of v5, /device:TPU:0, one launch (start us, length us, event | category | flops | bytes accessed | tf_op | source)
XLA Modules:
  0.0 551.5 jit_solution(12238986982548903943)
XLA Ops:
  0.6 0.7 fusion.10
  1.3 0.8 copy.30
  2.1 1.3 fusion.4.small_ref
  3.4 1.3 pad.16.routes_ref
  4.7 138.5 %front.1 = (bf16[4,256,768]{2,1,0:T(8,128)(2,1)}, bf16[4,256,768]{2,1,0:T(8,128)(2,1)}, bf16[768,384]{1,0:T(8,128)(2,1)}, bf16[768,384]{1,0:T(8,128)(2,1)}, bf16...) custom-call(bf16[4,256,768]{2,1,0:T(8,128)(2,1)} %x_ref.1, ...), custom_call_target="tpu_custom_call" | custom-call | flops 3623878656 | tf_op jit(solution)/shard_map/front/pallas_call | solution.py:1446
  143.2 174.2 %experts.1 = (bf16[4,768,768]{2,1,0:T(8,128)(2,1)}, bf16[4,768,768]{2,1,0:T(8,128)(2,1)}, bf16[4,8,2,768,384]{4,3,2,1,0:T(8,128)(2,1)}, bf16[2,768,384]{2,1,0:T(...) custom-call(bf16[1024,768]{1,0:T(8,128)(2,1)} %get-tuple-element.66., ...), custom_call_target="tpu_custom_call" | custom-call | flops 86973087744 | bytes 100663296 | tf_op jit(solution)/shard_map/experts/pallas_call | solution.py:1476
  317.4 73.7 %combine.1 = (bf16[4,256,768]{2,1,0:T(8,128)(2,1)}, f32[1024,768]{1,0:T(8,128)}, bf16[1024,768]{1,0:T(8,128)(2,1)}, f32[768,768]{1,0:T(8,128)}, f32[1,768]{1,0:T...) custom-call(f32[1024,768]{1,0:T(8,128)} %get-tuple-element.65.h_ref, bf16[1024,768]{1,0:T(8,128)(2,1)} %get-tuple-element.66.a_ref, ...), custom_call_target="tpu_custom_call" | custom-call | flops 14495514624 | bytes 33554432 | tf_op jit(solution)/shard_map/combine/pallas_call | solution.py:1490
  391.1 56.2 %attend_back.1 = (bf16[1024,768]{1,0:T(8,128)(2,1)}, bf16[1024,768]{1,0:T(8,128)(2,1)}, bf16[1024,768]{1,0:T(8,128)(2,1)}, bf16[8,2,224,768]{3,2,1,0:T(8,128)(2,...) custom-call(bf16[1024,768]{1,0:T(8,128)(2,1)} %get-tuple-element.85.q_ref, ...), custom_call_target="tpu_custom_call" | custom-call | flops 16106127360 | bytes 25165824 | tf_op jit(solution)/shard_map/attend_back/pallas_call | solution.py:1502
  447.3 0.0 copy-start.1
  447.3 83.3 %close.1 = (bf16[4,256,768]{2,1,0:T(8,128)(2,1)}, bf16[8,768,384]{2,1,0:T(8,128)(2,1)}, bf16[8,768,384]{2,1,0:T(8,128)(2,1)}, bf16[4,112,768]{2,1,0:T(8,128)(2,1)}) custom-call(bf16[1024,768]{1,0:T(8,128)(2,1)} %bitcast.31, bf16[1024,768]{1,0:T(8,128)(2,1)} %get-tuple-element.96.dq_ref, bf16[1024,768]{1,0:T(8,128)(2,1)} %get-tuple-element.97.dk_ref, ...), custom_call_target="tpu_custom_call" | custom-call | flops 7247757312 | bytes 25165824 | tf_op jit(solution)/shard_map/close/pallas_call | solution.py:1517
  530.6 0.0 copy-done.1
  530.6 0.7 copy.31.gain_ref
  531.3 0.0 copy-start
  531.3 13.8 %unpack.1 = (f32[1,768,3072]{2,1,0:T(8,128)}, f32[1,3072,768]{2,1,0:T(8,128)}, f32[1024,768]{1,0:T(8,128)}, f32[96,768]{1,0:T(8,128)}, f32[96,768]{1,0:T(8,128)}...) custom-call(bf16[8,768,384]{2,1,0:T(8,128)(2,1)} %get-tuple-element.105.first_ref, ...), custom_call_target="tpu_custom_call" | custom-call | bytes 35651584 | tf_op jit(solution)/shard_map/unpack/pallas_call | solution.py:1531
  545.1 0.8 slice.15
  545.9 0.1 dynamic-slice_bitcast_fusion
  546.0 0.7 copy.32
  546.7 0.8 slice.12
  547.5 0.7 dynamic-slice_bitcast_fusion.1
  548.1 0.6 dynamic-slice_bitcast_fusion.2
  548.7 1.4 reduce
  550.1 0.0 copy-done
  550.1 1.1 copy.34
Async XLA Ops:
  447.3 83.3 %copy-start.1 = (bf16[96]{0:T(256)(128)(2,1)S(1)}, bf16[96]{0:T(256)(128)(2,1)}, u32[]{:S(2)}) copy-start(bf16[96]{0:T(256)(128)(2,1)} %param.20) | copy-start | bytes 580
  531.3 18.8 %copy-start = (bf16[4,256,768]{2,1,0:T(8,128)(2,1)S(1)}, bf16[4,256,768]{2,1,0:T(8,128)(2,1)}, u32[]{:S(2)}) copy-start(bf16[4,256,768]{2,1,0:T(8,128)(2,1)} %get-tuple-element.154) | copy-start | bytes 4718596
